TPU v7x, 32 devices: a whole 2x2x4 slice. The times are simulated.
32 devices in a mesh: dp: 8 (over z, y), head: 4 (over x, core).
Axes of the slice: x: 2, y: 2, z: 4, core: 2. Of those that a mesh axis runs over, the one named last changes fastest.
Arguments:
- tokens: bfloat16 [32768, 768], P(('dp', 'head')), may hold values from -6 to 6
- w_query: bfloat16 [768, 768], replicated, may hold values from -0.21875 to 0.21875
- w_key: bfloat16 [768, 768], replicated, may hold values from -0.21875 to 0.21875
- w_value: bfloat16 [768, 768], replicated, may hold values from -0.21875 to 0.21875
- w_out: bfloat16 [768, 768], replicated, may hold values from -6 to 6
- w_up: bfloat16 [768, 3072], replicated, may hold values from -0.21875 to 0.21875
- w_down: bfloat16 [3072, 768], replicated, may hold values from -0.109375 to 0.109375
- norm_gains: float32 [2, 768], replicated, may hold values from 0.25 to 1.75
- norm_biases: float32 [2, 768], replicated, may hold values from -2 to 2
- cotangent: bfloat16 [32768, 768], P(('dp', 'head')), may hold values from -6 to 6
Outputs:
- output: bfloat16 [32768, 768], P(('dp', 'head'))
- d_tokens: float32 [32768, 768], P(('dp', 'head'))
- grad_w_query: float32 [768, 768], replicated
- grad_w_key: float32 [768, 768], replicated
- grad_w_value: float32 [768, 768], replicated
- grad_w_out: float32 [768, 768], replicated
- grad_w_up: float32 [768, 3072], replicated
- grad_w_down: float32 [3072, 768], replicated
- grad_norm_gains: float32 [2, 768], replicated
- grad_norm_biases: float32 [2, 768], replicated
All inputs are finite; a program needn't handle non-finite values.
Results may differ from a plain program's by a relative error of at most 0.014.
Values may be sent and summed in bfloat16 or wider, within the bound.
No kernel may reach another device: no remote copies, remote signals or barrier semaphores. Data moves between devices by JAX's collectives and lax.ppermute only.
A program may use at most 256 MiB of HBM per device.

v0:
```python
import math

import jax
import jax.numpy as jnp
from jax import lax
from jax.sharding import PartitionSpec as P

D = 768
E = 64
FF = 3072
LENGTH = 2048
STRETCH = 128


EPSILON = 1e-05
HIGHEST = lax.Precision.HIGHEST


def plain_dot(first_arg, second_arg):
    return jnp.dot(first_arg, second_arg, preferred_element_type=jnp.float32)


def first_trans_dot(first_arg, second_arg):
    return lax.dot_general(
        first_arg, second_arg, (((0,), (0,)), ((), ())), preferred_element_type=jnp.float32
    )


def second_trans_dot(first_arg, second_arg):
    return lax.dot_general(
        first_arg, second_arg, (((1,), (1,)), ((), ())), preferred_element_type=jnp.float32
    )


def layer_norm(inputs, norm_gain, norm_shift):
    centre = jnp.mean(inputs, axis=-1, keepdims=True)
    centred = inputs - centre
    spread = jnp.mean(centred * centred, axis=-1, keepdims=True)
    return centred * lax.rsqrt(spread + EPSILON) * norm_gain + norm_shift


def exact_gelu(inputs):
    return jax.nn.gelu(inputs, approximate=False)


def earlier_sum(blocks):
    running = jnp.cumsum(blocks, axis=1)
    return jnp.concatenate([jnp.zeros_like(running[:, :1]), running[:, :-1]], axis=1)


def blocked_shape(flat_arr):
    token_count, local_width = flat_arr.shape
    return (token_count // LENGTH, LENGTH // STRETCH, STRETCH, local_width // E, E)


def raw_scores(queries, key_part):
    shape = blocked_shape(queries)
    return jnp.einsum(
        "sbihe,sbjhe->sbhij",
        queries.reshape(shape),
        key_part.reshape(shape),
        preferred_element_type=jnp.float32,
    )


def attend_core(raw, queries, key_part, value_part):
    token_count, local_width = queries.shape
    seq_count, block_count, block_len, head_count, head_size = blocked_shape(queries)
    step_angle = 0.5 * math.pi / LENGTH
    angles = step_angle * jnp.arange(LENGTH, dtype=jnp.float32)
    cosine = jnp.cos(angles)[None, :, None, None]
    sine_row = jnp.sin(angles)[None, :, None, None]
    seq_shape = (seq_count, LENGTH, head_count, head_size)
    blocked = (seq_count, block_count, block_len, head_count, head_size)
    q_seq = queries.reshape(seq_shape)
    k_seq = key_part.reshape(seq_shape)
    v_block = value_part.reshape(blocked)
    q_cos = (q_seq * cosine).reshape(blocked)
    q_sin = (q_seq * sine_row).reshape(blocked)
    k_cos = (k_seq * cosine).reshape(blocked)
    k_sin = (k_seq * sine_row).reshape(blocked)
    offsets = jnp.arange(STRETCH)
    distance = offsets[:, None] - offsets[None, :]
    weight_table = jnp.where(distance >= 0, jnp.cos(step_angle * distance.astype(jnp.float32)), 0.0)
    scores = raw * weight_table
    numerator = jnp.einsum("sbhij,sbjhe->sbihe", scores, v_block, precision=HIGHEST)
    denominator = jnp.einsum("sbhij->sbih", scores)
    state_cos = jnp.einsum("sbjhe,sbjhf->sbhef", k_cos, v_block, precision=HIGHEST)
    state_sin = jnp.einsum("sbjhe,sbjhf->sbhef", k_sin, v_block, precision=HIGHEST)
    total_cos = jnp.sum(k_cos, axis=2)
    total_sin = jnp.sum(k_sin, axis=2)
    numerator = numerator + jnp.einsum(
        "sbihe,sbhef->sbihf", q_cos, earlier_sum(state_cos), precision=HIGHEST
    )
    numerator = numerator + jnp.einsum(
        "sbihe,sbhef->sbihf", q_sin, earlier_sum(state_sin), precision=HIGHEST
    )
    denominator = denominator + jnp.einsum(
        "sbihe,sbhe->sbih", q_cos, earlier_sum(total_cos), precision=HIGHEST
    )
    denominator = denominator + jnp.einsum(
        "sbihe,sbhe->sbih", q_sin, earlier_sum(total_sin), precision=HIGHEST
    )
    return (numerator / denominator[..., None]).reshape(token_count, local_width)


def attend_forward(head_query, head_key, head_value):
    raw = raw_scores(head_query, head_key)
    query_wide = head_query.astype(jnp.float32)
    key_wide = head_key.astype(jnp.float32)
    attended, core_back = jax.vjp(
        attend_core, raw, query_wide, key_wide, head_value.astype(jnp.float32)
    )
    return (attended, (core_back, query_wide, key_wide))


def attend_backward(saved, d_attended):
    core_back, query_wide, key_wide = saved
    d_raw, d_query, d_key, d_value = core_back(d_attended)
    shape = blocked_shape(query_wide)
    d_query = d_query + jnp.einsum(
        "sbhij,sbjhe->sbihe", d_raw, key_wide.reshape(shape), precision=HIGHEST
    ).reshape(query_wide.shape)
    d_key = d_key + jnp.einsum(
        "sbhij,sbihe->sbjhe", d_raw, query_wide.reshape(shape), precision=HIGHEST
    ).reshape(key_wide.shape)
    return (d_query, d_key, d_value)


def local(tokens, w_query, w_key, w_value, w_out, w_up, w_down, norm_gains, norm_biases, cotangent):
    inputs = tokens.astype(jnp.float32)
    query_pre = plain_dot(tokens, w_query)
    key_pre = plain_dot(tokens, w_key)
    queries = jax.nn.softplus(query_pre).astype(jnp.bfloat16)
    key_low = jax.nn.softplus(key_pre).astype(jnp.bfloat16)
    value_low = plain_dot(tokens, w_value).astype(jnp.bfloat16)
    head_query, head_key, head_value = (
        lax.all_to_all(queries, "head", split_axis=1, concat_axis=0, tiled=True),
        lax.all_to_all(key_low, "head", split_axis=1, concat_axis=0, tiled=True),
        lax.all_to_all(value_low, "head", split_axis=1, concat_axis=0, tiled=True),
    )
    attended, saved = attend_forward(head_query, head_key, head_value)
    mixed_heads = attended.astype(jnp.bfloat16)
    mixed_low = lax.all_to_all(mixed_heads, "head", split_axis=0, concat_axis=1, tiled=True)
    branch = plain_dot(mixed_low, w_out)
    normed, norm_back_one = jax.vjp(layer_norm, inputs + branch, norm_gains[0], norm_biases[0])
    normed_low = normed.astype(jnp.bfloat16)
    hidden_in = plain_dot(normed_low, w_up)
    hidden_out, gelu_back = jax.vjp(exact_gelu, hidden_in)
    hidden = hidden_out.astype(jnp.bfloat16)
    ffn_out = plain_dot(hidden, w_down)
    result, norm_back_two = jax.vjp(layer_norm, normed + ffn_out, norm_gains[1], norm_biases[1])
    d_resid_two, d_gain_two, d_bias_two = norm_back_two(cotangent.astype(jnp.float32))
    d_ffn = d_resid_two.astype(jnp.bfloat16)
    grad_down = first_trans_dot(hidden, d_ffn)
    (d_hidden_full,) = gelu_back(second_trans_dot(d_ffn, w_down))
    d_hidden_in = d_hidden_full.astype(jnp.bfloat16)
    grad_up = first_trans_dot(normed_low, d_hidden_in)
    d_normed = d_resid_two + second_trans_dot(d_hidden_in, w_up)
    d_resid_one, d_gain_one, d_bias_one = norm_back_one(d_normed)
    d_branch = d_resid_one.astype(jnp.bfloat16)
    grad_out = first_trans_dot(mixed_low, d_branch)
    d_mixed = second_trans_dot(d_branch, w_out).astype(jnp.bfloat16)
    head_dmix = lax.all_to_all(d_mixed, "head", split_axis=1, concat_axis=0, tiled=True)
    back_terms = attend_backward(saved, head_dmix.astype(jnp.float32))
    d_heads = tuple((term.astype(jnp.bfloat16) for term in back_terms))
    d_queries, d_keys, d_values = (
        lax.all_to_all(d_heads[0], "head", split_axis=0, concat_axis=1, tiled=True),
        lax.all_to_all(d_heads[1], "head", split_axis=0, concat_axis=1, tiled=True),
        lax.all_to_all(d_heads[2], "head", split_axis=0, concat_axis=1, tiled=True),
    )
    d_query_pre = (d_queries.astype(jnp.float32) * jax.nn.sigmoid(query_pre)).astype(jnp.bfloat16)
    d_key_pre = (d_keys.astype(jnp.float32) * jax.nn.sigmoid(key_pre)).astype(jnp.bfloat16)
    grad_query = first_trans_dot(tokens, d_query_pre)
    grad_key = first_trans_dot(tokens, d_key_pre)
    grad_value = first_trans_dot(tokens, d_values)
    d_inputs = (
        d_resid_one + second_trans_dot(d_query_pre, w_query) + second_trans_dot(d_key_pre, w_key)
    )
    d_inputs = d_inputs + second_trans_dot(d_values, w_value)
    norm_terms = jnp.concatenate([d_gain_one, d_gain_two, d_bias_one, d_bias_two])
    shares = (
        lax.psum_scatter(grad_query.reshape(-1), ("dp", "head"), scatter_dimension=0, tiled=True),
        lax.psum_scatter(grad_key.reshape(-1), ("dp", "head"), scatter_dimension=0, tiled=True),
        lax.psum_scatter(grad_value.reshape(-1), ("dp", "head"), scatter_dimension=0, tiled=True),
        lax.psum_scatter(grad_out.reshape(-1), ("dp", "head"), scatter_dimension=0, tiled=True),
        lax.psum_scatter(grad_up.reshape(-1), ("dp", "head"), scatter_dimension=0, tiled=True),
        lax.psum_scatter(grad_down.reshape(-1), ("dp", "head"), scatter_dimension=0, tiled=True),
        lax.psum_scatter(norm_terms, ("dp", "head"), scatter_dimension=0, tiled=True),
    )
    totals = (
        lax.all_gather(shares[0].astype(jnp.bfloat16), ("dp", "head"), axis=0, tiled=True).astype(
            jnp.float32
        ),
        lax.all_gather(shares[1].astype(jnp.bfloat16), ("dp", "head"), axis=0, tiled=True).astype(
            jnp.float32
        ),
        lax.all_gather(shares[2].astype(jnp.bfloat16), ("dp", "head"), axis=0, tiled=True).astype(
            jnp.float32
        ),
        lax.all_gather(shares[3].astype(jnp.bfloat16), ("dp", "head"), axis=0, tiled=True).astype(
            jnp.float32
        ),
        lax.all_gather(shares[4].astype(jnp.bfloat16), ("dp", "head"), axis=0, tiled=True).astype(
            jnp.float32
        ),
        lax.all_gather(shares[5].astype(jnp.bfloat16), ("dp", "head"), axis=0, tiled=True).astype(
            jnp.float32
        ),
        lax.all_gather(shares[6].astype(jnp.bfloat16), ("dp", "head"), axis=0, tiled=True).astype(
            jnp.float32
        ),
    )
    norm_grads = totals[6].reshape(4, D)
    return (
        result.astype(jnp.bfloat16),
        d_inputs,
        totals[0].reshape(D, D),
        totals[1].reshape(D, D),
        totals[2].reshape(D, D),
        totals[3].reshape(D, D),
        totals[4].reshape(D, FF),
        totals[5].reshape(FF, D),
        norm_grads[0:2],
        norm_grads[2:4],
    )


def solution(mesh):
    in_specs = (
        P(("dp", "head"), None),
        P(),
        P(),
        P(),
        P(),
        P(),
        P(),
        P(),
        P(),
        P(("dp", "head"), None),
    )
    out_specs = (
        P(("dp", "head"), None),
        P(("dp", "head"), None),
        P(),
        P(),
        P(),
        P(),
        P(),
        P(),
        P(),
        P(),
    )
    return jax.shard_map(local, mesh=mesh, in_specs=in_specs, out_specs=out_specs, check_vma=False)
```

profile of v0, /device:TPU:0, one launch (start us, length us, event | category | flops | bytes accessed | tf_op | source)
XLA Modules:
  0.0 1424.2 jit_solution(247779797283213576)
XLA Ops:
  22.5 13.4 all-to-all-done
  46.6 13.7 all-to-all-done.1
  107.1 7.1 fusion.47
  114.3 7.3 fusion.129
  200.0 35.6 %multiply_convert_fusion = (bf16[1024,3072]{1,0:T(8,128)(2,1)}, f32[1024,3072]{1,0:T(8,128)}, f32[1024,3072]{1,0:T(8,128)}) fusion(bf16[768,3072]{1,0:T(8,128)(2,1)S(1)} %bitcast.201, f32[1024,768]{0,1:T(8,128)S(1)} %get-tuple-element.97, f32[768]{0:T(1024)S(1)} %get-tuple-element.53, f32[768]{0:T(1024)S(1)} %get-tuple-element.104, f32[1024]{0:T(1024)S(1)} %fusion.111, ...), kind=kOutput, calls=%fused_computation.3 | convolution fusion | flops 5040242688 | bytes 39335936 | tf_op jit(solution)/shard_map/dot_general | solution.py:20
  235.6 7.5 fusion.128
  247.7 8.5 fusion.93
  256.2 19.5 %add_convert_fusion = bf16[1024,3072]{1,0:T(8,128)(2,1)} fusion(f32[1024,3072]{1,0:T(8,128)} %get-tuple-element.66, f32[1024,3072]{1,0:T(8,128)} %get-tuple-element.98, bf16[3072,768]{1,0:T(8,128)(2,1)} %param.16, f32[1024]{0:T(1024)S(1)} %negate_multiply_fusion.2, bf16[1024,768]{0,1:T(8,128)(2,1)S(1)} %copy.117, f32[1024,768]{0,1:T(8,128)} %copy-done.21, ...), kind=kOutput, calls=%fused_computation.2 | convolution fusion | flops 4882956288 | bytes 40913920 | tf_op jit(solution)/shard_map/dot_general | solution.py:30
  275.8 12.0 multiply_reduce_fusion.1
  300.2 10.5 convolution_bitcast_fusion
  310.7 9.5 all-to-all-done.4
  329.6 12.4 fusion.21
  344.4 7.2 fusion.59
  358.7 9.9 fusion.23
  375.0 7.9 fusion.76
  388.7 8.0 add_bitcast_fusion.2
  405.1 8.9 add_bitcast_fusion.3
  470.1 8.9 add_convert_fusion.3
  485.0 10.8 reshape.344
  495.8 9.7 copy.179
  512.0 10.3 fusion.41
  522.3 14.7 %fusion.8 = f32[2,16,3,64,128]{4,3,2,1,0:T(8,128)} fusion(f32[2,16,3,128,128]{3,4,2,1,0:T(8,128)S(1)} %bitcast.190, f32[128,128]{0,1:T(8,128)S(1)} %copy-done.28, f32[2,16,128,3,64]{2,1,0,4,3:T(8,128)S(1)} %copy-done.20, f32[2,16,128,3]{2,3,1,0:T(4,128)S(1)} %copy-done.38), kind=kOutput, calls=%fused_computation.22 | convolution fusion | flops 1210318848 | bytes 12697600 | tf_op jit(solution)/shard_map/transpose(jvp(sbhij,sbjhe->sbihe))/dot_general | solution.py:86
  541.8 11.9 fusion.79
  596.2 457.4 %all-reduce.14 = (bf16[3072]{0:T(1024)(128)(2,1)S(1)}, bf16[589824]{0:T(1024)(128)(2,1)}, bf16[589824]{0:T(1024)(128)(2,1)}, bf16[589824]{0:T(1024)(128)(2,1)}, ...) all-reduce(f32[3072]{0:T(1024)S(1)} %pad_maximum_fusion, ...), channel_id=8, replica_groups=mesh['dp'=8,'head'=4] {'dp','head'}, use_global_device_ids=true, to_apply=%region_30.31.clone | all-reduce | flops 7080960 | bytes 42485760
  1078.0 39.3 %all-reduce.4 = bf16[3072]{0:T(1024)(128)(2,1)S(1)} all-reduce(bf16[3072]{0:T(1024)(128)(2,1)S(1)} %dynamic-update-slice), channel_id=1, replica_groups=mesh['dp'=8,'head'=4] {'dp','head'}, use_global_device_ids=true, to_apply=%add.4 | all-reduce | flops 3072 | bytes 12288
  1121.9 41.3 %all-gather.13.cloned.1.call-done = bf16[589824]{0:T(1024)(128)(2,1)} async-done(((bf16[18432]{0:T(1024)(128)(2,1)}), bf16[589824]{0:T(1024)(128)(2,1)}) %all-gather.13.cloned.1.call-update) | async-done | bytes 1179664 | tf_op jit(solution)/shard_map/all_gather | solution.py:201
  1166.5 53.1 %all-gather.9.cloned.1.call-done = bf16[589824]{0:T(1024)(128)(2,1)} async-done(((bf16[18432]{0:T(1024)(128)(2,1)}), bf16[589824]{0:T(1024)(128)(2,1)}) %all-gather.9.cloned.1.call-update) | async-done | bytes 1179664 | tf_op jit(solution)/shard_map/all_gather | solution.py:195
  1223.0 53.0 %all-gather.7.cloned.1.call-done = bf16[589824]{0:T(1024)(128)(2,1)} async-done(((bf16[18432]{0:T(1024)(128)(2,1)}), bf16[589824]{0:T(1024)(128)(2,1)}) %all-gather.7.cloned.1.call-update) | async-done | bytes 1179664 | tf_op jit(solution)/shard_map/all_gather | solution.py:192
  1279.3 62.6 %all-gather.15.cloned.1.call-done = bf16[2359296]{0:T(1024)(128)(2,1)} async-done(((bf16[73728]{0:T(1024)(128)(2,1)}), bf16[2359296]{0:T(1024)(128)(2,1)}) %all-gather.15.cloned.1.call-update) | async-done | bytes 4718608 | tf_op jit(solution)/shard_map/all_gather | solution.py:204
  1341.9 8.7 reshape.359
  1350.6 56.5 %all-gather.17.cloned.1.call-done = bf16[2359296]{0:T(1024)(128)(2,1)} async-done(((bf16[73728]{0:T(1024)(128)(2,1)}), bf16[2359296]{0:T(1024)(128)(2,1)}) %all-gather.17.cloned.1.call-update) | async-done | bytes 4718608 | tf_op jit(solution)/shard_map/all_gather | solution.py:207
  1407.1 10.0 reshape.361
  (278 shorter events, 361.6 us)
Async XLA Ops:
  7.2 33.1 %copy-start = (bf16[768,768]{1,0:T(8,128)(2,1)S(1)}, bf16[768,768]{1,0:T(8,128)(2,1)}, u32[]{:S(2)}) copy-start(bf16[768,768]{1,0:T(8,128)(2,1)} %param.12) | copy-start | bytes 3538948
  11.6 24.3 %all-to-all-start = ((bf16[1024,4,192]{0,2,1:T(8,128)(2,1)}), bf16[1024,4,192]{0,2,1:T(8,128)(2,1)S(1)}, u32[]{:S(2)}, u32[]{:S(2)}) async-start(bf16[1024,4,192]{0,2,1:T(8,128)(2,1)} %bitcast.195), calls=%async_computation | async-start | bytes 3145728 | tf_op jit(solution)/shard_map/all_to_all | solution.py:140
  35.9 24.5 %all-to-all-start.1 = ((bf16[1024,4,192]{0,2,1:T(8,128)(2,1)}), bf16[1024,4,192]{0,2,1:T(8,128)(2,1)}, u32[]{:S(2)}, u32[]{:S(2)}) async-start(bf16[1024,4,192]{0,2,1:T(8,128)(2,1)} %bitcast.193), calls=%async_computation.1 | async-start | bytes 3145728 | tf_op jit(solution)/shard_map/all_to_all | solution.py:138
  60.4 25.0 %all-to-all-start.2 = ((bf16[1024,4,192]{0,2,1:T(8,128)(2,1)}), bf16[1024,4,192]{0,2,1:T(8,128)(2,1)}, u32[]{:S(2)}, u32[]{:S(2)}) async-start(bf16[1024,4,192]{0,2,1:T(8,128)(2,1)} %bitcast.192), calls=%async_computation.2 | async-start | bytes 3145728 | tf_op jit(solution)/shard_map/all_to_all | solution.py:139
  65.6 93.4 %copy-start.27 = (f32[128,128]{0,1:T(8,128)}, f32[128,128]{0,1:T(8,128)S(1)}, u32[]{:S(2)}) copy-start(f32[128,128]{0,1:T(8,128)S(1)} %cosine_select_fusion) | copy-start | bytes 196612
  70.5 88.5 %copy-start.4 = (bf16[2,16,128,3,64]{2,1,0,4,3:T(8,128)(2,1)}, bf16[2,16,128,3,64]{2,1,0,4,3:T(8,128)(2,1)S(1)}, u32[]{:S(2)}) copy-start(bf16[2,16,128,3,64]{2,1,0,4,3:T(8,128)(2,1)S(1)} %reshape.320) | copy-start | bytes 4718596
  121.5 12.6 copy-start.1
  146.5 11.8 copy-start.2
  146.6 12.5 slice-start
  171.1 24.5 %all-to-all-start.3 = ((bf16[4,1024,192]{1,2,0:T(8,128)(2,1)}), bf16[4,1024,192]{1,2,0:T(8,128)(2,1)}, u32[]{:S(2)}, u32[]{:S(2)}) async-start(bf16[4,1024,192]{1,2,0:T(8,128)(2,1)} %copy.116), calls=%async_computation.3 | async-start | bytes 3145728 | tf_op jit(solution)/shard_map/all_to_all | solution.py:144
  195.6 40.0 %slice-start.4 = ((s8[4718592]{0:T(1024)(128)(4,1)}), s8[4194304]{0:T(1024)(128)(4,1)S(1)}, s32[]{:S(2)}) async-start(s8[4718592]{0:T(1024)(128)(4,1)} %bitcast.198), calls=%async_computation.18 | async-start | bytes 8388608
  199.5 36.1 %copy-start.22 = (f32[1024,768]{0,1:T(8,128)}, f32[1024,768]{0,1:T(8,128)S(1)}, u32[]{:S(2)}) copy-start(f32[1024,768]{0,1:T(8,128)S(1)} %get-tuple-element.97) | copy-start | bytes 9437188
  199.9 35.7 %copy-start.44 = (f32[1024]{0:T(1024)}, f32[1024]{0:T(1024)S(1)}, u32[]{:S(2)}) copy-start(f32[1024]{0:T(1024)S(1)} %multiply_reduce_fusion.4) | copy-start | bytes 12292
  200.0 35.6 %slice-start.5 = ((s8[4718592]{0:T(1024)(128)(4,1)}), s8[524288]{0:T(1024)(128)(4,1)S(1)}, s32[]{:S(2)}) async-start(s8[4718592]{0:T(1024)(128)(4,1)} %bitcast.198), calls=%async_computation.19 | async-start | bytes 1048576
  275.8 12.0 copy-start.45
  275.8 12.0 copy-start.23
  296.6 23.6 %all-to-all-start.4 = ((bf16[1024,4,192]{0,2,1:T(8,128)(2,1)}), bf16[1024,4,192]{0,2,1:T(8,128)(2,1)S(1)}, u32[]{:S(2)}, u32[]{:S(2)}) async-start(bf16[1024,4,192]{0,2,1:T(8,128)(2,1)} %bitcast.194), calls=%async_computation.4 | async-start | bytes 3145728 | tf_op jit(solution)/shard_map/all_to_all | solution.py:164
  329.5 12.4 copy-start.18
  329.5 12.4 copy-start.19
  329.6 12.4 copy-start.39
  480.5 56.5 %all-to-all-start.6 = ((bf16[4,1024,192]{1,2,0:T(8,128)(2,1)}), bf16[4,1024,192]{1,2,0:T(8,128)(2,1)}, u32[]{:S(2)}, u32[]{:S(2)}) async-start(bf16[4,1024,192]{1,2,0:T(8,128)(2,1)} %copy.142), calls=%async_computation.6 | async-start | bytes 3145728 | tf_op jit(solution)/shard_map/all_to_all | solution.py:169
  505.4 16.9 %slice-start.2 = ((s8[6291456]{0:T(1024)(128)(4,1)}), s8[2097152]{0:T(1024)(128)(4,1)S(1)}, s32[]{:S(2)}) async-start(s8[6291456]{0:T(1024)(128)(4,1)} %bitcast.189), calls=%async_computation.16 | async-start | bytes 4194304
  512.0 10.3 copy-start.20
  537.1 26.3 %all-to-all-start.5 = ((bf16[4,1024,192]{1,2,0:T(8,128)(2,1)}), bf16[4,1024,192]{1,2,0:T(8,128)(2,1)}, u32[]{:S(2)}, u32[]{:S(2)}) async-start(bf16[4,1024,192]{1,2,0:T(8,128)(2,1)} %copy.131), calls=%async_computation.5 | async-start | bytes 3145728 | tf_op jit(solution)/shard_map/all_to_all | solution.py:168
  563.4 24.5 %all-to-all-start.7 = ((bf16[4,1024,192]{1,2,0:T(8,128)(2,1)}), bf16[4,1024,192]{1,2,0:T(8,128)(2,1)}, u32[]{:S(2)}, u32[]{:S(2)}) async-start(bf16[4,1024,192]{1,2,0:T(8,128)(2,1)} %copy.150), calls=%async_computation.7 | async-start | bytes 3145728 | tf_op jit(solution)/shard_map/all_to_all | solution.py:170
  567.8 550.8 %all-gather.11.cloned.1.call-start = ((), (), s32[]{:S(2)}) async-start(), calls=%async_computation.10 | async-start | bytes 1216512 | tf_op jit(solution)/shard_map/all_gather | solution.py:198
  596.2 466.5 %copy-start.26 = (bf16[1024,768]{0,1:T(8,128)(2,1)S(1)}, bf16[1024,768]{0,1:T(8,128)(2,1)}, u32[]{:S(2)}) copy-start(bf16[1024,768]{0,1:T(8,128)(2,1)} %get-tuple-element.67) | copy-start | bytes 4718596
  1055.0 108.2 %all-gather.13.cloned.1.call-start = ((), (), s32[]{:S(2)}) async-start(), calls=%async_computation.11 | async-start | bytes 1216512 | tf_op jit(solution)/shard_map/all_gather | solution.py:201
  1056.4 163.2 %all-gather.9.cloned.1.call-start = ((), (), s32[]{:S(2)}) async-start(), calls=%async_computation.9 | async-start | bytes 1216512 | tf_op jit(solution)/shard_map/all_gather | solution.py:195
  1057.9 218.1 %all-gather.7.cloned.1.call-start = ((), (), s32[]{:S(2)}) async-start(), calls=%async_computation.8 | async-start | bytes 1216512 | tf_op jit(solution)/shard_map/all_gather | solution.py:192
  1059.3 282.5 %all-gather.15.cloned.1.call-start = ((), (), s32[]{:S(2)}) async-start(), calls=%async_computation.12 | async-start | bytes 4866048 | tf_op jit(solution)/shard_map/all_gather | solution.py:204
  1061.0 346.1 %all-gather.17.cloned.1.call-start = ((), (), s32[]{:S(2)}) async-start(), calls=%async_computation.13 | async-start | bytes 4866048 | tf_op jit(solution)/shard_map/all_gather | solution.py:207
  (43 other events, 227.4 us)
Sparse Core Ops, SparseCore 0:
  1055.1 52.0 all-gather.10
  1110.1 53.0 all-gather.12
  1166.6 52.9 all-gather.8
  1222.9 52.9 all-gather.6
  1279.3 62.5 all-gather.14
  1344.6 62.4 all-gather.16
where the time goes:
time: 1430 us; the launch traced here: 1420 us
  blocking collectives  497 us (35%)
  waiting for transfers between devices  314 us (22%)
  matrix products  308 us (22%)
  local copies, waits for them, and re-layouts  203 us (14%)
  other arithmetic  52.1 us (4%)
  starting transfers between devices  35.1 us (2%)
  between operations  15.4 us (1%)
    unnamed x2, blocking collectives  497 us
    dot_general x6, matrix products, plain_dot(): return jnp.dot(first_arg, second_arg, preferred_element_type=jnp.float32)  64.6 us
    all_gather x1, waiting for transfers between devices, local(): lax.all_gather(shares[4].astype(jnp.bfloat16), ('dp', 'head'), axis=0, ti...  62.6 us
    all_gather x1, waiting for transfers between devices, local(): lax.all_gather(shares[5].astype(jnp.bfloat16), ('dp', 'head'), axis=0, ti...  56.5 us
    all_gather x1, waiting for transfers between devices, local(): lax.all_gather(shares[1].astype(jnp.bfloat16), ('dp', 'head'), axis=0, ti...  53.1 us
    all_gather x1, waiting for transfers between devices, local(): lax.all_gather(shares[0].astype(jnp.bfloat16), ('dp', 'head'), axis=0, ti...  53 us
    dot_general x6, matrix products, second_trans_dot(): lax.dot_general(first_arg, second_arg, (((1,), (1,)), ((), ())), preferre...  42.9 us
    all_gather x1, waiting for transfers between devices, local(): lax.all_gather(shares[3].astype(jnp.bfloat16), ('dp', 'head'), axis=0, ti...  41.3 us
  transfers between devices with their start and end apart: 14, of which 11 were waited for; matrix products, arithmetic and copies ran while one was open for 13% of the time, Pallas kernels for 0%

commit v1 on v0

v1 whole, which is shorter than its diff:
```python
import functools
import math

import jax
import jax.numpy as jnp
import numpy as np
from jax import lax
from jax.experimental import pallas as pl
from jax.experimental.pallas import tpu as pltpu
from jax.sharding import PartitionSpec as P

D = 768
E = 64
FF = 3072
LENGTH = 2048
CHUNK = 256
PAIR = 2 * E
PAIRS = D // PAIR
FEAT = 2 * PAIR
EPSILON = 1e-05
STEP_ANGLE = 0.5 * math.pi / LENGTH
QUARTER = D // 4
LIMIT = 56 * 2**20

f32 = jnp.float32
bf16 = jnp.bfloat16


def nn(a, b):
    return jnp.dot(a, b, preferred_element_type=f32)


def tn(a, b):
    return lax.dot_general(a, b, (((0,), (0,)), ((), ())), preferred_element_type=f32)


def nt(a, b):
    return lax.dot_general(a, b, (((1,), (1,)), ((), ())), preferred_element_type=f32)


def params(**kw):
    return pltpu.CompilerParams(vmem_limit_bytes=LIMIT, **kw)


def softplus(x):
    return jnp.maximum(x, 0.0) + jnp.log1p(jnp.exp(-jnp.abs(x)))


def lane_head(rows):
    return (lax.broadcasted_iota(jnp.int32, (rows, PAIR), 1) >= E).astype(jnp.int32)


def row_head():
    return (lax.broadcasted_iota(jnp.int32, (FEAT, PAIR), 0) % PAIR >= E).astype(jnp.int32)


def unpack_state(packed):
    same = row_head() == lane_head(FEAT)
    left = jnp.where(same, packed, 0.0)
    right = jnp.where(same, pltpu.roll(packed, E, 1), 0.0)
    return jnp.concatenate([left, right], axis=1).astype(bf16)


def features(x, cosine, sine):
    return jnp.concatenate([x * cosine, x * sine], axis=1).astype(bf16)


def with_ones(v):
    return jnp.concatenate([v, jnp.ones_like(v)], axis=1)


def project_kernel(tok, wq, wk, wv, cos, sin, q_ref, k_ref, v_ref, pre_ref, tot_ref):
    @pl.when(pl.program_id(0) == 0)
    def _():
        tot_ref[...] = jnp.zeros_like(tot_ref)

    x = tok[...]
    q_ref[...] = softplus(nn(x, wq[...])).astype(bf16)
    k = softplus(nn(x, wk[...])).astype(bf16)
    k_ref[...] = k
    v = nn(x, wv[...]).astype(bf16)
    v_ref[...] = v
    same = row_head() == lane_head(FEAT)
    for p in range(PAIRS):
        cols = slice(p * PAIR, (p + 1) * PAIR)
        k_feat = features(k[:, cols].astype(f32), cos[...], sin[...])
        both = tn(k_feat, with_ones(v[:, cols]))
        pre_ref[0, p] = tot_ref[p]
        tot_ref[p] += jnp.where(same, both[:, :PAIR], both[:, PAIR:])


def project(tokens, wq, wk, wv, cos, sin):
    rows = tokens.shape[0]
    steps = rows // CHUNK
    chunk = pl.BlockSpec((CHUNK, D), lambda i: (i, 0))
    weight = pl.BlockSpec((D, D), lambda i: (0, 0))
    table = pl.BlockSpec((CHUNK, PAIR), lambda i: (i, 0))
    act = jax.ShapeDtypeStruct((rows, D), bf16)
    return pl.pallas_call(
        project_kernel,
        grid=(steps,),
        in_specs=[chunk, weight, weight, weight, table, table],
        out_specs=[
            chunk,
            chunk,
            chunk,
            pl.BlockSpec((1, PAIRS, FEAT, PAIR), lambda i: (i, 0, 0, 0)),
            pl.BlockSpec((PAIRS, FEAT, PAIR), lambda i: (0, 0, 0)),
        ],
        out_shape=[
            act,
            act,
            act,
            jax.ShapeDtypeStruct((steps, PAIRS, FEAT, PAIR), f32),
            jax.ShapeDtypeStruct((PAIRS, FEAT, PAIR), f32),
        ],
        compiler_params=params(),
        cost_estimate=pl.CostEstimate(flops=6 * rows * D * D, bytes_accessed=16 * rows * D, transcendentals=0),
        name="project",
    )(tokens, wq, wk, wv, cos, sin)


def norm_parts(z):
    centred = z - jnp.mean(z, axis=-1, keepdims=True)
    rstd = lax.rsqrt(jnp.mean(centred * centred, axis=-1, keepdims=True) + EPSILON)
    return centred * rstd, rstd


def norm_back(t, n, rstd):
    return (t - jnp.mean(t, axis=-1, keepdims=True) - n * jnp.mean(t * n, axis=-1, keepdims=True)) * rstd


def forward_kernel(
    coef, tok, q_ref, k_ref, v_ref, pre, init, cos, sin, table, w_out, w_up, w_down, gains, biases, cot,
    mixed_ref, inv_ref, state_ref, n0_ref, rstd_ref, low_ref, hidden_ref, slope_ref, out_ref, dres_ref, dffn_ref, ng_ref,
):
    turn_cos, turn_sin = coef[0], coef[1]
    second = lane_head(CHUNK) == 1
    second2 = jnp.concatenate([second, second], axis=1)
    for p in range(PAIRS):
        cols = slice(p * PAIR, (p + 1) * PAIR)
        start_cos, start_sin = init[p, :PAIR], init[p, PAIR:]
        turned = jnp.concatenate(
            [turn_cos * start_cos + turn_sin * start_sin, turn_cos * start_sin - turn_sin * start_cos], axis=0
        )
        state = unpack_state(pre[0, p] + turned)
        state_ref[0, p] = state
        q, k, v = q_ref[:, cols], k_ref[:, cols], v_ref[:, cols]
        total = nn(features(q.astype(f32), cos[...], sin[...]), state)
        v_ones = with_ones(v)
        zero = jnp.zeros_like(q)
        score_0 = (nt(jnp.where(second, zero, q), k) * table[...]).astype(bf16)
        score_1 = (nt(jnp.where(second, q, zero), k) * table[...]).astype(bf16)
        total += jnp.where(second2, nn(score_1, v_ones), nn(score_0, v_ones))
        inv = 1.0 / total[:, PAIR:]
        mixed_ref[:, cols] = (total[:, :PAIR] * inv).astype(bf16)
        inv_ref[:, cols] = inv
    z = tok[...].astype(f32) + nn(mixed_ref[...], w_out[...])
    n0, rstd = norm_parts(z)
    n0_ref[...] = n0.astype(bf16)
    rstd_ref[...] = jnp.broadcast_to(rstd, rstd_ref.shape)
    normed = n0 * gains[0:1] + biases[0:1]
    low = normed.astype(bf16)
    low_ref[...] = low
    for j in range(FF // D):
        cols = slice(j * D, (j + 1) * D)
        h = nn(low, w_up[:, cols])
        phi = 0.5 * (1.0 + lax.erf(h * (0.5**0.5)))
        hidden_ref[:, cols] = (h * phi).astype(bf16)
        slope_ref[:, cols] = (phi + h * jnp.exp(-0.5 * h * h) * ((2 * math.pi) ** -0.5)).astype(bf16)
    z = normed + nn(hidden_ref[...], w_down[...])
    n1, rstd = norm_parts(z)
    out_ref[...] = (n1 * gains[1:2] + biases[1:2]).astype(bf16)
    g = cot[...].astype(f32)
    dres = norm_back(g * gains[1:2], n1, rstd)
    dres_ref[...] = dres
    dffn_ref[...] = dres.astype(bf16)

    @pl.when(pl.program_id(0) == 0)
    def _():
        ng_ref[...] = jnp.zeros_like(ng_ref)

    ng_ref[0:1] += jnp.sum(g * n1, axis=0, keepdims=True)
    ng_ref[1:2] += jnp.sum(g, axis=0, keepdims=True)


def forward(coef, tokens, q, k, v, pre, init, cos, sin, table, w_out, w_up, w_down, gains, biases, cot):
    rows = tokens.shape[0]
    steps = rows // CHUNK
    chunk = pl.BlockSpec((CHUNK, D), lambda i: (i, 0))
    wide = pl.BlockSpec((CHUNK, FF), lambda i: (i, 0))
    thin = pl.BlockSpec((CHUNK, PAIR), lambda i: (i, 0))

    def whole(*shape):
        return pl.BlockSpec(shape, lambda i: (0,) * len(shape))

    state = pl.BlockSpec((1, PAIRS, FEAT, PAIR), lambda i: (i, 0, 0, 0))
    state_out = pl.BlockSpec((1, PAIRS, FEAT, FEAT), lambda i: (i, 0, 0, 0))

    def make(width, dtype):
        return jax.ShapeDtypeStruct((rows, width), dtype)

    return pl.pallas_call(
        forward_kernel,
        grid=(steps,),
        in_specs=[
            pl.BlockSpec(memory_space=pltpu.SMEM), chunk, chunk, chunk, chunk, state, whole(PAIRS, FEAT, PAIR), thin, thin,
            whole(CHUNK, CHUNK), whole(D, D), whole(D, FF), whole(FF, D), whole(2, D), whole(2, D), chunk,
        ],
        out_specs=[chunk, chunk, state_out, chunk, thin, chunk, wide, wide, chunk, chunk, chunk, whole(2, D)],
        out_shape=[
            make(D, bf16), make(D, f32), jax.ShapeDtypeStruct((steps, PAIRS, FEAT, FEAT), bf16), make(D, bf16),
            make(PAIR, f32), make(D, bf16), make(FF, bf16), make(FF, bf16), make(D, bf16), make(D, f32), make(D, bf16),
            jax.ShapeDtypeStruct((2, D), f32),
        ],
        compiler_params=params(),
        cost_estimate=pl.CostEstimate(
            flops=2 * rows * (D * D + 2 * D * FF) + 24 * 6 * 2 * 256**3, bytes_accessed=60 * rows * D, transcendentals=0
        ),
        name="forward",
    )(coef, tokens, q, k, v, pre, init, cos, sin, table, w_out, w_up, w_down, gains, biases, cot)


def backward_kernel(
    dffn, slope, dres, n0_ref, rstd_ref, mixed, inv, q_ref, cos, sin, w_out, w_up, w_down, gains,
    dhid_ref, dres_one_ref, dbranch_ref, dnum_ref, dden_ref, part_ref, tot_ref, ng_ref,
):
    @pl.when(pl.program_id(0) == 0)
    def _():
        ng_ref[...] = jnp.zeros_like(ng_ref)
        tot_ref[...] = jnp.zeros_like(tot_ref)

    for j in range(FF // D):
        cols = slice(j * D, (j + 1) * D)
        dhid_ref[:, cols] = (nt(dffn[...], w_down[cols, :]) * slope[:, cols].astype(f32)).astype(bf16)
    g = dres[...] + nt(dhid_ref[...], w_up[...])
    n0 = n0_ref[...].astype(f32)
    ng_ref[0:1] += jnp.sum(g * n0, axis=0, keepdims=True)
    ng_ref[1:2] += jnp.sum(g, axis=0, keepdims=True)
    dres_one = norm_back(g * gains[0:1], n0, rstd_ref[:, 0:1])
    dres_one_ref[...] = dres_one
    dbranch = dres_one.astype(bf16)
    dbranch_ref[...] = dbranch
    dmixed = nt(dbranch, w_out[...]).astype(bf16).astype(f32)
    second = lane_head(CHUNK) == 1
    lane = lax.broadcasted_iota(jnp.int32, (CHUNK, PAIR), 1)
    same = row_head() == lane_head(FEAT)
    for p in range(PAIRS):
        cols = slice(p * PAIR, (p + 1) * PAIR)
        inv_p = inv[:, cols]
        dnum = (dmixed[:, cols] * inv_p).astype(bf16)
        dnum_ref[:, cols] = dnum
        moment = dnum.astype(f32) * mixed[:, cols].astype(f32)
        first_sum = jnp.sum(jnp.where(second, 0.0, moment), axis=1, keepdims=True)
        second_sum = jnp.sum(jnp.where(second, moment, 0.0), axis=1, keepdims=True)
        dden = jnp.where(second, second_sum, first_sum) * (-2.0 / E)
        high = dden.astype(bf16)
        rest = (dden - high.astype(f32)).astype(bf16)
        dden = jnp.where(lane % E < E // 2, high, rest)
        dden_ref[:, cols] = dden
        both = tn(features(q_ref[:, cols].astype(f32), cos[...], sin[...]), jnp.concatenate([dnum, dden], axis=1))
        part = jnp.where(same, both[:, :PAIR], pltpu.roll(both[:, PAIR:], E, 1))
        part_ref[0, p] = part
        tot_ref[p] += part


def backward(dffn, slope, dres, n0, rstd, mixed, inv, q, cos, sin, w_out, w_up, w_down, gains):
    rows = dffn.shape[0]
    steps = rows // CHUNK
    chunk = pl.BlockSpec((CHUNK, D), lambda i: (i, 0))
    wide = pl.BlockSpec((CHUNK, FF), lambda i: (i, 0))
    thin = pl.BlockSpec((CHUNK, PAIR), lambda i: (i, 0))

    def whole(*shape):
        return pl.BlockSpec(shape, lambda i: (0,) * len(shape))

    def make(width, dtype):
        return jax.ShapeDtypeStruct((rows, width), dtype)

    return pl.pallas_call(
        backward_kernel,
        grid=(steps,),
        in_specs=[
            chunk, wide, chunk, chunk, thin, chunk, chunk, chunk, thin, thin,
            whole(D, D), whole(D, FF), whole(FF, D), whole(2, D),
        ],
        out_specs=[
            wide, chunk, chunk, chunk, chunk, pl.BlockSpec((1, PAIRS, FEAT, PAIR), lambda i: (i, 0, 0, 0)),
            whole(PAIRS, FEAT, PAIR), whole(2, D),
        ],
        out_shape=[
            make(FF, bf16), make(D, f32), make(D, bf16), make(D, bf16), make(D, bf16),
            jax.ShapeDtypeStruct((steps, PAIRS, FEAT, PAIR), f32), jax.ShapeDtypeStruct((PAIRS, FEAT, PAIR), f32),
            jax.ShapeDtypeStruct((2, D), f32),
        ],
        compiler_params=params(),
        cost_estimate=pl.CostEstimate(
            flops=2 * rows * (D * D + 2 * D * FF), bytes_accessed=50 * rows * D, transcendentals=0
        ),
        name="backward",
    )(dffn, slope, dres, n0, rstd, mixed, inv, q, cos, sin, w_out, w_up, w_down, gains)


def attend_back_kernel(
    coef, q_ref, k_ref, v_ref, dnum_ref, dden_ref, state_ref, part, init, cos, sin, table, table_t,
    dq_ref, dk_ref, dv_ref, run,
):
    @pl.when(pl.program_id(0) == 0)
    def _():
        turn_cos, turn_sin = coef[0], coef[1]
        for p in range(PAIRS):
            d_cos, d_sin = init[p, :PAIR], init[p, PAIR:]
            run[p, :PAIR] = turn_cos * d_cos - turn_sin * d_sin
            run[p, PAIR:] = turn_sin * d_cos + turn_cos * d_sin

    second = lane_head(CHUNK) == 1
    second2 = jnp.concatenate([second, second], axis=1)

    def split(x, mask):
        zero = jnp.zeros_like(x)
        return jnp.where(mask, zero, x), jnp.where(mask, x, zero)

    for p in range(PAIRS):
        cols = slice(p * PAIR, (p + 1) * PAIR)
        q, k, v = q_ref[:, cols], k_ref[:, cols], v_ref[:, cols]
        q_wide, k_wide = q.astype(f32), k.astype(f32)
        dnum = dnum_ref[:, cols]
        grad = jnp.concatenate([dnum, dden_ref[:, cols]], axis=1)
        v_ones = with_ones(v)
        d_state = unpack_state(run[p])
        run[p] += part[0, p]
        dq_feat = nt(grad, state_ref[0, p])
        dk_feat = nt(v_ones, d_state)
        dv = nn(features(k_wide, cos[...], sin[...]), d_state[:, :PAIR])
        dq = dq_feat[:, :PAIR] * cos[...] + dq_feat[:, PAIR:] * sin[...]
        dk = dk_feat[:, :PAIR] * cos[...] + dk_feat[:, PAIR:] * sin[...]
        for grad_h, q_h, k_h, dnum_h in zip(split(grad, second2), split(q, second), split(k, second), split(dnum, second)):
            d_score = (nt(grad_h, v_ones) * table[...]).astype(bf16)
            dq += nn(d_score, k_h)
            score_t = (nt(k_h, q) * table_t[...]).astype(bf16)
            d_score_t = (nt(v_ones, grad_h) * table_t[...]).astype(bf16)
            dk += nn(d_score_t, q_h)
            dv += nn(score_t, dnum_h)
        dq_ref[:, cols] = (dq.astype(bf16).astype(f32) * sigmoid_of(q_wide)).astype(bf16)
        dk_ref[:, cols] = (dk.astype(bf16).astype(f32) * sigmoid_of(k_wide)).astype(bf16)
        dv_ref[:, cols] = dv.astype(bf16)


def sigmoid_of(soft):
    return jnp.where(soft < 0.01, soft * (1.0 - 0.5 * soft), 1.0 - jnp.exp(-soft))


def attend_back(coef, q, k, v, dnum, dden, state, part, init, cos, sin, table, table_t):
    rows = q.shape[0]
    steps = rows // CHUNK
    last = steps - 1
    chunk = pl.BlockSpec((CHUNK, D), lambda i: (last - i, 0))
    thin = pl.BlockSpec((CHUNK, PAIR), lambda i: (last - i, 0))
    square = pl.BlockSpec((CHUNK, CHUNK), lambda i: (0, 0))
    act = jax.ShapeDtypeStruct((rows, D), bf16)
    return pl.pallas_call(
        attend_back_kernel,
        grid=(steps,),
        in_specs=[
            pl.BlockSpec(memory_space=pltpu.SMEM), chunk, chunk, chunk, chunk, chunk,
            pl.BlockSpec((1, PAIRS, FEAT, FEAT), lambda i: (last - i, 0, 0, 0)),
            pl.BlockSpec((1, PAIRS, FEAT, PAIR), lambda i: (last - i, 0, 0, 0)),
            pl.BlockSpec((PAIRS, FEAT, PAIR), lambda i: (0, 0, 0)), thin, thin, square, square,
        ],
        out_specs=[chunk, chunk, chunk],
        out_shape=[act, act, act],
        scratch_shapes=[pltpu.VMEM((PAIRS, FEAT, PAIR), f32)],
        compiler_params=params(),
        cost_estimate=pl.CostEstimate(flops=24 * 16 * 2 * 256**3, bytes_accessed=24 * rows * D, transcendentals=0),
        name="attend_back",
    )(coef, q, k, v, dnum, dden, state, part, init, cos, sin, table, table_t)


def token_grad_kernel(dres_one, dq, dk, dv, wq, wk, wv, out):
    out[...] = dres_one[...] + nt(dq[...], wq[...]) + nt(dk[...], wk[...]) + nt(dv[...], wv[...])


def token_grad(dres_one, dq, dk, dv, wq, wk, wv):
    rows = dq.shape[0]
    chunk = pl.BlockSpec((CHUNK, D), lambda i: (i, 0))
    weight = pl.BlockSpec((D, D), lambda i: (0, 0))
    return pl.pallas_call(
        token_grad_kernel,
        grid=(rows // CHUNK,),
        in_specs=[chunk] * 4 + [weight] * 3,
        out_specs=chunk,
        out_shape=jax.ShapeDtypeStruct((rows, D), f32),
        compiler_params=params(),
        cost_estimate=pl.CostEstimate(flops=6 * rows * D * D, bytes_accessed=14 * rows * D, transcendentals=0),
        name="token_grad",
    )(dres_one, dq, dk, dv, wq, wk, wv)


def place_rows(value, ref, me, block, index):
    for b in range(D // block):
        to = pl.multiple_of((jnp.int32(b) ^ me) * block, block)
        ref[index, pl.ds(to, block), :] = value[b * block : (b + 1) * block]


def unit_send_kernel(block, pick, sc, a, b, out):
    u = pl.program_id(0)
    place_rows(tn(a[...], b[...]).astype(bf16), out, sc[1 + u], block, 0)


def unit_keep_kernel(block, pick, sc, a, b, got, out, wide):
    u = pl.program_id(0)
    place_rows(tn(a[...], b[...]), wide, sc[1 + u], block, 0)
    out[0] = (wide[0] + got[0].astype(f32)).astype(bf16)


def unit_call(sc, a, b, own, block, a_split, b_split, got=None):
    rows = a.shape[0]

    def unit(i, sc):
        return 2 * (sc[0] if own else 1 - sc[0]) + i

    def spec(split):
        return pl.BlockSpec((rows, D), (lambda i, sc: (0, unit(i, sc))) if split else (lambda i, sc: (0, 0)))

    out_spec = pl.BlockSpec((1, D, D), lambda i, sc: (i, 0, 0))
    ins, specs, scratch = [a, b], [spec(a_split), spec(b_split)], []
    kernel = unit_send_kernel
    if got is not None:
        ins.append(got)
        specs.append(out_spec)
        scratch = [pltpu.VMEM((1, D, D), f32)]
        kernel = unit_keep_kernel
    return pl.pallas_call(
        functools.partial(kernel, block, None),
        grid_spec=pltpu.PrefetchScalarGridSpec(
            num_scalar_prefetch=1, grid=(2,), in_specs=specs, out_specs=out_spec, scratch_shapes=scratch
        ),
        out_shape=jax.ShapeDtypeStruct((2, D, D), bf16),
        compiler_params=params(),
        cost_estimate=pl.CostEstimate(flops=4 * rows * D * D, bytes_accessed=8 * rows * D, transcendentals=0),
        name="unit_keep" if own else "unit_send",
    )(sc, *ins)


def pick_kernel(block, unit, sc, mine, other, out):
    owner, me = unit // 2, sc[1 + unit % 2]

    def put(ref):
        for b in range(D // block):
            at = pl.multiple_of((jnp.int32(b) ^ me) * block, block)
            out[b * block : (b + 1) * block, :] = ref[0, pl.ds(at, block), :].astype(f32)

    @pl.when(sc[0] == owner)
    def _():
        put(mine)

    @pl.when(sc[0] != owner)
    def _():
        put(other)


def pick_unit(sc, mine, other, unit, block):
    spec = pl.BlockSpec((1, D, D), lambda i, sc: (unit % 2, 0, 0))
    return pl.pallas_call(
        functools.partial(pick_kernel, block, unit),
        grid_spec=pltpu.PrefetchScalarGridSpec(
            num_scalar_prefetch=1,
            grid=(1,),
            in_specs=[spec, spec],
            out_specs=pl.BlockSpec((D, D), lambda i, sc: (0, 0)),
        ),
        out_shape=jax.ShapeDtypeStruct((D, D), f32),
        compiler_params=params(),
        name="pick_unit",
    )(sc, mine, other)


def gather_kernel(block, sc, mine, other, out):
    g = pl.program_id(0)
    me = jnp.where(g % 2 == 0, sc[1], sc[2])

    def put(ref):
        for b in range(D // block):
            at = pl.multiple_of((jnp.int32(b) ^ me) * block, block)
            out[b * block : (b + 1) * block, :] = ref[0, pl.ds(at, block), :].astype(f32)

    @pl.when(g // 2 == sc[0])
    def _():
        put(mine)

    @pl.when(g // 2 != sc[0])
    def _():
        put(other)


def gather_units(sc, mine, other, block, by_rows):
    def at(own):
        def index(g, sc):
            first = 2 * (sc[0] if own else 1 - sc[0])
            return (jnp.clip(g - first, 0, 1), 0, 0)

        return index

    return pl.pallas_call(
        functools.partial(gather_kernel, block),
        grid_spec=pltpu.PrefetchScalarGridSpec(
            num_scalar_prefetch=1,
            grid=(4,),
            in_specs=[pl.BlockSpec((1, D, D), at(True)), pl.BlockSpec((1, D, D), at(False))],
            out_specs=pl.BlockSpec((D, D), (lambda g, sc: (g, 0)) if by_rows else (lambda g, sc: (0, g))),
        ),
        out_shape=jax.ShapeDtypeStruct((4 * D, D) if by_rows else (D, 4 * D), f32),
        compiler_params=params(),
        name="gather_units",
    )(sc, mine, other)


def add_low(*terms):
    total = terms[0].astype(f32)
    for term in terms[1:]:
        total = total + term.astype(f32)
    return total.astype(bf16)


def make_local(n_dp, n_head):
    n_z = n_dp // 2
    direct = QUARTER % (16 * n_z) == 0 and n_z & (n_z - 1) == 0
    places = n_z if direct else 1
    block = QUARTER // places

    def swap(x, axis, size, bit):
        return lax.ppermute(x, axis, [(i, i ^ bit) for i in range(size)])

    def swap_core(x):
        return swap(x, "head", n_head, 1)

    def swap_x(x):
        return swap(x, "head", n_head, 2)

    def swap_y(x):
        return swap(x, "dp", n_dp, 1)

    def swap_z(x, k):
        return swap(x, "dp", n_dp, 2 * k)

    half = D // 2

    def reduce_units(units):
        a, b = units[0], units[1]
        got_a, got_b = swap_x(a[half:]), swap_y(b[half:])
        a, b = add_low(a[:half], got_a), add_low(b[:half], got_b)
        got_a, got_b = swap_y(a[QUARTER:]), swap_x(b[QUARTER:])
        if direct:
            def part(k):
                at = slice(k * block, (k + 1) * block)
                return jnp.concatenate([add_low(a[at], got_a[at]), add_low(b[at], got_b[at])])

            got = [swap_z(part(k), k) for k in range(1, n_z)]
            share = add_low(part(0), *got)
            parts = [share] + [swap_z(share, k) for k in range(1, n_z)]
            a = jnp.concatenate([p[:block] for p in parts])
            b = jnp.concatenate([p[block:] for p in parts])
        else:
            both = jnp.concatenate([add_low(a[:QUARTER], got_a), add_low(b[:QUARTER], got_b)])
            same_z = [[2 * z + y for z in range(n_z)] for y in range(2)]
            both = lax.psum(both.astype(f32), "dp", axis_index_groups=same_z).astype(bf16)
            a, b = both[:QUARTER], both[QUARTER:]
        got_a, got_b = swap_y(a), swap_x(b)
        a, b = jnp.concatenate([a, got_a]), jnp.concatenate([b, got_b])
        got_a, got_b = swap_x(a), swap_y(b)
        return jnp.stack([jnp.concatenate([a, got_a]), jnp.concatenate([b, got_b])])

    def local(tokens, w_query, w_key, w_value, w_out, w_up, w_down, norm_gains, norm_biases, cotangent):
        rows = tokens.shape[0]
        assert LENGTH == 2 * rows and n_head % 4 == 0 and n_dp % 2 == 0
        head, dp = lax.axis_index("head"), lax.axis_index("dp")
        core, x, y, z = head % 2, head // 2, dp % 2, dp // 2
        rank = z if direct else 0
        sc = jnp.stack([core, (2 * x + y) * places + rank, (2 * y + x) * places + rank]).astype(jnp.int32)
        angle = STEP_ANGLE * np.arange(rows)
        cos = jnp.asarray(np.broadcast_to(np.cos(angle)[:, None], (rows, PAIR)), f32)
        sin = jnp.asarray(np.broadcast_to(np.sin(angle)[:, None], (rows, PAIR)), f32)
        gap = np.arange(CHUNK)[:, None] - np.arange(CHUNK)[None, :]
        weights = np.where(gap >= 0, np.cos(STEP_ANGLE * gap), 0.0)
        table, table_t = jnp.asarray(weights, f32), jnp.asarray(weights.T, f32)
        turn = jnp.asarray([math.cos(STEP_ANGLE * rows), math.sin(STEP_ANGLE * rows)], f32)
        later = core.astype(f32)

        q, k, v, pre, total = project(tokens, w_query, w_key, w_value, cos, sin)
        init = swap_core(total)
        mixed, inv, state, n0, rstd, low, hidden, slope, out, dres, dffn, ng_two = forward(
            turn * later, tokens, q, k, v, pre, init, cos, sin, table, w_out, w_up, w_down, norm_gains, norm_biases, cotangent
        )
        down_got = swap_core(unit_call(sc, hidden, dffn, False, block, True, False))
        down = unit_call(sc, hidden, dffn, True, block, True, False, down_got)
        dhid, dres_one, dbranch, dnum, dden, part, d_total, ng_one = backward(
            dffn, slope, dres, n0, rstd, mixed, inv, q, cos, sin, w_out, w_up, w_down, norm_gains
        )
        d_init = swap_core(d_total)
        up_got = swap_core(unit_call(sc, low, dhid, False, block, False, True))
        up = unit_call(sc, low, dhid, True, block, False, True, up_got)
        dq, dk, dv = attend_back(turn * (1.0 - later), q, k, v, dnum, dden, state, part, d_init, cos, sin, table, table_t)
        rest_a = jnp.concatenate([mixed, tokens, tokens, tokens], axis=1)
        rest_b = jnp.concatenate([dbranch, dq, dk, dv], axis=1)
        rest_got = swap_core(unit_call(sc, rest_a, rest_b, False, block, True, True))
        rest = unit_call(sc, rest_a, rest_b, True, block, True, True, rest_got)
        d_tokens = token_grad(dres_one, dq, dk, dv, w_query, w_key, w_value)

        down = reduce_units(down)
        up = reduce_units(up)
        rest = reduce_units(rest)
        down_other, up_other, rest_other = swap_core(down), swap_core(up), swap_core(rest)
        grad_down = gather_units(sc, down, down_other, block, True)
        grad_up = gather_units(sc, up, up_other, block, False)
        grads = [pick_unit(sc, rest, rest_other, u, block) for u in range(4)]

        norm = jnp.concatenate([ng_one, ng_two])
        norm = norm + swap_core(norm)
        norm = norm + swap_x(norm)
        norm = norm + swap_y(norm)
        if n_z & (n_z - 1) == 0:
            bit = 1
            while bit < n_z:
                norm = norm + swap_z(norm, bit)
                bit *= 2
        else:
            norm = lax.psum(norm, "dp", axis_index_groups=[[2 * i + j for i in range(n_z)] for j in range(2)])
        return (
            out, d_tokens, grads[1], grads[2], grads[3], grads[0], grad_up, grad_down,
            jnp.stack([norm[0], norm[2]]), jnp.stack([norm[1], norm[3]]),
        )

    return local


def solution(mesh):
    rows, whole = P(("dp", "head"), None), P()
    return jax.shard_map(
        make_local(mesh.shape["dp"], mesh.shape["head"]),
        mesh=mesh,
        in_specs=(rows,) + (whole,) * 8 + (rows,),
        out_specs=(rows, rows) + (whole,) * 8,
        check_vma=False,
    )
```

time: 1430 us -> 396 us (0.28)
  blocking collectives: 497 us -> 0 us
  matrix products: 308 us -> 0 us
  waiting for transfers between devices: 314 us -> 110 us
  local copies, waits for them, and re-layouts: 203 us -> 22.3 us
  Pallas kernels: 0 us -> 180 us
  other arithmetic: 52.1 us -> 5.14 us
  starting transfers between devices: 35.1 us -> 69.5 us
    unnamed x2 -> x0, blocking collectives: 497 us -> none
    dot_general x38 -> x0, matrix products: 286 us -> none  [the longest x6 64.6 us: plain_dot(): return jnp.dot(first_arg, second_arg, preferred_element_type=jnp.float32)]
    all_gather x6 -> x0, waiting for transfers between devices: 266 us -> none  [the longest x1 62.6 us: local(): lax.all_gather(shares[4].astype(jnp.bfloat16), ('dp', 'head'), axis=0, ti...]
    pallas_call x0 -> x17, Pallas kernels: none -> 180 us  [the longest x6 42.8 us: unit_call(): pl.pallas_call(functools.partial(kernel, block, None), grid_spec=pltpu.Pr...]
    ppermute x0 -> x55, waiting for transfers between devices: none -> 110 us  [swap(): return lax.ppermute(x, axis, [(i, i ^ bit) for i in range(size)])]
    reshape x20 -> x0, local copies, waits for them, and re-layouts: 90.3 us -> none  [the longest x1 10.8 us: local(): grad_down.reshape(-1)]
    ppermute x0 -> x55, starting transfers between devices: none -> 69.5 us  [swap(): return lax.ppermute(x, axis, [(i, i ^ bit) for i in range(size)])]
    all_to_all x8 -> x0, waiting for transfers between devices: 47.3 us -> none  [the longest x1 13.7 us: local(): lax.all_to_all(queries, 'head', split_axis=1, concat_axis=0, tiled=True)]
  transfers between devices with their start and end apart: 14 -> 55, of which waited for: 11 -> 28; matrix products, arithmetic and copies ran while one was open for 13% -> 4% of each run, Pallas kernels for 0% -> 28%
where the time goes in v1:
time: 396 us; the launch traced here: 389 us
  Pallas kernels  180 us (45%)
  waiting for transfers between devices  110 us (28%)
  starting transfers between devices  69.5 us (18%)
  local copies, waits for them, and re-layouts  22.3 us (6%)
  other arithmetic  5.14 us (1%)
    ppermute x55, waiting for transfers between devices, swap(): return lax.ppermute(x, axis, [(i, i ^ bit) for i in range(size)])  110 us
    ppermute x55, starting transfers between devices, swap(): return lax.ppermute(x, axis, [(i, i ^ bit) for i in range(size)])  69.5 us
    pallas_call x6, Pallas kernels, unit_call(): pl.pallas_call(functools.partial(kernel, block, None), grid_spec=pltpu.Pr...  42.8 us
    pallas_call x1, Pallas kernels, forward(): pl.pallas_call(forward_kernel, grid=(steps,), in_specs=[pl.BlockSpec(memo...  36.1 us
    pallas_call x1, Pallas kernels, backward(): pl.pallas_call(backward_kernel, grid=(steps,), in_specs=[chunk, wide, chu...  26.8 us
    pallas_call x1, Pallas kernels, attend_back(): pl.pallas_call(attend_back_kernel, grid=(steps,), in_specs=[pl.BlockSpec(...  23.5 us
    unnamed x54, local copies, waits for them, and re-layouts  16 us
    pallas_call x4, Pallas kernels, pick_unit(): pl.pallas_call(functools.partial(pick_kernel, block, unit), grid_spec=plt...  15.4 us
  transfers between devices with their start and end apart: 55, of which 28 were waited for; matrix products, arithmetic and copies ran while one was open for 4% of the time, Pallas kernels for 28%

profile of v1, /device:TPU:0, one launch (start us, length us, event | category | flops | bytes accessed | tf_op | source)
XLA Modules:
  0.0 388.6 jit_solution(3302074434057900621)
XLA Ops:
  0.6 11.0 %project.1 = (bf16[1024,768]{1,0:T(8,128)(2,1)}, bf16[1024,768]{1,0:T(8,128)(2,1)}, bf16[1024,768]{1,0:T(8,128)(2,1)}, f32[4,6,256,128]{3,2,1,0:T(8,128)}, f32[6,256,128]{2,1,0:T(8,128)}) custom-call(bf16[1024,768]{1,0:T(8,128)(2,1)} %tok.3, bf16[768,768]{1,0:T(8,128)(2,1)} %wq.3, bf16[768,768]{1,0:T(8,128)(2,1)} %wk.3, bf16[768,768]{1,0:T(8,128)(2,1)} %wv.3, ...), custom_call_target="tpu_custom_call" | custom-call | flops 3623878656 | bytes 12582912 | tf_op jit(solution)/shard_map/project/pallas_call | solution.py:99
  15.2 36.1 %forward.1 = (bf16[1024,768]{1,0:T(8,128)(2,1)}, f32[1024,768]{1,0:T(8,128)}, bf16[4,6,256,256]{3,2,1,0:T(8,128)(2,1)}, bf16[1024,768]{1,0:T(8,128)(2,1)}, f32[1...) custom-call(f32[2]{0:T(128)} %broadcast.8.coef, ...), custom_call_target="tpu_custom_call" | custom-call | flops 15703474176 | bytes 47185920 | tf_op jit(solution)/shard_map/forward/pallas_call | solution.py:203
  51.3 6.5 %unit_send.5 = bf16[2,768,768]{2,1,0:T(8,128)(2,1)} custom-call(s32[3]{0:T(128)} %pad_add_fusion.sc, bf16[1024,3072]{1,0:T(8,128)(2,1)} %get-tuple-element.63.a, bf16[1024,768]{1,0:T(8,128)(2,1)} %get-tuple-element.44.dffn.b), custom_call_target="tpu_custom_call" | custom-call | flops 2415919104 | bytes 6291456 | tf_op jit(solution)/shard_map/unit_send/pallas_call | solution.py:433
  58.2 26.8 %backward.1 = (bf16[1024,3072]{1,0:T(8,128)(2,1)}, f32[1024,768]{1,0:T(8,128)}, bf16[1024,768]{1,0:T(8,128)(2,1)}, bf16[1024,768]{1,0:T(8,128)(2,1)}, bf16[1024,...) custom-call(bf16[1024,768]{1,0:T(8,128)(2,1)} %get-tuple-element.44.dffn.b, ...), custom_call_target="tpu_custom_call" | custom-call | flops 10871635968 | bytes 39321600 | tf_op jit(solution)/shard_map/backward/pallas_call | solution.py:280
  85.2 6.6 %unit_send.4 = bf16[2,768,768]{2,1,0:T(8,128)(2,1)} custom-call(s32[3]{0:T(128)} %pad_add_fusion.sc, bf16[1024,768]{1,0:T(8,128)(2,1)} %get-tuple-element.61.a, bf16[1024,3072]{1,0:T(8,128)(2,1)} %get-tuple-element.62.b), custom_call_target="tpu_custom_call" | custom-call | flops 2415919104 | bytes 6291456 | tf_op jit(solution)/shard_map/unit_send/pallas_call | solution.py:433
  97.7 23.5 %attend_back.1 = (bf16[1024,768]{1,0:T(8,128)(2,1)}, bf16[1024,768]{1,0:T(8,128)(2,1)}, bf16[1024,768]{1,0:T(8,128)(2,1)}) custom-call(f32[2]{0:T(128)} %broadcast.11.coef, bf16[1024,768]{1,0:T(8,128)(2,1)} %get-tuple-element.38.q_ref, bf16[1024,768]{1,0:T(8,128)(2,1)} %get-tuple-element.39.k_ref, bf16[1024,768]{1,0:T(8,128)(2,1)} %get-tuple-element.40.v_ref, ...), custom_call_target="tpu_custom_call" | custom-call | flops 12884901888 | bytes 18874368 | tf_op jit(solution)/shard_map/attend_back/pallas_call | solution.py:361
  127.4 6.7 %unit_send.3 = bf16[2,768,768]{2,1,0:T(8,128)(2,1)} custom-call(s32[3]{0:T(128)} %pad_add_fusion.sc, bf16[1024,3072]{1,0:T(8,128)(2,1)} %copy-done.3, bf16[1024,3072]{1,0:T(8,128)(2,1)} %copy-done.2), custom_call_target="tpu_custom_call" | custom-call | flops 2415919104 | bytes 6291456 | tf_op jit(solution)/shard_map/unit_send/pallas_call | solution.py:433
  134.5 7.6 %unit_keep.5 = bf16[2,768,768]{2,1,0:T(8,128)(2,1)} custom-call(s32[3]{0:T(128)} %pad_add_fusion.sc, bf16[1024,3072]{1,0:T(8,128)(2,1)} %get-tuple-element.63.a, bf16[1024,768]{1,0:T(8,128)(2,1)} %get-tuple-element.44.dffn.b, bf16[2,768,768]{2,1,0:T(8,128)(2,1)} %collective-permute-done.34.got), custom_call_target="tpu_custom_call" | custom-call | flops 2415919104 | bytes 6291456 | tf_op jit(solution)/shard_map/unit_keep/pallas_call | solution.py:433
  147.7 7.6 %unit_keep.4 = bf16[2,768,768]{2,1,0:T(8,128)(2,1)} custom-call(s32[3]{0:T(128)} %pad_add_fusion.sc, bf16[1024,768]{1,0:T(8,128)(2,1)} %get-tuple-element.61.a, bf16[1024,3072]{1,0:T(8,128)(2,1)} %get-tuple-element.62.b, bf16[2,768,768]{2,1,0:T(8,128)(2,1)} %collective-permute-done.18.got), custom_call_target="tpu_custom_call" | custom-call | flops 2415919104 | bytes 6291456 | tf_op jit(solution)/shard_map/unit_keep/pallas_call | solution.py:433
  164.8 8.3 %collective-permute-done.19 = bf16[384,768]{1,0:T(8,128)(2,1)S(1)} collective-permute-done((bf16[384,768]{1,0:T(8,128)(2,1)S(1)}, bf16[384,768]{1,0:T(8,128)(2,1)S(1)}, u32[]{:S(2)}, u32[]{:S(2)}) %collective-permute-start.19) | collective-permute-done | bytes 589856 | tf_op jit(solution)/shard_map/ppermute | solution.py:532
  178.9 7.8 %unit_keep.3 = bf16[2,768,768]{2,1,0:T(8,128)(2,1)} custom-call(s32[3]{0:T(128)} %pad_add_fusion.sc, bf16[1024,3072]{1,0:T(8,128)(2,1)} %copy-done.3, bf16[1024,3072]{1,0:T(8,128)(2,1)} %copy-done.2, bf16[2,768,768]{2,1,0:T(8,128)(2,1)} %copy-done.11), custom_call_target="tpu_custom_call" | custom-call | flops 2415919104 | bytes 6291456 | tf_op jit(solution)/shard_map/unit_keep/pallas_call | solution.py:433
  195.1 3.9 %collective-permute-done.39 = bf16[96,768]{1,0:T(8,128)(2,1)S(1)} collective-permute-done((bf16[96,768]{1,0:T(8,128)(2,1)S(1)}, bf16[96,768]{1,0:T(8,128)(2,1)S(1)}, u32[]{:S(2)}, u32[]{:S(2)}) %collective-permute-start.39) | collective-permute-done | bytes 147488 | tf_op jit(solution)/shard_map/ppermute | solution.py:532
  199.0 7.1 %collective-permute-done.40 = bf16[96,768]{1,0:T(8,128)(2,1)S(1)} collective-permute-done((bf16[96,768]{1,0:T(8,128)(2,1)S(1)}, bf16[96,768]{1,0:T(8,128)(2,1)S(1)}, u32[]{:S(2)}, u32[]{:S(2)}) %collective-permute-start.40) | collective-permute-done | bytes 147488 | tf_op jit(solution)/shard_map/ppermute | solution.py:532
  208.7 3.8 collective-permute-start.44
  212.6 8.9 %collective-permute-done.24 = bf16[96,768]{1,0:T(8,128)(2,1)S(1)} collective-permute-done((bf16[96,768]{1,0:T(8,128)(2,1)S(1)}, bf16[96,768]{1,0:T(8,128)(2,1)S(1)}, u32[]{:S(2)}, u32[]{:S(2)}) %collective-permute-start.24) | collective-permute-done | bytes 147488 | tf_op jit(solution)/shard_map/ppermute | solution.py:532
  235.1 7.4 %collective-permute-start.28 = (bf16[96,768]{1,0:T(8,128)(2,1)S(1)}, bf16[96,768]{1,0:T(8,128)(2,1)S(1)}, u32[]{:S(2)}, u32[]{:S(2)}) collective-permute-start(bf16[96,768]{1,0:T(8,128)(2,1)S(1)} %add_convert_fusion.1), channel_id=1, source_target_pairs={{0,24},{4,28},{8,16},{12,20},{16,8},{20,12},{24,0},{28,4},{1,25},{... | collective-permute-start | bytes 442376 | tf_op jit(solution)/shard_map/ppermute | solution.py:532
  242.6 3.9 collective-permute-done.28
  246.5 5.1 %collective-permute-done.42 = bf16[96,768]{1,0:T(8,128)(2,1)S(1)} collective-permute-done((bf16[96,768]{1,0:T(8,128)(2,1)S(1)}, bf16[96,768]{1,0:T(8,128)(2,1)S(1)}, u32[]{:S(2)}, u32[]{:S(2)}) %collective-permute-start.42) | collective-permute-done | bytes 147488 | tf_op jit(solution)/shard_map/ppermute | solution.py:532
  263.3 11.0 %collective-permute-done.4 = bf16[192,768]{1,0:T(8,128)(2,1)S(1)} collective-permute-done((bf16[192,768]{1,0:T(8,128)(2,1)S(1)}, bf16[192,768]{1,0:T(8,128)(2,1)S(1)}, u32[]{:S(2)}, u32[]{:S(2)}) %collective-permute-start.4) | collective-permute-done | bytes 294944 | tf_op jit(solution)/shard_map/ppermute | solution.py:532
  282.4 4.4 %collective-permute-done.8 = bf16[96,768]{1,0:T(8,128)(2,1)S(1)} collective-permute-done((bf16[96,768]{1,0:T(8,128)(2,1)S(1)}, bf16[96,768]{1,0:T(8,128)(2,1)S(1)}, u32[]{:S(2)}, u32[]{:S(2)}) %collective-permute-start.8) | collective-permute-done | bytes 147488 | tf_op jit(solution)/shard_map/ppermute | solution.py:532
  296.7 4.7 %collective-permute-done.11 = bf16[96,768]{1,0:T(8,128)(2,1)S(1)} collective-permute-done((bf16[96,768]{1,0:T(8,128)(2,1)S(1)}, bf16[96,768]{1,0:T(8,128)(2,1)S(1)}, u32[]{:S(2)}, u32[]{:S(2)}) %collective-permute-start.11) | collective-permute-done | bytes 147488 | tf_op jit(solution)/shard_map/ppermute | solution.py:532
  303.8 4.5 %collective-permute-done.12 = bf16[96,768]{1,0:T(8,128)(2,1)S(1)} collective-permute-done((bf16[96,768]{1,0:T(8,128)(2,1)S(1)}, bf16[96,768]{1,0:T(8,128)(2,1)S(1)}, u32[]{:S(2)}, u32[]{:S(2)}) %collective-permute-start.12) | collective-permute-done | bytes 147488 | tf_op jit(solution)/shard_map/ppermute | solution.py:532
  310.2 4.9 %collective-permute-done.15 = bf16[192,768]{1,0:T(8,128)(2,1)S(1)} collective-permute-done((bf16[192,768]{1,0:T(8,128)(2,1)S(1)}, bf16[192,768]{1,0:T(8,128)(2,1)S(1)}, u32[]{:S(2)}, u32[]{:S(2)}) %collective-permute-start.15) | collective-permute-done | bytes 294944 | tf_op jit(solution)/shard_map/ppermute | solution.py:532
  320.6 4.5 %collective-permute-done.16 = bf16[384,768]{1,0:T(8,128)(2,1)S(1)} collective-permute-done((bf16[384,768]{1,0:T(8,128)(2,1)S(1)}, bf16[384,768]{1,0:T(8,128)(2,1)S(1)}, u32[]{:S(2)}, u32[]{:S(2)}) %collective-permute-start.16) | collective-permute-done | bytes 589856 | tf_op jit(solution)/shard_map/ppermute | solution.py:532
  327.0 4.0 %collective-permute-done.50 = f32[4,768]{1,0:T(4,128)S(1)} collective-permute-done((f32[4,768]{1,0:T(4,128)S(1)}, f32[4,768]{1,0:T(4,128)S(1)}, u32[]{:S(2)}, u32[]{:S(2)}) %collective-permute-start.50) | collective-permute-done | bytes 12320 | tf_op jit(solution)/shard_map/ppermute | solution.py:532
  347.3 8.9 %token_grad.1 = f32[1024,768]{1,0:T(8,128)} custom-call(f32[1024,768]{1,0:T(8,128)} %get-tuple-element.51.dres_one, bf16[1024,768]{1,0:T(8,128)(2,1)} %get-tuple-element.57.dq, bf16[1024,768]{1,0:T(8,128)(2,1)} %get-tuple-element.58.dk, bf16[1024,768]{1,0:T(8,128)(2,1)} %get-tuple-element.59.dv, bf16[768,768]{1,0:T(8,128)(2,1)} %wq.3, bf16[768,768]{1,0:T(8,128)(2,1)} %wk.3, ...), custom_call_target="tpu_custom_call" | custom-call | flops 3623878656 | bytes 11010048 | tf_op jit(solution)/shard_map/token_grad/pallas_call | solution.py:387
  356.2 7.6 %gather_units.3 = f32[3072,768]{1,0:T(8,128)} custom-call(s32[3]{0:T(128)} %pad_add_fusion.sc, bf16[2,768,768]{2,1,0:T(8,128)(2,1)} %pad_maximum_fusion.2.mine, bf16[2,768,768]{2,1,0:T(8,128)(2,1)} %collective-permute-done.49.other), custom_call_target="tpu_custom_call" | custom-call | tf_op jit(solution)/shard_map/gather_units/pallas_call | solution.py:504
  363.8 7.6 %gather_units.2 = f32[768,3072]{1,0:T(8,128)} custom-call(s32[3]{0:T(128)} %pad_add_fusion.sc, bf16[2,768,768]{2,1,0:T(8,128)(2,1)} %copy-done.8, bf16[2,768,768]{2,1,0:T(8,128)(2,1)} %collective-permute-done.33.other), custom_call_target="tpu_custom_call" | custom-call | tf_op jit(solution)/shard_map/gather_units/pallas_call | solution.py:504
  372.8 3.9 pick_unit.7
  376.6 3.8 pick_unit.6
  380.4 3.8 pick_unit.5
  384.3 3.9 pick_unit.4
  (213 shorter events, 120.8 us)
Async XLA Ops:
  57.8 76.7 %collective-permute-start.34 = (bf16[2,768,768]{2,1,0:T(8,128)(2,1)}, bf16[2,768,768]{2,1,0:T(8,128)(2,1)}, u32[]{:S(2)}, u32[]{:S(2)}) collective-permute-start(bf16[2,768,768]{2,1,0:T(8,128)(2,1)} %unit_send.5), channel_id=1, source_target_pairs={{0,1},{1,0},{2,3},{3,2},{4,5},{5,4},{6,7},{7,6},{8,9},{9,8},{10,11... | collective-permute-start | bytes 7077896 | tf_op jit(solution)/shard_map/ppermute | solution.py:532
  85.0 11.8 %collective-permute-start.1 = (f32[6,256,128]{2,1,0:T(8,128)}, f32[6,256,128]{2,1,0:T(8,128)S(1)}, u32[]{:S(2)}, u32[]{:S(2)}) collective-permute-start(f32[6,256,128]{2,1,0:T(8,128)} %get-tuple-element.56), channel_id=1, source_target_pairs={{0,1},{1,0},{2,3},{3,2},{4,5},{5,4},{6,7},{7,6},{8,9},{9,8},{10,11... | collective-permute-start | bytes 2359304 | tf_op jit(solution)/shard_map/ppermute | solution.py:532
  91.8 55.9 %collective-permute-start.18 = (bf16[2,768,768]{2,1,0:T(8,128)(2,1)}, bf16[2,768,768]{2,1,0:T(8,128)(2,1)}, u32[]{:S(2)}, u32[]{:S(2)}) collective-permute-start(bf16[2,768,768]{2,1,0:T(8,128)(2,1)} %unit_send.4), channel_id=1, source_target_pairs={{0,1},{1,0},{2,3},{3,2},{4,5},{5,4},{6,7},{7,6},{8,9},{9,8},{10,11... | collective-permute-start | bytes 7077896 | tf_op jit(solution)/shard_map/ppermute | solution.py:532
  134.1 43.3 %collective-permute-start.2 = (bf16[2,768,768]{2,1,0:T(8,128)(2,1)}, bf16[2,768,768]{2,1,0:T(8,128)(2,1)S(1)}, u32[]{:S(2)}, u32[]{:S(2)}) collective-permute-start(bf16[2,768,768]{2,1,0:T(8,128)(2,1)} %unit_send.3), channel_id=1, source_target_pairs={{0,1},{1,0},{2,3},{3,2},{4,5},{5,4},{6,7},{7,6},{8,9},{9,8},{10,11... | collective-permute-start | bytes 7077896 | tf_op jit(solution)/shard_map/ppermute | solution.py:532
  143.4 16.9 %collective-permute-start.35 = (bf16[384,768]{1,0:T(8,128)(2,1)S(1)}, bf16[384,768]{1,0:T(8,128)(2,1)S(1)}, u32[]{:S(2)}, u32[]{:S(2)}) collective-permute-start(bf16[384,768]{1,0:T(8,128)(2,1)S(1)} %get-tuple-element.68), channel_id=1, source_target_pairs={{0,2},{1,3},{2,0},{3,1},{4,6},{5,7},{6,4},{7,5},{8,10},{9,11},{10,... | collective-permute-start | bytes 1769480 | tf_op jit(solution)/shard_map/ppermute | solution.py:532
  146.2 16.2 %collective-permute-start.37 = (bf16[384,768]{1,0:T(8,128)(2,1)S(1)}, bf16[384,768]{1,0:T(8,128)(2,1)S(1)}, u32[]{:S(2)}, u32[]{:S(2)}) collective-permute-start(bf16[384,768]{1,0:T(8,128)(2,1)S(1)} %get-tuple-element.69), channel_id=1, source_target_pairs={{0,4},{4,0},{8,12},{12,8},{16,20},{20,16},{24,28},{28,24},{1,5},{5... | collective-permute-start | bytes 1769480 | tf_op jit(solution)/shard_map/ppermute | solution.py:532
  156.8 16.3 %collective-permute-start.19 = (bf16[384,768]{1,0:T(8,128)(2,1)S(1)}, bf16[384,768]{1,0:T(8,128)(2,1)S(1)}, u32[]{:S(2)}, u32[]{:S(2)}) collective-permute-start(bf16[384,768]{1,0:T(8,128)(2,1)S(1)} %get-tuple-element.72), channel_id=1, source_target_pairs={{0,2},{1,3},{2,0},{3,1},{4,6},{5,7},{6,4},{7,5},{8,10},{9,11},{10,... | collective-permute-start | bytes 1769480 | tf_op jit(solution)/shard_map/ppermute | solution.py:532
  157.4 17.6 %collective-permute-start.21 = (bf16[384,768]{1,0:T(8,128)(2,1)S(1)}, bf16[384,768]{1,0:T(8,128)(2,1)S(1)}, u32[]{:S(2)}, u32[]{:S(2)}) collective-permute-start(bf16[384,768]{1,0:T(8,128)(2,1)S(1)} %get-tuple-element.73), channel_id=1, source_target_pairs={{0,4},{4,0},{8,12},{12,8},{16,20},{20,16},{24,28},{28,24},{1,5},{5... | collective-permute-start | bytes 1769480 | tf_op jit(solution)/shard_map/ppermute | solution.py:532
  162.7 26.9 %collective-permute-start.38 = (bf16[192,768]{1,0:T(8,128)(2,1)S(1)}, bf16[192,768]{1,0:T(8,128)(2,1)S(1)}, u32[]{:S(2)}, u32[]{:S(2)}) collective-permute-start(bf16[192,768]{1,0:T(8,128)(2,1)S(1)} %slice.492), channel_id=1, source_target_pairs={{0,2},{1,3},{2,0},{3,1},{4,6},{5,7},{6,4},{7,5},{8,10},{9,11},{10,... | collective-permute-start | bytes 884744 | tf_op jit(solution)/shard_map/ppermute | solution.py:532
  162.8 27.4 %collective-permute-start.36 = (bf16[192,768]{1,0:T(8,128)(2,1)S(1)}, bf16[192,768]{1,0:T(8,128)(2,1)S(1)}, u32[]{:S(2)}, u32[]{:S(2)}) collective-permute-start(bf16[192,768]{1,0:T(8,128)(2,1)S(1)} %slice.487), channel_id=1, source_target_pairs={{0,4},{4,0},{8,12},{12,8},{16,20},{20,16},{24,28},{28,24},{1,5},{5... | collective-permute-start | bytes 884744 | tf_op jit(solution)/shard_map/ppermute | solution.py:532
  175.3 16.6 %collective-permute-start.22 = (bf16[192,768]{1,0:T(8,128)(2,1)S(1)}, bf16[192,768]{1,0:T(8,128)(2,1)S(1)}, u32[]{:S(2)}, u32[]{:S(2)}) collective-permute-start(bf16[192,768]{1,0:T(8,128)(2,1)S(1)} %slice.462), channel_id=1, source_target_pairs={{0,2},{1,3},{2,0},{3,1},{4,6},{5,7},{6,4},{7,5},{8,10},{9,11},{10,... | collective-permute-start | bytes 884744 | tf_op jit(solution)/shard_map/ppermute | solution.py:532
  175.6 19.1 %collective-permute-start.20 = (bf16[192,768]{1,0:T(8,128)(2,1)S(1)}, bf16[192,768]{1,0:T(8,128)(2,1)S(1)}, u32[]{:S(2)}, u32[]{:S(2)}) collective-permute-start(bf16[192,768]{1,0:T(8,128)(2,1)S(1)} %slice.457), channel_id=1, source_target_pairs={{0,4},{4,0},{8,12},{12,8},{16,20},{20,16},{24,28},{28,24},{1,5},{5... | collective-permute-start | bytes 884744 | tf_op jit(solution)/shard_map/ppermute | solution.py:532
  188.0 66.5 %collective-permute-start.3 = (bf16[384,768]{1,0:T(8,128)(2,1)S(1)}, bf16[384,768]{1,0:T(8,128)(2,1)S(1)}, u32[]{:S(2)}, u32[]{:S(2)}) collective-permute-start(bf16[384,768]{1,0:T(8,128)(2,1)S(1)} %get-tuple-element.76), channel_id=1, source_target_pairs={{0,2},{1,3},{2,0},{3,1},{4,6},{5,7},{6,4},{7,5},{8,10},{9,11},{10,... | collective-permute-start | bytes 1769480 | tf_op jit(solution)/shard_map/ppermute | solution.py:532
  189.6 65.0 %collective-permute-start.5 = (bf16[384,768]{1,0:T(8,128)(2,1)S(1)}, bf16[384,768]{1,0:T(8,128)(2,1)S(1)}, u32[]{:S(2)}, u32[]{:S(2)}) collective-permute-start(bf16[384,768]{1,0:T(8,128)(2,1)S(1)} %get-tuple-element.77), channel_id=1, source_target_pairs={{0,4},{4,0},{8,12},{12,8},{16,20},{20,16},{24,28},{28,24},{1,5},{5... | collective-permute-start | bytes 1769480 | tf_op jit(solution)/shard_map/ppermute | solution.py:532
  192.0 14.2 %collective-permute-start.40 = (bf16[96,768]{1,0:T(8,128)(2,1)S(1)}, bf16[96,768]{1,0:T(8,128)(2,1)S(1)}, u32[]{:S(2)}, u32[]{:S(2)}) collective-permute-start(bf16[96,768]{1,0:T(8,128)(2,1)S(1)} %pad_maximum_fusion.16), channel_id=1, source_target_pairs={{0,16},{4,20},{8,24},{12,28},{16,0},{20,4},{24,8},{28,12},{1,17},{... | collective-permute-start | bytes 442376 | tf_op jit(solution)/shard_map/ppermute | solution.py:532
  194.7 11.4 %collective-permute-start.41 = (bf16[96,768]{1,0:T(8,128)(2,1)S(1)}, bf16[96,768]{1,0:T(8,128)(2,1)S(1)}, u32[]{:S(2)}, u32[]{:S(2)}) collective-permute-start(bf16[96,768]{1,0:T(8,128)(2,1)S(1)} %pad_maximum_fusion.17), channel_id=1, source_target_pairs={{0,24},{4,28},{8,16},{12,20},{16,8},{20,12},{24,0},{28,4},{1,25},{... | collective-permute-start | bytes 442376 | tf_op jit(solution)/shard_map/ppermute | solution.py:532
  206.1 15.3 %collective-permute-start.24 = (bf16[96,768]{1,0:T(8,128)(2,1)S(1)}, bf16[96,768]{1,0:T(8,128)(2,1)S(1)}, u32[]{:S(2)}, u32[]{:S(2)}) collective-permute-start(bf16[96,768]{1,0:T(8,128)(2,1)S(1)} %pad_maximum_fusion.13), channel_id=1, source_target_pairs={{0,16},{4,20},{8,24},{12,28},{16,0},{20,4},{24,8},{28,12},{1,17},{... | collective-permute-start | bytes 442376 | tf_op jit(solution)/shard_map/ppermute | solution.py:532
  206.1 15.3 %collective-permute-start.25 = (bf16[96,768]{1,0:T(8,128)(2,1)S(1)}, bf16[96,768]{1,0:T(8,128)(2,1)S(1)}, u32[]{:S(2)}, u32[]{:S(2)}) collective-permute-start(bf16[96,768]{1,0:T(8,128)(2,1)S(1)} %pad_maximum_fusion.14), channel_id=1, source_target_pairs={{0,24},{4,28},{8,16},{12,20},{16,8},{20,12},{24,0},{28,4},{1,25},{... | collective-permute-start | bytes 442376 | tf_op jit(solution)/shard_map/ppermute | solution.py:532
  208.7 45.2 %collective-permute-start.44 = (bf16[96,768]{1,0:T(8,128)(2,1)S(1)}, bf16[96,768]{1,0:T(8,128)(2,1)S(1)}, u32[]{:S(2)}, u32[]{:S(2)}) collective-permute-start(bf16[96,768]{1,0:T(8,128)(2,1)S(1)} %add_convert_fusion), channel_id=1, source_target_pairs={{0,24},{4,28},{8,16},{12,20},{16,8},{20,12},{24,0},{28,4},{1,25},{... | collective-permute-start | bytes 442376 | tf_op jit(solution)/shard_map/ppermute | solution.py:532
  221.4 31.8 %collective-permute-start.43 = (bf16[96,768]{1,0:T(8,128)(2,1)S(1)}, bf16[96,768]{1,0:T(8,128)(2,1)S(1)}, u32[]{:S(2)}, u32[]{:S(2)}) collective-permute-start(bf16[96,768]{1,0:T(8,128)(2,1)S(1)} %add_convert_fusion), channel_id=1, source_target_pairs={{0,16},{4,20},{8,24},{12,28},{16,0},{20,4},{24,8},{28,12},{1,17},{... | collective-permute-start | bytes 442376 | tf_op jit(solution)/shard_map/ppermute | solution.py:532
  235.1 11.3 %collective-permute-start.28 = (bf16[96,768]{1,0:T(8,128)(2,1)S(1)}, bf16[96,768]{1,0:T(8,128)(2,1)S(1)}, u32[]{:S(2)}, u32[]{:S(2)}) collective-permute-start(bf16[96,768]{1,0:T(8,128)(2,1)S(1)} %add_convert_fusion.1), channel_id=1, source_target_pairs={{0,24},{4,28},{8,16},{12,20},{16,8},{20,12},{24,0},{28,4},{1,25},{... | collective-permute-start | bytes 442376 | tf_op jit(solution)/shard_map/ppermute | solution.py:532
  254.0 24.0 %collective-permute-start.45 = (bf16[192,768]{1,0:T(8,128)(2,1)S(1)}, bf16[192,768]{1,0:T(8,128)(2,1)S(1)}, u32[]{:S(2)}, u32[]{:S(2)}) collective-permute-start(bf16[192,768]{1,0:T(8,128)(2,1)S(1)} %pad_maximum_fusion.7), channel_id=1, source_target_pairs={{0,4},{4,0},{8,12},{12,8},{16,20},{20,16},{24,28},{28,24},{1,5},{5... | collective-permute-start | bytes 884744 | tf_op jit(solution)/shard_map/ppermute | solution.py:532
  256.4 22.5 %collective-permute-start.47 = (bf16[192,768]{1,0:T(8,128)(2,1)S(1)}, bf16[192,768]{1,0:T(8,128)(2,1)S(1)}, u32[]{:S(2)}, u32[]{:S(2)}) collective-permute-start(bf16[192,768]{1,0:T(8,128)(2,1)S(1)} %pad_maximum_fusion.8), channel_id=1, source_target_pairs={{0,2},{1,3},{2,0},{3,1},{4,6},{5,7},{6,4},{7,5},{8,10},{9,11},{10,... | collective-permute-start | bytes 884744 | tf_op jit(solution)/shard_map/ppermute | solution.py:532
  260.0 14.2 %collective-permute-start.4 = (bf16[192,768]{1,0:T(8,128)(2,1)S(1)}, bf16[192,768]{1,0:T(8,128)(2,1)S(1)}, u32[]{:S(2)}, u32[]{:S(2)}) collective-permute-start(bf16[192,768]{1,0:T(8,128)(2,1)S(1)} %slice.427), channel_id=1, source_target_pairs={{0,4},{4,0},{8,12},{12,8},{16,20},{20,16},{24,28},{28,24},{1,5},{5... | collective-permute-start | bytes 884744 | tf_op jit(solution)/shard_map/ppermute | solution.py:532
  261.6 47.6 %collective-permute-start.32 = (bf16[384,768]{1,0:T(8,128)(2,1)S(1)}, bf16[384,768]{1,0:T(8,128)(2,1)S(1)}, u32[]{:S(2)}, u32[]{:S(2)}) collective-permute-start(bf16[384,768]{1,0:T(8,128)(2,1)S(1)} %get-tuple-element.108), channel_id=1, source_target_pairs={{0,4},{4,0},{8,12},{12,8},{16,20},{20,16},{24,28},{28,24},{1,5},{5... | collective-permute-start | bytes 1769480 | tf_op jit(solution)/shard_map/ppermute | solution.py:532
  274.4 12.4 %collective-permute-start.8 = (bf16[96,768]{1,0:T(8,128)(2,1)S(1)}, bf16[96,768]{1,0:T(8,128)(2,1)S(1)}, u32[]{:S(2)}, u32[]{:S(2)}) collective-permute-start(bf16[96,768]{1,0:T(8,128)(2,1)S(1)} %pad_maximum_fusion.10), channel_id=1, source_target_pairs={{0,16},{4,20},{8,24},{12,28},{16,0},{20,4},{24,8},{28,12},{1,17},{... | collective-permute-start | bytes 442376 | tf_op jit(solution)/shard_map/ppermute | solution.py:532
  279.0 31.2 %collective-permute-start.30 = (bf16[384,768]{1,0:T(8,128)(2,1)S(1)}, bf16[384,768]{1,0:T(8,128)(2,1)S(1)}, u32[]{:S(2)}, u32[]{:S(2)}) collective-permute-start(bf16[384,768]{1,0:T(8,128)(2,1)S(1)} %get-tuple-element.106), channel_id=1, source_target_pairs={{0,2},{1,3},{2,0},{3,1},{4,6},{5,7},{6,4},{7,5},{8,10},{9,11},{10,... | collective-permute-start | bytes 1769480 | tf_op jit(solution)/shard_map/ppermute | solution.py:532
  280.3 37.4 %collective-permute-start.48 = (bf16[384,768]{1,0:T(8,128)(2,1)S(1)}, bf16[384,768]{1,0:T(8,128)(2,1)S(1)}, u32[]{:S(2)}, u32[]{:S(2)}) collective-permute-start(bf16[384,768]{1,0:T(8,128)(2,1)S(1)} %get-tuple-element.104), channel_id=1, source_target_pairs={{0,4},{4,0},{8,12},{12,8},{16,20},{20,16},{24,28},{28,24},{1,5},{5... | collective-permute-start | bytes 1769480 | tf_op jit(solution)/shard_map/ppermute | solution.py:532
  286.8 31.0 %collective-permute-start.46 = (bf16[384,768]{1,0:T(8,128)(2,1)S(1)}, bf16[384,768]{1,0:T(8,128)(2,1)S(1)}, u32[]{:S(2)}, u32[]{:S(2)}) collective-permute-start(bf16[384,768]{1,0:T(8,128)(2,1)S(1)} %get-tuple-element.102), channel_id=1, source_target_pairs={{0,2},{1,3},{2,0},{3,1},{4,6},{5,7},{6,4},{7,5},{8,10},{9,11},{10,... | collective-permute-start | bytes 1769480 | tf_op jit(solution)/shard_map/ppermute | solution.py:532
  317.6 46.2 %collective-permute-start.33 = (bf16[2,768,768]{2,1,0:T(8,128)(2,1)S(1)}, bf16[2,768,768]{2,1,0:T(8,128)(2,1)}, u32[]{:S(2)}, u32[]{:S(2)}) collective-permute-start(bf16[2,768,768]{2,1,0:T(8,128)(2,1)S(1)} %pad_maximum_fusion.1.mine), channel_id=1, source_target_pairs={{0,1},{1,0},{2,3},{3,2},{4,5},{5,4},{6,7},{7,6},{8,9},{9,8},{10,11... | collective-permute-start | bytes 7077896 | tf_op jit(solution)/shard_map/ppermute | solution.py:532
  320.6 35.6 %collective-permute-start.49 = (bf16[2,768,768]{2,1,0:T(8,128)(2,1)}, bf16[2,768,768]{2,1,0:T(8,128)(2,1)}, u32[]{:S(2)}, u32[]{:S(2)}) collective-permute-start(bf16[2,768,768]{2,1,0:T(8,128)(2,1)} %pad_maximum_fusion.2.mine), channel_id=1, source_target_pairs={{0,1},{1,0},{2,3},{3,2},{4,5},{5,4},{6,7},{7,6},{8,9},{9,8},{10,11... | collective-permute-start | bytes 7077896 | tf_op jit(solution)/shard_map/ppermute | solution.py:532
  326.3 45.0 %collective-permute-start.17 = (bf16[2,768,768]{2,1,0:T(8,128)(2,1)S(1)}, bf16[2,768,768]{2,1,0:T(8,128)(2,1)S(1)}, u32[]{:S(2)}, u32[]{:S(2)}) collective-permute-start(bf16[2,768,768]{2,1,0:T(8,128)(2,1)S(1)} %pad_maximum_fusion.mine), channel_id=1, source_target_pairs={{0,1},{1,0},{2,3},{3,2},{4,5},{5,4},{6,7},{7,6},{8,9},{9,8},{10,11... | collective-permute-start | bytes 7077896 | tf_op jit(solution)/shard_map/ppermute | solution.py:532
  (41 other events, 232.8 us)

commit v2 on v1

v2 whole, which is shorter than its diff:
```python
import functools
import math

import jax
import jax.numpy as jnp
import numpy as np
from jax import lax
from jax.experimental import pallas as pl
from jax.experimental.pallas import tpu as pltpu
from jax.sharding import PartitionSpec as P

D = 768
E = 64
FF = 3072
LENGTH = 2048
CHUNK = 256
PAIR = 2 * E
PAIRS = D // PAIR
FEAT = 2 * PAIR
EPSILON = 1e-05
STEP_ANGLE = 0.5 * math.pi / LENGTH
HALF = D // 2
QUARTER = D // 4
LIMIT = 63 * 2**20
PACE = 1.0
WEIGHTS = dict(
    project=11, rows=60, attend_back=19, token_grad=10, gather_units=8, gather_qkv=5.5, gather_rest=4, add_cut=2.5, add_all=2, join=2
)

f32 = jnp.float32
bf16 = jnp.bfloat16


def nn(a, b):
    return jnp.dot(a, b, preferred_element_type=f32)


def tn(a, b):
    return lax.dot_general(a, b, (((0,), (0,)), ((), ())), preferred_element_type=f32)


def nt(a, b):
    return lax.dot_general(a, b, (((1,), (1,)), ((), ())), preferred_element_type=f32)


def ordered_call(
    kernel, name, grid, in_specs, out_specs, out_shape, scratch_shapes=(), scalars=0, deps=(),
):
    deps = list(deps)

    def body(*refs):
        first = scalars + len(in_specs)
        kernel(*refs[:first], *refs[first + len(deps) :])

    call = pl.pallas_call(
        body,
        grid_spec=pltpu.PrefetchScalarGridSpec(
            num_scalar_prefetch=scalars,
            grid=grid,
            in_specs=list(in_specs) + [pl.BlockSpec(memory_space=pl.ANY)] * len(deps),
            out_specs=out_specs,
            scratch_shapes=list(scratch_shapes),
        ),
        out_shape=out_shape,
        compiler_params=pltpu.CompilerParams(vmem_limit_bytes=LIMIT),
        cost_estimate=pl.CostEstimate(
            flops=int(PACE * WEIGHTS[name] * 1.15e9) + 1, bytes_accessed=1, transcendentals=0
        ),
        name=name,
    )
    return lambda *args: call(*args, *deps)


def whole(*shape):
    return pl.BlockSpec(shape, lambda *_: (0,) * len(shape))


def by_chunk(width, last=None):
    if last is None:
        return pl.BlockSpec((CHUNK, width), lambda i, *_: (i, 0))
    return pl.BlockSpec((CHUNK, width), lambda i, *_: (last - i, 0))


ANY = pl.BlockSpec(memory_space=pl.ANY)


def softplus(x):
    return jnp.maximum(x, 0.0) + jnp.log1p(jnp.exp(-jnp.abs(x)))


def lane_head(rows):
    return (lax.broadcasted_iota(jnp.int32, (rows, PAIR), 1) >= E).astype(jnp.int32)


def row_head():
    return (lax.broadcasted_iota(jnp.int32, (FEAT, PAIR), 0) % PAIR >= E).astype(jnp.int32)


def unpack_state(packed):
    same = row_head() == lane_head(FEAT)
    left = jnp.where(same, packed, 0.0)
    right = jnp.where(same, pltpu.roll(packed, E, 1), 0.0)
    return jnp.concatenate([left, right], axis=1).astype(bf16)


def features(x, cosine, sine):
    return jnp.concatenate([x * cosine, x * sine], axis=1).astype(bf16)


def with_ones(v):
    return jnp.concatenate([v, jnp.ones_like(v)], axis=1)


def turn_state(state, angle, on):
    cosine, sine = math.cos(angle) * on, math.sin(angle) * on
    first, second = state[:PAIR], state[PAIR:]
    return jnp.concatenate([cosine * first + sine * second, cosine * second - sine * first], axis=0)


def project_kernel(tok, wq, wk, wv, cos, sin, q_ref, k_ref, v_ref, pre_ref, tot_ref):
    @pl.when(pl.program_id(0) == 0)
    def _():
        tot_ref[...] = jnp.zeros_like(tot_ref)

    x = tok[...]
    q_ref[...] = softplus(nn(x, wq[...])).astype(bf16)
    k = softplus(nn(x, wk[...])).astype(bf16)
    k_ref[...] = k
    v = nn(x, wv[...]).astype(bf16)
    v_ref[...] = v
    same = row_head() == lane_head(FEAT)
    for p in range(PAIRS):
        cols = slice(p * PAIR, (p + 1) * PAIR)
        k_feat = features(k[:, cols].astype(f32), cos[...], sin[...])
        both = tn(k_feat, with_ones(v[:, cols]))
        pre_ref[0, p] = tot_ref[p]
        tot_ref[p] += jnp.where(same, both[:, :PAIR], both[:, PAIR:])


def project(tokens, wq, wk, wv, cos, sin):
    rows = tokens.shape[0]
    steps = rows // CHUNK
    act = jax.ShapeDtypeStruct((rows, D), bf16)
    return ordered_call(
        project_kernel,
        "project",
        grid=(steps,),
        in_specs=[by_chunk(D), whole(D, D), whole(D, D), whole(D, D), by_chunk(PAIR), by_chunk(PAIR)],
        out_specs=[
            by_chunk(D), by_chunk(D), by_chunk(D),
            pl.BlockSpec((1, PAIRS, FEAT, PAIR), lambda i: (i, 0, 0, 0)), whole(PAIRS, FEAT, PAIR),
        ],
        out_shape=[
            act, act, act,
            jax.ShapeDtypeStruct((steps, PAIRS, FEAT, PAIR), f32), jax.ShapeDtypeStruct((PAIRS, FEAT, PAIR), f32),
        ],
    )(tokens, wq, wk, wv, cos, sin)


def norm_parts(z):
    centred = z - jnp.mean(z, axis=-1, keepdims=True)
    rstd = lax.rsqrt(jnp.mean(centred * centred, axis=-1, keepdims=True) + EPSILON)
    return centred * rstd, rstd


def norm_back(t, n, rstd):
    return (t - jnp.mean(t, axis=-1, keepdims=True) - n * jnp.mean(t * n, axis=-1, keepdims=True)) * rstd


def rows_kernel(
    angle, block, sc, tok, q_ref, k_ref, v_ref, pre, init, cos, sin, table, w_out, w_up, w_down, gains, biases, cot,
    out_ref, dres_one_ref, dnum_ref, dden_ref, part_ref, tot_ref, one_own, one_other, two_own, two_first, two_second, two_rest,
    mixed, hid, slope, dhid, acc_down, acc_up, acc_out, ng, stage, norm_stage, sems, norm_sems,
):
    core = sc[0]
    step = pl.program_id(0)
    first = step == 0

    @pl.when(first)
    def _():
        ng[...] = jnp.zeros_like(ng)
        tot_ref[...] = jnp.zeros_like(tot_ref)

    later = core.astype(f32)
    second = lane_head(CHUNK) == 1
    second2 = jnp.concatenate([second, second], axis=1)
    inverse = []
    for p in range(PAIRS):
        cols = slice(p * PAIR, (p + 1) * PAIR)
        state = unpack_state(pre[0, p] + turn_state(init[p], angle, later))
        q, k, v = q_ref[:, cols], k_ref[:, cols], v_ref[:, cols]
        total = nn(features(q.astype(f32), cos[...], sin[...]), state)
        v_ones = with_ones(v)
        zero = jnp.zeros_like(q)
        score_0 = (nt(jnp.where(second, zero, q), k) * table[...]).astype(bf16)
        score_1 = (nt(jnp.where(second, q, zero), k) * table[...]).astype(bf16)
        total += jnp.where(second2, nn(score_1, v_ones), nn(score_0, v_ones))
        inv = 1.0 / total[:, PAIR:]
        inverse.append(inv)
        mixed[:, cols] = (total[:, :PAIR] * inv).astype(bf16)
    z = tok[...].astype(f32) + nn(mixed[...], w_out[...])
    n0, rstd0 = norm_parts(z)
    normed = n0 * gains[0:1] + biases[0:1]
    low = normed.astype(bf16)
    z = normed
    for j in range(FF // D):
        cols = slice(j * D, (j + 1) * D)
        h = nn(low, w_up[:, cols])
        phi = 0.5 * (1.0 + lax.erf(h * (0.5**0.5)))
        hid[:, cols] = (h * phi).astype(bf16)
        slope[:, cols] = phi + h * jnp.exp(-0.5 * h * h) * ((2 * math.pi) ** -0.5)
    z = normed + nn(hid[...], w_down[...])
    n1, rstd1 = norm_parts(z)
    out_ref[...] = (n1 * gains[1:2] + biases[1:2]).astype(bf16)
    g = cot[...].astype(f32)
    ng[2:3] += jnp.sum(g * n1, axis=0, keepdims=True)
    ng[3:4] += jnp.sum(g, axis=0, keepdims=True)
    dres = norm_back(g * gains[1:2], n1, rstd1)
    dffn = dres.astype(bf16)
    for j in range(FF // D):
        cols = slice(j * D, (j + 1) * D)
        dhid[:, cols] = (nt(dffn, w_down[cols, :]) * slope[:, cols]).astype(bf16)
    g = dres + nt(dhid[...], w_up[...])
    ng[0:1] += jnp.sum(g * n0, axis=0, keepdims=True)
    ng[1:2] += jnp.sum(g, axis=0, keepdims=True)
    dres_one = norm_back(g * gains[0:1], n0, rstd0)
    dres_one_ref[...] = dres_one
    dbranch = dres_one.astype(bf16)
    dmixed = nt(dbranch, w_out[...]).astype(bf16).astype(f32)
    lane = lax.broadcasted_iota(jnp.int32, (CHUNK, PAIR), 1)
    same = row_head() == lane_head(FEAT)
    for p in range(PAIRS):
        cols = slice(p * PAIR, (p + 1) * PAIR)
        dnum = (dmixed[:, cols] * inverse[p]).astype(bf16)
        dnum_ref[:, cols] = dnum
        moment = dnum.astype(f32) * mixed[:, cols].astype(f32)
        first_sum = jnp.sum(jnp.where(second, 0.0, moment), axis=1, keepdims=True)
        second_sum = jnp.sum(jnp.where(second, moment, 0.0), axis=1, keepdims=True)
        dden = jnp.where(second, second_sum, first_sum) * (-2.0 / E)
        high = dden.astype(bf16)
        rest = (dden - high.astype(f32)).astype(bf16)
        dden = jnp.where(lane % E < E // 2, high, rest)
        dden_ref[:, cols] = dden
        both = tn(features(q_ref[:, cols].astype(f32), cos[...], sin[...]), jnp.concatenate([dnum, dden], axis=1))
        part = jnp.where(same, both[:, :PAIR], pltpu.roll(both[:, PAIR:], E, 1))
        part_ref[0, p] = part
        tot_ref[p] += part
    for j in range(FF // D):
        cols = slice(j * D, (j + 1) * D)
        acc_down[cols, :] = jnp.where(first, 0.0, acc_down[cols, :]) + tn(hid[:, cols], dffn)
        acc_up[:, cols] = jnp.where(first, 0.0, acc_up[:, cols]) + tn(low, dhid[:, cols])
    acc_out[...] = jnp.where(first, 0.0, acc_out[...]) + tn(mixed[...], dbranch)

    @pl.when(step == pl.num_programs(0) - 1)
    def _():
        slots = stage.shape[0]
        jobs = []
        for j in range(4):
            jobs.append((acc_down.at[j * D : (j + 1) * D, :], j // 2, one_own, one_other, j % 2 * D, j % 2 * D, D))
        for j in range(4):
            jobs.append((acc_up.at[:, j * D : (j + 1) * D], j // 2, two_own, two_second if j % 2 else two_first, j % 2 * D, 0, D))
        for j in range(2):
            jobs.append((acc_out.at[:, j * HALF : (j + 1) * HALF], j, two_own, two_rest, 2 * D, 0, HALF))

        def move(i, do):
            _, owner, own, other, own_at, other_at, size = jobs[i]
            slot = i % slots

            def one(to, start):
                do(pltpu.make_async_copy(stage.at[slot, :, pl.ds(0, size)], to.at[:, pl.ds(start, size)], sems.at[slot]))

            @pl.when(core == owner)
            def _():
                one(own, own_at)

            @pl.when(core != owner)
            def _():
                one(other, other_at)

        for i, (acc, owner, _, _, _, _, size) in enumerate(jobs):
            if i >= slots:
                move(i - slots, lambda copy: copy.wait())
            me = jnp.where(core == owner, sc[1], sc[2])
            for b in range(D // block):
                to = pl.multiple_of((jnp.int32(b) ^ me) * block, block)
                stage[i % slots, pl.ds(to, block), :size] = acc[b * block : (b + 1) * block, :].astype(bf16)
            move(i, lambda copy: copy.start())
        norm_stage[...] = jnp.zeros_like(norm_stage)
        copies = []
        for i, (me, to, start) in enumerate(((sc[1], two_own, 2 * D + HALF), (sc[2], two_rest, HALF))):
            base = pl.multiple_of(me * block, block)
            rows = [ng[r : r + 1, j * PAIR : (j + 1) * PAIR] for r in range(4) for j in range(PAIRS)]
            rows.append(jnp.zeros((block - len(rows), PAIR), f32))
            norm_stage[i, pl.ds(base, block), :] = jnp.concatenate(rows, axis=0).astype(bf16)
            copy = pltpu.make_async_copy(norm_stage.at[i], to.at[:, pl.ds(start, PAIR)], norm_sems.at[i])
            copy.start()
            copies.append(copy)
        for i in range(len(jobs) - slots, len(jobs)):
            move(i, lambda copy: copy.wait())
        for copy in copies:
            copy.wait()


def rows_call(sc, tokens, q, k, v, pre, init, cos, sin, table, w_out, w_up, w_down, gains, biases, cot, block):
    rows = tokens.shape[0]
    steps = rows // CHUNK

    def make(width, dtype=bf16, height=rows):
        return jax.ShapeDtypeStruct((height, width), dtype)

    def once(*shape):
        return pl.BlockSpec(shape, lambda *_: (0,) * len(shape), pipeline_mode=pl.Buffered(1))

    chunk, thin = by_chunk(D), by_chunk(PAIR)
    states = pl.BlockSpec((1, PAIRS, FEAT, PAIR), lambda i, sc: (i, 0, 0, 0))
    one, two = 2 * D, 2 * D + HALF + PAIR
    return ordered_call(
        functools.partial(rows_kernel, STEP_ANGLE * rows, block),
        "rows",
        scalars=1,
        grid=(steps,),
        in_specs=[
            chunk, chunk, chunk, chunk, states, once(PAIRS, FEAT, PAIR), thin, thin, once(CHUNK, CHUNK),
            once(D, D), once(D, FF), once(FF, D), once(2, D), once(2, D), chunk,
        ],
        out_specs=[chunk, chunk, chunk, chunk, states, whole(PAIRS, FEAT, PAIR)] + [ANY] * 6,
        out_shape=[
            make(D), make(D, f32), make(D), make(D), jax.ShapeDtypeStruct((steps, PAIRS, FEAT, PAIR), f32),
            jax.ShapeDtypeStruct((PAIRS, FEAT, PAIR), f32),
            make(one, bf16, D), make(one, bf16, D), make(two, bf16, D), make(D, bf16, D), make(D, bf16, D),
            make(HALF + PAIR, bf16, D),
        ],
        scratch_shapes=[
            pltpu.VMEM((CHUNK, D), bf16), pltpu.VMEM((CHUNK, FF), bf16), pltpu.VMEM((CHUNK, FF), f32),
            pltpu.VMEM((CHUNK, FF), bf16), pltpu.VMEM((FF, D), f32), pltpu.VMEM((D, FF), f32), pltpu.VMEM((D, D), f32),
            pltpu.VMEM((4, D), f32), pltpu.VMEM((3, D, D), bf16), pltpu.VMEM((2, D, PAIR), bf16),
            pltpu.SemaphoreType.DMA((3,)), pltpu.SemaphoreType.DMA((2,)),
        ],
    )(sc, tokens, q, k, v, pre, init, cos, sin, table, w_out, w_up, w_down, gains, biases, cot)


def sigmoid_of(soft):
    return jnp.where(soft < 0.01, soft * (1.0 - 0.5 * soft), 1.0 - jnp.exp(-soft))


def attend_back_kernel(
    angle, block, own, sc, tok, q_ref, k_ref, v_ref, dnum_ref, dden_ref, pre, init, part, d_init, cos, sin, table, table_t,
    *refs,
):
    if own:
        *got, out_ref, keep_ref, send_ref, run, acc, wide = refs
    else:
        out_ref, *other_refs, run, acc = refs
    pairs = PAIRS // 2
    later = sc[0].astype(f32)

    @pl.when(pl.program_id(0) == 0)
    def _():
        for p in range(pairs):
            run[p] = turn_state(d_init[p], -angle, 1.0 - later)

    second = lane_head(CHUNK) == 1
    second2 = jnp.concatenate([second, second], axis=1)

    def split(x, mask):
        zero = jnp.zeros_like(x)
        return jnp.where(mask, zero, x), jnp.where(mask, x, zero)

    for p in range(pairs):
        cols = slice(p * PAIR, (p + 1) * PAIR)
        q, k, v = q_ref[:, cols], k_ref[:, cols], v_ref[:, cols]
        q_wide, k_wide = q.astype(f32), k.astype(f32)
        dnum = dnum_ref[:, cols]
        grad = jnp.concatenate([dnum, dden_ref[:, cols]], axis=1)
        v_ones = with_ones(v)
        state = unpack_state(pre[0, p] + turn_state(init[p], angle, later))
        d_state = unpack_state(run[p])
        run[p] += part[0, p]
        dq_feat = nt(grad, state)
        dk_feat = nt(v_ones, d_state)
        dv = nn(features(k_wide, cos[...], sin[...]), d_state[:, :PAIR])
        dq = dq_feat[:, :PAIR] * cos[...] + dq_feat[:, PAIR:] * sin[...]
        dk = dk_feat[:, :PAIR] * cos[...] + dk_feat[:, PAIR:] * sin[...]
        for grad_h, q_h, k_h, dnum_h in zip(split(grad, second2), split(q, second), split(k, second), split(dnum, second)):
            d_score = (nt(grad_h, v_ones) * table[...]).astype(bf16)
            dq += nn(d_score, k_h)
            score_t = (nt(k_h, q) * table_t[...]).astype(bf16)
            d_score_t = (nt(v_ones, grad_h) * table_t[...]).astype(bf16)
            dk += nn(d_score_t, q_h)
            dv += nn(score_t, dnum_h)
        out_ref[:, cols] = (dq.astype(bf16).astype(f32) * sigmoid_of(q_wide)).astype(bf16)
        out_ref[:, slice(HALF + p * PAIR, HALF + (p + 1) * PAIR)] = (
            dk.astype(bf16).astype(f32) * sigmoid_of(k_wide)
        ).astype(bf16)
        out_ref[:, slice(D + p * PAIR, D + (p + 1) * PAIR)] = dv.astype(bf16)
    acc[...] = jnp.where(pl.program_id(0) == 0, 0.0, acc[...]) + tn(tok[...], out_ref[...])

    @pl.when(pl.program_id(0) == pl.num_programs(0) - 1)
    def _():
        me = sc[1] if own else sc[2]
        for b in range(D // block):
            to = pl.ds(pl.multiple_of((jnp.int32(b) ^ me) * block, block), block)
            for j in range(3):
                cols = slice(j * HALF, (j + 1) * HALF)
                piece = acc[b * block : (b + 1) * block, cols]
                if own:
                    wide[to, cols] = (piece + got[j][to, :].astype(f32)).astype(bf16)
                else:
                    other_refs[j][to, :] = piece.astype(bf16)
        if own:
            keep_ref[...] = wide[:HALF]
            send_ref[...] = wide[HALF:]


def attend_back(
    sc, tokens, q, k, v, dnum, dden, pre, init, part, d_init, cos, sin, table, table_t, block, got=None, deps=()
):
    own = got is not None
    rows = q.shape[0]
    steps = rows // CHUNK
    last = steps - 1
    pairs = PAIRS // 2

    def half(sc):
        return sc[0] if own else 1 - sc[0]

    def make(height):
        return jax.ShapeDtypeStruct((height, 3 * HALF), bf16)

    chunk = pl.BlockSpec((CHUNK, HALF), lambda i, sc: (last - i, half(sc)))
    states = pl.BlockSpec((1, pairs, FEAT, PAIR), lambda i, sc: (last - i, half(sc), 0, 0))
    state = pl.BlockSpec((pairs, FEAT, PAIR), lambda i, sc: (half(sc), 0, 0))
    thin = by_chunk(PAIR, last)
    return ordered_call(
        functools.partial(attend_back_kernel, STEP_ANGLE * rows, block, own),
        "attend_back",
        scalars=1,
        deps=deps,
        grid=(steps,),
        in_specs=[
            by_chunk(D, last), chunk, chunk, chunk, chunk, chunk, states, state, states, state, thin, thin,
            whole(CHUNK, CHUNK), whole(CHUNK, CHUNK),
        ] + [whole(D, HALF)] * (3 * own),
        out_specs=[by_chunk(3 * HALF, last)] + ([whole(HALF, 3 * HALF)] * 2 if own else [whole(D, HALF)] * 3),
        out_shape=[make(rows)] + ([make(HALF)] * 2 if own else [jax.ShapeDtypeStruct((D, HALF), bf16)] * 3),
        scratch_shapes=[pltpu.VMEM((pairs, FEAT, PAIR), f32), pltpu.VMEM((D, 3 * HALF), f32)]
        + [pltpu.VMEM((D, 3 * HALF), bf16)] * own,
    )(sc, tokens, q, k, v, dnum, dden, pre, init, part, d_init, cos, sin, table, table_t, *(got or ()))


def token_grad_kernel(sc, dres_one, first, second, wq1, wk1, wv1, wq2, wk2, wv2, out):
    total = dres_one[...]
    for d, weights in ((first, (wq1, wk1, wv1)), (second, (wq2, wk2, wv2))):
        for j, w in enumerate(weights):
            total += nt(d[:, j * HALF : (j + 1) * HALF], w[...])
    out[...] = total


def token_grad(sc, dres_one, other, own, wq, wk, wv, deps=()):
    rows = own.shape[0]
    w_other = pl.BlockSpec((D, HALF), lambda i, sc: (0, 1 - sc[0]))
    w_own = pl.BlockSpec((D, HALF), lambda i, sc: (0, sc[0]))
    return ordered_call(
        token_grad_kernel,
        "token_grad",
        scalars=1,
        deps=deps,
        grid=(rows // CHUNK,),
        in_specs=[by_chunk(D), by_chunk(3 * HALF), by_chunk(3 * HALF)] + [w_other] * 3 + [w_own] * 3,
        out_specs=by_chunk(D),
        out_shape=jax.ShapeDtypeStruct((rows, D), f32),
    )(sc, dres_one, other, own, wq, wk, wv, wq, wk, wv)


def small_call(kernel, ins, out_rows, name, deps=()):
    width = ins[0].shape[1]
    many = isinstance(out_rows, (list, tuple))

    def shape(rows):
        return jax.ShapeDtypeStruct((rows, width), bf16)

    return ordered_call(
        kernel,
        name,
        deps=deps,
        grid=(1,),
        in_specs=[whole(*x.shape) for x in ins],
        out_specs=[whole(r, width) for r in out_rows] if many else whole(out_rows, width),
        out_shape=[shape(r) for r in out_rows] if many else shape(out_rows),
    )(*ins)


def add_cut_kernel(a, b, *outs):
    rows = outs[0].shape[0]
    for i, out in enumerate(outs):
        at = slice(i * rows, (i + 1) * rows)
        out[...] = (a[at].astype(f32) + b[at].astype(f32)).astype(bf16)


def add_cut_parts_kernel(a, first, second, rest, keep, send):
    start = 0
    for part in (first, second, rest):
        cols = slice(start, start + part.shape[1])
        keep[:, cols] = (a[:HALF, cols].astype(f32) + part[:HALF].astype(f32)).astype(bf16)
        send[:, cols] = (a[HALF:, cols].astype(f32) + part[HALF:].astype(f32)).astype(bf16)
        start += part.shape[1]


def add_all_kernel(*refs):
    total = refs[0][...].astype(f32)
    for ref in refs[1:-1]:
        total += ref[...].astype(f32)
    refs[-1][...] = total.astype(bf16)


def join_kernel(*refs):
    rows = refs[0].shape[0]
    for i, ref in enumerate(refs[:-1]):
        refs[-1][i * rows : (i + 1) * rows] = ref[...]


def add_cut(a, b, parts, deps=()):
    return small_call(add_cut_kernel, [a, b], [a.shape[0] // parts] * parts, "add_cut", deps)


def add_all(parts, deps=()):
    return small_call(add_all_kernel, parts, parts[0].shape[0], "add_all", deps)


def join(parts, deps=()):
    return small_call(join_kernel, parts, len(parts) * parts[0].shape[0], "join", deps)


def restore(me, block, quarters, put):
    for place in range(D // block):
        ref, at = quarters[place * block // QUARTER], place * block % QUARTER
        put(pl.multiple_of((jnp.int32(place) ^ me) * block, block), ref[at : at + block, :].astype(f32))


def gather_kernel(block, per_core, sc, *refs):
    mine, other, out = refs[:4], refs[4:8], refs[8]

    def put(row, piece):
        out[pl.ds(row, block), :] = piece

    is_mine = pl.program_id(0) // per_core == sc[0]

    @pl.when(is_mine)
    def _():
        restore(sc[1], block, mine, put)

    @pl.when(jnp.logical_not(is_mine))
    def _():
        restore(sc[2], block, other, put)


def gather_units(sc, parts, block, by_rows, deps=()):
    def at(own):
        def index(g, sc):
            return (0, jnp.clip(g - 2 * (sc[0] if own else 1 - sc[0]), 0, 1))

        return pl.BlockSpec((QUARTER, D), index)

    return ordered_call(
        functools.partial(gather_kernel, block, 2),
        "gather_units",
        scalars=1,
        deps=deps,
        grid=(4,),
        in_specs=[at(True)] * 4 + [at(False)] * 4,
        out_specs=pl.BlockSpec((D, D), (lambda g, sc: (g, 0)) if by_rows else (lambda g, sc: (0, g))),
        out_shape=jax.ShapeDtypeStruct((4 * D, D) if by_rows else (D, 4 * D), f32),
    )(sc, *parts)


def half_of(block, sc, group, start, size, store):
    mine, other = group[:4], group[4:]

    def cut(refs):
        return [ref.at[:, start : start + size] for ref in refs]

    is_mine = pl.program_id(0) == sc[0]

    @pl.when(is_mine)
    def _():
        restore(sc[1], block, cut(mine), store)

    @pl.when(jnp.logical_not(is_mine))
    def _():
        restore(sc[2], block, cut(other), store)


def gather_qkv_kernel(block, sc, *refs):
    for j, out in enumerate(refs[8:]):
        def put(row, piece, out=out):
            out[pl.ds(row, block), :] = piece

        half_of(block, sc, refs[:8], j * HALF, HALF, put)


def gather_qkv(sc, parts, block, deps=()):
    shape = jax.ShapeDtypeStruct((D, D), f32)
    return ordered_call(
        functools.partial(gather_qkv_kernel, block),
        "gather_qkv",
        scalars=1,
        deps=deps,
        grid=(2,),
        in_specs=[whole(QUARTER, 3 * HALF)] * 8,
        out_specs=[pl.BlockSpec((D, HALF), lambda g, sc: (0, g))] * 3,
        out_shape=[shape] * 3,
    )(sc, *parts)


def gather_rest_kernel(block, sc, *refs):
    group, out, gains, biases, rows = refs[:8], *refs[8:]

    def put(row, piece):
        out[pl.ds(row, block), :] = piece

    def put_norm(row, piece):
        rows[pl.ds(row, block), :] = piece

    half_of(block, sc, group, 0, HALF, put)

    @pl.when(pl.program_id(0) == 0)
    def _():
        half_of(block, sc, group, HALF, PAIR, put_norm)
        for i in range(2):
            for j in range(PAIRS):
                cols = slice(j * PAIR, (j + 1) * PAIR)
                first, second = 2 * i * PAIRS + j, (2 * i + 1) * PAIRS + j
                gains[i : i + 1, cols] = rows[first : first + 1, :]
                biases[i : i + 1, cols] = rows[second : second + 1, :]


def gather_rest(sc, parts, block, deps=()):
    norm = jax.ShapeDtypeStruct((2, D), f32)
    spec = pl.BlockSpec((QUARTER, HALF + PAIR), lambda g, sc: (0, 2 * D // (HALF + PAIR)))
    return ordered_call(
        functools.partial(gather_rest_kernel, block),
        "gather_rest",
        scalars=1,
        deps=deps,
        grid=(2,),
        in_specs=[spec] * 8,
        out_specs=[pl.BlockSpec((D, HALF), lambda g, sc: (0, g)), whole(2, D), whole(2, D)],
        out_shape=[jax.ShapeDtypeStruct((D, D), f32), norm, norm],
        scratch_shapes=[pltpu.VMEM((D, PAIR), f32)],
    )(sc, *parts)


def make_local(n_dp, n_head):
    n_z = n_dp // 2
    direct = QUARTER % (16 * n_z) == 0 and n_z & (n_z - 1) == 0
    places = n_z if direct else 1
    block = QUARTER // places
    both_axes = ("dp", "head")

    def swap(x, partner):
        pairs = []
        for d in range(n_dp):
            for h in range(n_head):
                to_d, to_h = partner(d, h)
                pairs.append((d * n_head + h, to_d * n_head + to_h))
        return lax.ppermute(x, both_axes, pairs)

    def swap_core(x):
        return swap(x, lambda d, h: (d, h ^ 1))

    def swap_first(x):
        return swap(x, lambda d, h: (d ^ 1, h) if h % 2 else (d, h ^ 2))

    def swap_second(x):
        return swap(x, lambda d, h: (d, h ^ 2) if h % 2 else (d ^ 1, h))

    def swap_z(x, k):
        return swap(x, lambda d, h: (d ^ (2 * k), h))

    def cut_z(keep, got, deps=()):
        if direct:
            parts = add_cut(keep, got, n_z, deps)
            return [parts[0]] + [swap_z(parts[i], i) for i in range(1, n_z)]
        both = keep.astype(f32) + got.astype(f32)
        same_z = [[2 * i + j for i in range(n_z)] for j in range(2)]
        return lax.psum(both, "dp", axis_index_groups=same_z).astype(bf16)

    def share_z(parts, deps=()):
        if not direct:
            return parts
        share = add_all(parts, deps)
        return [share] + [swap_z(share, i) for i in range(1, n_z)]

    def spread(parts, deps=()):
        own = join(parts, deps) if direct else parts
        second = swap_second(own)
        first = swap_first(own)
        both = swap_first(second)
        quarters = [own, second, first, both]
        return quarters + [swap_core(x) for x in quarters]

    def local(tokens, w_query, w_key, w_value, w_out, w_up, w_down, norm_gains, norm_biases, cotangent):
        rows = tokens.shape[0]
        assert LENGTH == 2 * rows and n_head % 4 == 0 and n_dp % 2 == 0
        head, dp = lax.axis_index("head"), lax.axis_index("dp")
        core, x, y, z = head % 2, head // 2, dp % 2, dp // 2
        rank = z if direct else 0
        by_x, by_y = (2 * x + y) * places + rank, (2 * y + x) * places + rank
        sc = jnp.stack([core, jnp.where(core == 0, by_x, by_y), jnp.where(core == 0, by_y, by_x)]).astype(jnp.int32)
        angle = STEP_ANGLE * np.arange(rows)
        cos = jnp.asarray(np.broadcast_to(np.cos(angle)[:, None], (rows, PAIR)), f32)
        sin = jnp.asarray(np.broadcast_to(np.sin(angle)[:, None], (rows, PAIR)), f32)
        gap = np.arange(CHUNK)[:, None] - np.arange(CHUNK)[None, :]
        weights = np.where(gap >= 0, np.cos(STEP_ANGLE * gap), 0.0)
        table, table_t = jnp.asarray(weights, f32), jnp.asarray(weights.T, f32)

        q, k, v, pre, total = project(tokens, w_query, w_key, w_value, cos, sin)
        init = swap_core(total)
        out, dres_one, dnum, dden, part, d_total, one_own, one_other, two_own, *two_other = rows_call(
            sc, tokens, q, k, v, pre, init, cos, sin, table, w_out, w_up, w_down, norm_gains, norm_biases, cotangent, block
        )
        one_got = swap_core(one_other)
        d_init = swap_core(d_total)
        two_got = [swap_core(x) for x in two_other]
        one_keep, one_send = add_cut(one_own, one_got, 2)
        one_got = swap_first(one_send)
        two_keep, two_send = small_call(
            add_cut_parts_kernel, [two_own, *two_got], [HALF, HALF], "add_cut", deps=(one_keep,)
        )
        two_got = swap_first(two_send)
        att = functools.partial(
            attend_back, sc, tokens, q, k, v, dnum, dden, pre, init, part, d_init, cos, sin, table, table_t, block
        )
        d_other, *three_other = att(deps=(two_keep,))
        three_got = [swap_core(x) for x in three_other]
        one_keep, one_send = add_cut(one_keep, one_got, 2, deps=(d_other,))
        one_got = swap_second(one_send)
        two_keep, two_send = add_cut(two_keep, two_got, 2, deps=(one_keep,))
        two_got = swap_second(two_send)
        d_own, three_keep, three_send = att(three_got, deps=(two_keep,))
        three_got = swap_first(three_send)
        one_parts = cut_z(one_keep, one_got, deps=(three_keep,))
        two_parts = cut_z(two_keep, two_got, deps=(one_parts[0],))
        d_tokens = token_grad(sc, dres_one, d_other, d_own, w_query, w_key, w_value, deps=(two_parts[0],))
        three_keep, three_send = add_cut(three_keep, three_got, 2, deps=(d_tokens,))
        three_got = swap_second(three_send)
        one_parts = share_z(one_parts, deps=(three_keep,))
        three_parts = cut_z(three_keep, three_got, deps=(one_parts[0],))
        two_parts = share_z(two_parts, deps=(three_parts[0],))
        one_parts = spread(one_parts, deps=(two_parts[0],))
        three_parts = share_z(three_parts, deps=(one_parts[0],))
        two_parts = spread(two_parts, deps=(three_parts[0],))
        three_parts = spread(three_parts, deps=(two_parts[0],))
        grad_down = gather_units(sc, one_parts, block, True, deps=(three_parts[0],))
        grad_up = gather_units(sc, two_parts, block, False, deps=(grad_down,))
        grad_out, grad_gains, grad_biases = gather_rest(sc, two_parts, block, deps=(grad_up,))
        grad_qkv = gather_qkv(sc, three_parts, block, deps=(grad_out,))
        return out, d_tokens, *grad_qkv, grad_out, grad_up, grad_down, grad_gains, grad_biases

    return local


def solution(mesh):
    rows, same = P(("dp", "head"), None), P()
    return jax.shard_map(
        make_local(mesh.shape["dp"], mesh.shape["head"]),
        mesh=mesh,
        in_specs=(rows,) + (same,) * 8 + (rows,),
        out_specs=(rows, rows) + (same,) * 8,
        check_vma=False,
    )
```

time: 396 us -> 328 us (0.83); the launches traced: 389 us -> 325 us
  waiting for transfers between devices: 110 us -> 58.9 us
  local copies, waits for them, and re-layouts: 22.3 us -> 7.26 us
  Pallas kernels: 180 us -> 185 us
  other arithmetic: 5.14 us -> 0.61 us
    ppermute x55 -> x54, waiting for transfers between devices: 110 us -> 58.9 us  [swap(): return lax.ppermute(x, both_axes, pairs)]
    unnamed x54 -> x44, local copies, waits for them, and re-layouts: 16 us -> 7.26 us
    pallas_call x17 -> x23, Pallas kernels: 180 us -> 185 us  [ordered_call(): return lambda *args: call(*args, *deps)]
    slice x10 -> x0, local copies, waits for them, and re-layouts: 4.25 us -> none  [the longest x3 4.11 us: reduce_units(): got_a, got_b = (swap_x(a[half:]), swap_y(b[half:]))]
    ppermute x55 -> x54, starting transfers between devices: 69.5 us -> 72.6 us  [swap(): return lax.ppermute(x, both_axes, pairs)]
  transfers between devices with their start and end apart: 55 -> 54, of which waited for: 28 -> 14; matrix products, arithmetic and copies ran while one was open for 4% -> 0% of each run, Pallas kernels for 28% -> 31%
where the time goes in v2:
time: 328 us; the launch traced here: 325 us
  Pallas kernels  185 us (56%)
  starting transfers between devices  72.6 us (22%)
  waiting for transfers between devices  58.9 us (18%)
  local copies, waits for them, and re-layouts  7.26 us (2%)
    pallas_call x23, Pallas kernels, ordered_call(): return lambda *args: call(*args, *deps)  185 us
    ppermute x54, starting transfers between devices, swap(): return lax.ppermute(x, both_axes, pairs)  72.6 us
    ppermute x54, waiting for transfers between devices, swap(): return lax.ppermute(x, both_axes, pairs)  58.9 us
    unnamed x44, local copies, waits for them, and re-layouts  7.26 us
  transfers between devices with their start and end apart: 54, of which 14 were waited for; matrix products, arithmetic and copies ran while one was open for 0% of the time, Pallas kernels for 31%

profile of v2, /device:TPU:0, one launch (start us, length us, event | category | flops | bytes accessed | tf_op | source)
XLA Modules:
  0.0 325.3 jit_solution(12393715410929621984)
XLA Ops:
  0.6 11.0 %project.1 = (bf16[1024,768]{1,0:T(8,128)(2,1)}, bf16[1024,768]{1,0:T(8,128)(2,1)}, bf16[1024,768]{1,0:T(8,128)(2,1)}, f32[4,6,256,128]{3,2,1,0:T(8,128)}, f32[6,256,128]{2,1,0:T(8,128)}) custom-call(bf16[1024,768]{1,0:T(8,128)(2,1)} %refs_1_.7, bf16[768,768]{1,0:T(8,128)(2,1)} %refs_7_.2, bf16[768,768]{1,0:T(8,128)(2,1)} %refs_8_.2, ...), custom_call_target="tpu_custom_call" | custom-call | flops 12650000384 | bytes 1 | tf_op jit(solution)/shard_map/project/pallas_call | solution.py:71
  15.2 64.5 %rows.1 = (bf16[1024,768]{1,0:T(8,128)(2,1)}, f32[1024,768]{1,0:T(8,128)}, bf16[1024,768]{1,0:T(8,128)(2,1)}, bf16[1024,768]{1,0:T(8,128)(2,1)}, f32[4,6,256,128...) custom-call(s32[3]{0:T(128)} %pad_add_fusion.refs_0_, ...), custom_call_target="tpu_custom_call" | custom-call | flops 69000003584 | bytes 1 | tf_op jit(solution)/shard_map/rows/pallas_call | solution.py:71
  81.2 3.5 %collective-permute-done.5.refs_1_ = bf16[768,1536]{1,0:T(8,128)(2,1)} collective-permute-done((bf16[768,1536]{1,0:T(8,128)(2,1)}, bf16[768,1536]{1,0:T(8,128)(2,1)}, u32[]{:S(2)}, u32[]{:S(2)}) %collective-permute-start.5) | collective-permute-done | bytes 2359328 | tf_op jit(solution)/shard_map/ppermute | solution.py:666
  84.7 4.1 %add_cut.8 = (bf16[384,1536]{1,0:T(8,128)(2,1)}, bf16[384,1536]{1,0:T(8,128)(2,1)}) custom-call(bf16[768,1536]{1,0:T(8,128)(2,1)} %get-tuple-element.77.refs_0_, bf16[768,1536]{1,0:T(8,128)(2,1)} %collective-permute-done.5.refs_1_), custom_call_target="tpu_custom_call" | custom-call | flops 2875000064 | bytes 1 | tf_op jit(solution)/shard_map/add_cut/pallas_call | solution.py:71
  88.8 2.8 collective-permute-start.10
  91.6 5.1 %add_cut.9 = (bf16[384,2048]{1,0:T(8,128)(2,1)}, bf16[384,2048]{1,0:T(8,128)(2,1)}) custom-call(bf16[768,2048]{1,0:T(8,128)(2,1)} %get-tuple-element.73.refs_0_, bf16[768,768]{1,0:T(8,128)(2,1)} %collective-permute-done.2.refs_1_, bf16[768,768]{1,0:T(8,128)(2,1)} %collective-permute-done.3.refs_2_, bf16[768,512]{1,0:T(8,128)(2,1)} %collective-permute-done.4.refs_3_, ...), custom_call_target="tpu_custom_call" | custom-call | flops 2875000064 | bytes 1 | tf_op jit(solution)/shard_map/add_cut/pallas_call | solution.py:71
  99.1 18.7 %attend_back.2 = (bf16[1024,1152]{1,0:T(8,128)(2,1)}, bf16[768,384]{1,0:T(8,128)(2,1)}, bf16[768,384]{1,0:T(8,128)(2,1)}, bf16[768,384]{1,0:T(8,128)(2,1)}) custom-call(s32[3]{0:T(128)} %pad_add_fusion.refs_0_, bf16[1024,768]{1,0:T(8,128)(2,1)} %refs_1_.7, bf16[1024,768]{1,0:T(8,128)(2,1)} %get-tuple-element.62.refs_2_, ...), custom_call_target="tpu_custom_call" | custom-call | flops 21849999360 | bytes 1 | tf_op jit(solution)/shard_map/attend_back/pallas_call | solution.py:71
  118.5 2.8 add_cut.10
  122.9 3.2 add_cut.11
  129.0 19.9 %attend_back.3 = (bf16[1024,1152]{1,0:T(8,128)(2,1)}, bf16[384,1152]{1,0:T(8,128)(2,1)}, bf16[384,1152]{1,0:T(8,128)(2,1)}) custom-call(s32[3]{0:T(128)} %pad_add_fusion.refs_0_, bf16[1024,768]{1,0:T(8,128)(2,1)} %refs_1_.7, bf16[1024,768]{1,0:T(8,128)(2,1)} %get-tuple-element.62.refs_2_, bf16[1024,768]{1,0:T(8,128)(2,1)} %get-tuple-element.63.refs_3_, ...), custom_call_target="tpu_custom_call" | custom-call | flops 21849999360 | bytes 1 | tf_op jit(solution)/shard_map/attend_back/pallas_call | solution.py:71
  154.8 10.6 %token_grad.1.refs_2_ = f32[1024,768]{1,0:T(8,128)} custom-call(s32[3]{0:T(128)} %pad_add_fusion.refs_0_, f32[1024,768]{1,0:T(8,128)} %get-tuple-element.68.refs_1_, bf16[1024,1152]{1,0:T(8,128)(2,1)} %get-tuple-element.81.refs_2_, bf16[1024,1152]{1,0:T(8,128)(2,1)} %get-tuple-element.89.refs_3_, bf16[768,768]{1,0:T(8,128)(2,1)} %refs_7_.2, ...), custom_call_target="tpu_custom_call" | custom-call | flops 11500000256 | bytes 1 | tf_op jit(solution)/shard_map/token_grad/pallas_call | solution.py:71
  166.4 2.4 add_cut.14
  170.9 2.6 collective-permute-start.16
  174.4 5.4 %collective-permute-done.15.refs_1_ = bf16[48,1536]{1,0:T(8,128)(2,1)S(1)} collective-permute-done((bf16[48,1536]{1,0:T(8,128)(2,1)}, bf16[48,1536]{1,0:T(8,128)(2,1)S(1)}, u32[]{:S(2)}, u32[]{:S(2)}) %collective-permute-start.15) | collective-permute-done | bytes 147488 | tf_op jit(solution)/shard_map/ppermute | solution.py:666
  179.7 3.7 %collective-permute-done.16.refs_2_ = bf16[48,1536]{1,0:T(8,128)(2,1)} collective-permute-done((bf16[48,1536]{1,0:T(8,128)(2,1)}, bf16[48,1536]{1,0:T(8,128)(2,1)}, u32[]{:S(2)}, u32[]{:S(2)}) %collective-permute-start.16) | collective-permute-done | bytes 147488 | tf_op jit(solution)/shard_map/ppermute | solution.py:666
  183.5 3.4 %collective-permute-start.26 = (bf16[48,2048]{1,0:T(8,128)(2,1)}, bf16[48,2048]{1,0:T(8,128)(2,1)}, u32[]{:S(2)}, u32[]{:S(2)}) collective-permute-start(bf16[48,2048]{1,0:T(8,128)(2,1)} %get-tuple-element.107), channel_id=1, source_target_pairs={{0,24},{1,25},{2,26},{3,27},{4,28},{5,29},{6,30},{7,31},{8,16},{9,... | collective-permute-start | bytes 589832 | tf_op jit(solution)/shard_map/ppermute | solution.py:666
  189.2 15.0 %collective-permute-start.22 = (bf16[48,1536]{1,0:T(8,128)(2,1)}, bf16[48,1536]{1,0:T(8,128)(2,1)}, u32[]{:S(2)}, u32[]{:S(2)}) collective-permute-start(bf16[48,1536]{1,0:T(8,128)(2,1)} %add_all.3.refs_2_.refs_0_), channel_id=1, source_target_pairs={{0,16},{1,17},{2,18},{3,19},{4,20},{5,21},{6,22},{7,23},{8,24},{9,... | collective-permute-start | bytes 442376 | tf_op jit(solution)/shard_map/ppermute | solution.py:666
  211.7 6.7 %collective-permute-start.31 = (bf16[48,2048]{1,0:T(8,128)(2,1)}, bf16[48,2048]{1,0:T(8,128)(2,1)S(1)}, u32[]{:S(2)}, u32[]{:S(2)}) collective-permute-start(bf16[48,2048]{1,0:T(8,128)(2,1)} %add_all.4.refs_4_.refs_0_), channel_id=1, source_target_pairs={{0,16},{1,17},{2,18},{3,19},{4,20},{5,21},{6,22},{7,23},{8,24},{9,... | collective-permute-start | bytes 589832 | tf_op jit(solution)/shard_map/ppermute | solution.py:666
  220.5 2.6 collective-permute-done.22.refs_2_
  223.7 7.5 %collective-permute-start.20 = (bf16[48,1152]{1,0:T(8,128)(2,1)}, bf16[48,1152]{1,0:T(8,128)(2,1)S(1)}, u32[]{:S(2)}, u32[]{:S(2)}) collective-permute-start(bf16[48,1152]{1,0:T(8,128)(2,1)} %get-tuple-element.104), channel_id=1, source_target_pairs={{0,24},{1,25},{2,26},{3,27},{4,28},{5,29},{6,30},{7,31},{8,16},{9,... | collective-permute-start | bytes 331784 | tf_op jit(solution)/shard_map/ppermute | solution.py:666
  233.8 6.4 %collective-permute-done.19.refs_2_ = bf16[48,1152]{1,0:T(8,128)(2,1)} collective-permute-done((bf16[48,1152]{1,0:T(8,128)(2,1)}, bf16[48,1152]{1,0:T(8,128)(2,1)}, u32[]{:S(2)}, u32[]{:S(2)}) %collective-permute-start.19) | collective-permute-done | bytes 110624 | tf_op jit(solution)/shard_map/ppermute | solution.py:666
  247.7 2.6 collective-permute-start.29
  250.7 4.8 %collective-permute-done.29.refs_3_ = bf16[48,1152]{1,0:T(8,128)(2,1)S(1)} collective-permute-done((bf16[48,1152]{1,0:T(8,128)(2,1)S(1)}, bf16[48,1152]{1,0:T(8,128)(2,1)S(1)}, u32[]{:S(2)}, u32[]{:S(2)}) %collective-permute-start.29) | collective-permute-done | bytes 110624 | tf_op jit(solution)/shard_map/ppermute | solution.py:666
  257.1 3.4 %collective-permute-done.28.refs_2_ = bf16[48,1152]{1,0:T(8,128)(2,1)S(1)} collective-permute-done((bf16[48,1152]{1,0:T(8,128)(2,1)S(1)}, bf16[48,1152]{1,0:T(8,128)(2,1)S(1)}, u32[]{:S(2)}, u32[]{:S(2)}) %collective-permute-start.28) | collective-permute-done | bytes 110624 | tf_op jit(solution)/shard_map/ppermute | solution.py:666
  262.5 2.9 collective-permute-done.27.refs_1_
  271.0 10.3 %collective-permute-done.34.refs_3_ = bf16[192,1152]{1,0:T(8,128)(2,1)S(1)} collective-permute-done((bf16[192,1152]{1,0:T(8,128)(2,1)}, bf16[192,1152]{1,0:T(8,128)(2,1)S(1)}, u32[]{:S(2)}, u32[]{:S(2)}) %collective-permute-start.34) | collective-permute-done | bytes 442400 | tf_op jit(solution)/shard_map/ppermute | solution.py:666
  282.5 7.4 %collective-permute-done.41.refs_3_ = bf16[192,2048]{1,0:T(8,128)(2,1)} collective-permute-done((bf16[192,2048]{1,0:T(8,128)(2,1)S(1)}, bf16[192,2048]{1,0:T(8,128)(2,1)}, u32[]{:S(2)}, u32[]{:S(2)}) %collective-permute-start.41) | collective-permute-done | bytes 786464 | tf_op jit(solution)/shard_map/ppermute | solution.py:666
  292.1 6.2 %collective-permute-done.42.refs_4_ = bf16[192,2048]{1,0:T(8,128)(2,1)} collective-permute-done((bf16[192,2048]{1,0:T(8,128)(2,1)}, bf16[192,2048]{1,0:T(8,128)(2,1)}, u32[]{:S(2)}, u32[]{:S(2)}) %collective-permute-start.42) | collective-permute-done | bytes 786464 | tf_op jit(solution)/shard_map/ppermute | solution.py:666
  298.3 7.5 %gather_units.2.refs_9_ = f32[3072,768]{1,0:T(8,128)} custom-call(s32[3]{0:T(128)} %pad_add_fusion.refs_0_, bf16[192,1536]{1,0:T(8,128)(2,1)} %join.3.refs_4_.refs_1_, bf16[192,1536]{1,0:T(8,128)(2,1)} %collective-permute-done.47.refs_2_, bf16[192,1536]{1,0:T(8,128)(2,1)} %collective-permute-done.48.refs_3_, ...), custom_call_target="tpu_custom_call" | custom-call | flops 9200000000 | bytes 1 | tf_op jit(solution)/shard_map/gather_units/pallas_call | solution.py:71
  307.1 7.6 %gather_units.3.refs_9_ = f32[768,3072]{1,0:T(8,128)} custom-call(s32[3]{0:T(128)} %pad_add_fusion.refs_0_, bf16[192,2048]{1,0:T(8,128)(2,1)} %join.4.refs_4_.refs_1_, bf16[192,2048]{1,0:T(8,128)(2,1)} %collective-permute-done.40.refs_2_, bf16[192,2048]{1,0:T(8,128)(2,1)} %collective-permute-done.41.refs_3_, ...), custom_call_target="tpu_custom_call" | custom-call | flops 9200000000 | bytes 1 | tf_op jit(solution)/shard_map/gather_units/pallas_call | solution.py:71
  314.7 3.7 %gather_rest.1 = (f32[768,768]{1,0:T(8,128)}, f32[2,768]{1,0:T(2,128)}, f32[2,768]{1,0:T(2,128)}) custom-call(s32[3]{0:T(128)} %pad_add_fusion.refs_0_, bf16[192,2048]{1,0:T(8,128)(2,1)} %join.4.refs_4_.refs_1_, bf16[192,2048]{1,0:T(8,128)(2,1)} %collective-permute-done.40.refs_2_, bf16[192,2048]{1,0:T(8,128)(2,1)} %collective-permute-done.41.refs_3_, ...), custom_call_target="tpu_custom_call" | custom-call | flops 4600000000 | bytes 1 | tf_op jit(solution)/shard_map/gather_rest/pallas_call | solution.py:71
  319.4 5.9 %gather_qkv.1 = (f32[768,768]{1,0:T(8,128)}, f32[768,768]{1,0:T(8,128)}, f32[768,768]{1,0:T(8,128)}) custom-call(s32[3]{0:T(128)} %pad_add_fusion.refs_0_, bf16[192,1152]{1,0:T(8,128)(2,1)} %join.5.refs_9_.refs_1_, bf16[192,1152]{1,0:T(8,128)(2,1)} %collective-permute-done.33.refs_2_, bf16[192,1152]{1,0:T(8,128)(2,1)} %copy-done.5, ...), custom_call_target="tpu_custom_call" | custom-call | flops 6325000192 | bytes 1 | tf_op jit(solution)/shard_map/gather_qkv/pallas_call | solution.py:71
  (144 shorter events, 60.1 us)
Async XLA Ops:
  80.8 17.4 %collective-permute-start.1 = (f32[6,256,128]{2,1,0:T(8,128)}, f32[6,256,128]{2,1,0:T(8,128)S(1)}, u32[]{:S(2)}, u32[]{:S(2)}) collective-permute-start(f32[6,256,128]{2,1,0:T(8,128)} %get-tuple-element.72), channel_id=1, source_target_pairs={{0,1},{1,0},{2,3},{3,2},{4,5},{5,4},{6,7},{7,6},{8,9},{9,8},{10,11... | collective-permute-start | bytes 2359304 | tf_op jit(solution)/shard_map/ppermute | solution.py:666
  88.8 29.7 %collective-permute-start.10 = (bf16[384,1536]{1,0:T(8,128)(2,1)}, bf16[384,1536]{1,0:T(8,128)(2,1)}, u32[]{:S(2)}, u32[]{:S(2)}) collective-permute-start(bf16[384,1536]{1,0:T(8,128)(2,1)} %get-tuple-element.86), channel_id=1, source_target_pairs={{0,2},{1,5},{2,0},{3,7},{4,6},{5,1},{6,4},{7,3},{8,10},{9,13},{10,... | collective-permute-start | bytes 3538952 | tf_op jit(solution)/shard_map/ppermute | solution.py:666
  96.7 26.2 %collective-permute-start.9 = (bf16[384,2048]{1,0:T(8,128)(2,1)}, bf16[384,2048]{1,0:T(8,128)(2,1)}, u32[]{:S(2)}, u32[]{:S(2)}) collective-permute-start(bf16[384,2048]{1,0:T(8,128)(2,1)} %get-tuple-element.85), channel_id=1, source_target_pairs={{0,2},{1,5},{2,0},{3,7},{4,6},{5,1},{6,4},{7,3},{8,10},{9,13},{10,... | collective-permute-start | bytes 4718600 | tf_op jit(solution)/shard_map/ppermute | solution.py:666
  121.3 29.2 %collective-permute-start.12 = (bf16[192,1536]{1,0:T(8,128)(2,1)}, bf16[192,1536]{1,0:T(8,128)(2,1)}, u32[]{:S(2)}, u32[]{:S(2)}) collective-permute-start(bf16[192,1536]{1,0:T(8,128)(2,1)} %get-tuple-element.91), channel_id=1, source_target_pairs={{0,4},{1,3},{2,6},{3,1},{4,0},{5,7},{6,2},{7,5},{8,12},{9,11},{10,... | collective-permute-start | bytes 1769480 | tf_op jit(solution)/shard_map/ppermute | solution.py:666
  126.1 26.4 %collective-permute-start.11 = (bf16[192,2048]{1,0:T(8,128)(2,1)}, bf16[192,2048]{1,0:T(8,128)(2,1)}, u32[]{:S(2)}, u32[]{:S(2)}) collective-permute-start(bf16[192,2048]{1,0:T(8,128)(2,1)} %get-tuple-element.90), channel_id=1, source_target_pairs={{0,4},{1,3},{2,6},{3,1},{4,0},{5,7},{6,2},{7,5},{8,12},{9,11},{10,... | collective-permute-start | bytes 2359304 | tf_op jit(solution)/shard_map/ppermute | solution.py:666
  148.9 16.6 %collective-permute-start.13 = (bf16[384,1152]{1,0:T(8,128)(2,1)}, bf16[384,1152]{1,0:T(8,128)(2,1)S(1)}, u32[]{:S(2)}, u32[]{:S(2)}) collective-permute-start(bf16[384,1152]{1,0:T(8,128)(2,1)} %get-tuple-element.95), channel_id=1, source_target_pairs={{0,2},{1,5},{2,0},{3,7},{4,6},{5,1},{6,4},{7,3},{8,10},{9,13},{10,... | collective-permute-start | bytes 2654216 | tf_op jit(solution)/shard_map/ppermute | solution.py:666
  168.8 20.3 %collective-permute-start.14 = (bf16[192,1152]{1,0:T(8,128)(2,1)}, bf16[192,1152]{1,0:T(8,128)(2,1)S(1)}, u32[]{:S(2)}, u32[]{:S(2)}) collective-permute-start(bf16[192,1152]{1,0:T(8,128)(2,1)} %get-tuple-element.97), channel_id=1, source_target_pairs={{0,4},{1,3},{2,6},{3,1},{4,0},{5,7},{6,2},{7,5},{8,12},{9,11},{10,... | collective-permute-start | bytes 1327112 | tf_op jit(solution)/shard_map/ppermute | solution.py:666
  173.5 13.4 %collective-permute-start.17 = (bf16[48,1536]{1,0:T(8,128)(2,1)}, bf16[48,1536]{1,0:T(8,128)(2,1)}, u32[]{:S(2)}, u32[]{:S(2)}) collective-permute-start(bf16[48,1536]{1,0:T(8,128)(2,1)} %get-tuple-element.100), channel_id=1, source_target_pairs={{0,24},{1,25},{2,26},{3,27},{4,28},{5,29},{6,30},{7,31},{8,16},{9,... | collective-permute-start | bytes 442376 | tf_op jit(solution)/shard_map/ppermute | solution.py:666
  173.7 32.4 %collective-permute-start.24 = (bf16[48,2048]{1,0:T(8,128)(2,1)}, bf16[48,2048]{1,0:T(8,128)(2,1)S(1)}, u32[]{:S(2)}, u32[]{:S(2)}) collective-permute-start(bf16[48,2048]{1,0:T(8,128)(2,1)} %get-tuple-element.105), channel_id=1, source_target_pairs={{0,8},{1,9},{2,10},{3,11},{4,12},{5,13},{6,14},{7,15},{8,0},{9,1},... | collective-permute-start | bytes 589832 | tf_op jit(solution)/shard_map/ppermute | solution.py:666
  179.7 27.7 %collective-permute-start.25 = (bf16[48,2048]{1,0:T(8,128)(2,1)}, bf16[48,2048]{1,0:T(8,128)(2,1)S(1)}, u32[]{:S(2)}, u32[]{:S(2)}) collective-permute-start(bf16[48,2048]{1,0:T(8,128)(2,1)} %get-tuple-element.106), channel_id=1, source_target_pairs={{0,16},{1,17},{2,18},{3,19},{4,20},{5,21},{6,22},{7,23},{8,24},{9,... | collective-permute-start | bytes 589832 | tf_op jit(solution)/shard_map/ppermute | solution.py:666
  183.5 24.0 %collective-permute-start.26 = (bf16[48,2048]{1,0:T(8,128)(2,1)}, bf16[48,2048]{1,0:T(8,128)(2,1)}, u32[]{:S(2)}, u32[]{:S(2)}) collective-permute-start(bf16[48,2048]{1,0:T(8,128)(2,1)} %get-tuple-element.107), channel_id=1, source_target_pairs={{0,24},{1,25},{2,26},{3,27},{4,28},{5,29},{6,30},{7,31},{8,16},{9,... | collective-permute-start | bytes 589832 | tf_op jit(solution)/shard_map/ppermute | solution.py:666
  188.7 29.8 %collective-permute-start.23 = (bf16[48,1536]{1,0:T(8,128)(2,1)}, bf16[48,1536]{1,0:T(8,128)(2,1)}, u32[]{:S(2)}, u32[]{:S(2)}) collective-permute-start(bf16[48,1536]{1,0:T(8,128)(2,1)} %add_all.3.refs_2_.refs_0_), channel_id=1, source_target_pairs={{0,24},{1,25},{2,26},{3,27},{4,28},{5,29},{6,30},{7,31},{8,16},{9,... | collective-permute-start | bytes 442376 | tf_op jit(solution)/shard_map/ppermute | solution.py:666
  189.2 33.9 %collective-permute-start.22 = (bf16[48,1536]{1,0:T(8,128)(2,1)}, bf16[48,1536]{1,0:T(8,128)(2,1)}, u32[]{:S(2)}, u32[]{:S(2)}) collective-permute-start(bf16[48,1536]{1,0:T(8,128)(2,1)} %add_all.3.refs_2_.refs_0_), channel_id=1, source_target_pairs={{0,16},{1,17},{2,18},{3,19},{4,20},{5,21},{6,22},{7,23},{8,24},{9,... | collective-permute-start | bytes 442376 | tf_op jit(solution)/shard_map/ppermute | solution.py:666
  206.1 16.9 %collective-permute-start.21 = (bf16[48,1536]{1,0:T(8,128)(2,1)S(1)}, bf16[48,1536]{1,0:T(8,128)(2,1)S(1)}, u32[]{:S(2)}, u32[]{:S(2)}) collective-permute-start(bf16[48,1536]{1,0:T(8,128)(2,1)S(1)} %copy-done.15), channel_id=1, source_target_pairs={{0,8},{1,9},{2,10},{3,11},{4,12},{5,13},{6,14},{7,15},{8,0},{9,1},... | collective-permute-start | bytes 442376 | tf_op jit(solution)/shard_map/ppermute | solution.py:666
  210.1 32.6 %collective-permute-start.32 = (bf16[48,2048]{1,0:T(8,128)(2,1)}, bf16[48,2048]{1,0:T(8,128)(2,1)S(1)}, u32[]{:S(2)}, u32[]{:S(2)}) collective-permute-start(bf16[48,2048]{1,0:T(8,128)(2,1)} %add_all.4.refs_4_.refs_0_), channel_id=1, source_target_pairs={{0,24},{1,25},{2,26},{3,27},{4,28},{5,29},{6,30},{7,31},{8,16},{9,... | collective-permute-start | bytes 589832 | tf_op jit(solution)/shard_map/ppermute | solution.py:666
  211.7 30.9 %collective-permute-start.31 = (bf16[48,2048]{1,0:T(8,128)(2,1)}, bf16[48,2048]{1,0:T(8,128)(2,1)S(1)}, u32[]{:S(2)}, u32[]{:S(2)}) collective-permute-start(bf16[48,2048]{1,0:T(8,128)(2,1)} %add_all.4.refs_4_.refs_0_), channel_id=1, source_target_pairs={{0,16},{1,17},{2,18},{3,19},{4,20},{5,21},{6,22},{7,23},{8,24},{9,... | collective-permute-start | bytes 589832 | tf_op jit(solution)/shard_map/ppermute | solution.py:666
  218.5 14.8 %collective-permute-start.18 = (bf16[48,1152]{1,0:T(8,128)(2,1)}, bf16[48,1152]{1,0:T(8,128)(2,1)}, u32[]{:S(2)}, u32[]{:S(2)}) collective-permute-start(bf16[48,1152]{1,0:T(8,128)(2,1)} %get-tuple-element.102), channel_id=1, source_target_pairs={{0,8},{1,9},{2,10},{3,11},{4,12},{5,13},{6,14},{7,15},{8,0},{9,1},... | collective-permute-start | bytes 331784 | tf_op jit(solution)/shard_map/ppermute | solution.py:666
  223.1 17.2 %collective-permute-start.19 = (bf16[48,1152]{1,0:T(8,128)(2,1)}, bf16[48,1152]{1,0:T(8,128)(2,1)}, u32[]{:S(2)}, u32[]{:S(2)}) collective-permute-start(bf16[48,1152]{1,0:T(8,128)(2,1)} %get-tuple-element.103), channel_id=1, source_target_pairs={{0,16},{1,17},{2,18},{3,19},{4,20},{5,21},{6,22},{7,23},{8,24},{9,... | collective-permute-start | bytes 331784 | tf_op jit(solution)/shard_map/ppermute | solution.py:666
  223.7 16.5 %collective-permute-start.20 = (bf16[48,1152]{1,0:T(8,128)(2,1)}, bf16[48,1152]{1,0:T(8,128)(2,1)S(1)}, u32[]{:S(2)}, u32[]{:S(2)}) collective-permute-start(bf16[48,1152]{1,0:T(8,128)(2,1)} %get-tuple-element.104), channel_id=1, source_target_pairs={{0,24},{1,25},{2,26},{3,27},{4,28},{5,29},{6,30},{7,31},{8,16},{9,... | collective-permute-start | bytes 331784 | tf_op jit(solution)/shard_map/ppermute | solution.py:666
  240.3 28.3 %collective-permute-start.50 = (bf16[192,1536]{1,0:T(8,128)(2,1)}, bf16[192,1536]{1,0:T(8,128)(2,1)}, u32[]{:S(2)}, u32[]{:S(2)}) collective-permute-start(bf16[192,1536]{1,0:T(8,128)(2,1)} %join.3.refs_4_.refs_1_), channel_id=1, source_target_pairs={{0,1},{1,0},{2,3},{3,2},{4,5},{5,4},{6,7},{7,6},{8,9},{9,8},{10,11... | collective-permute-start | bytes 1769480 | tf_op jit(solution)/shard_map/ppermute | solution.py:666
  240.3 20.8 %collective-permute-start.47 = (bf16[192,1536]{1,0:T(8,128)(2,1)}, bf16[192,1536]{1,0:T(8,128)(2,1)}, u32[]{:S(2)}, u32[]{:S(2)}) collective-permute-start(bf16[192,1536]{1,0:T(8,128)(2,1)} %join.3.refs_4_.refs_1_), channel_id=1, source_target_pairs={{0,4},{1,3},{2,6},{3,1},{4,0},{5,7},{6,2},{7,5},{8,12},{9,11},{10,... | collective-permute-start | bytes 1769480 | tf_op jit(solution)/shard_map/ppermute | solution.py:666
  246.2 23.7 %collective-permute-start.40 = (bf16[192,2048]{1,0:T(8,128)(2,1)}, bf16[192,2048]{1,0:T(8,128)(2,1)}, u32[]{:S(2)}, u32[]{:S(2)}) collective-permute-start(bf16[192,2048]{1,0:T(8,128)(2,1)} %join.4.refs_4_.refs_1_), channel_id=1, source_target_pairs={{0,4},{1,3},{2,6},{3,1},{4,0},{5,7},{6,2},{7,5},{8,12},{9,11},{10,... | collective-permute-start | bytes 2359304 | tf_op jit(solution)/shard_map/ppermute | solution.py:666
  255.5 13.5 %collective-permute-start.48 = (bf16[192,1536]{1,0:T(8,128)(2,1)}, bf16[192,1536]{1,0:T(8,128)(2,1)}, u32[]{:S(2)}, u32[]{:S(2)}) collective-permute-start(bf16[192,1536]{1,0:T(8,128)(2,1)} %join.3.refs_4_.refs_1_), channel_id=1, source_target_pairs={{0,2},{1,5},{2,0},{3,7},{4,6},{5,1},{6,4},{7,3},{8,10},{9,13},{10,... | collective-permute-start | bytes 1769480 | tf_op jit(solution)/shard_map/ppermute | solution.py:666
  261.2 20.8 %collective-permute-start.49 = (bf16[192,1536]{1,0:T(8,128)(2,1)}, bf16[192,1536]{1,0:T(8,128)(2,1)}, u32[]{:S(2)}, u32[]{:S(2)}) collective-permute-start(bf16[192,1536]{1,0:T(8,128)(2,1)} %collective-permute-done.47.refs_2_), channel_id=1, source_target_pairs={{0,2},{1,5},{2,0},{3,7},{4,6},{5,1},{6,4},{7,3},{8,10},{9,13},{10,... | collective-permute-start | bytes 1769480 | tf_op jit(solution)/shard_map/ppermute | solution.py:666
  267.2 14.1 %collective-permute-start.34 = (bf16[192,1152]{1,0:T(8,128)(2,1)}, bf16[192,1152]{1,0:T(8,128)(2,1)S(1)}, u32[]{:S(2)}, u32[]{:S(2)}) collective-permute-start(bf16[192,1152]{1,0:T(8,128)(2,1)} %join.5.refs_9_.refs_1_), channel_id=1, source_target_pairs={{0,2},{1,5},{2,0},{3,7},{4,6},{5,1},{6,4},{7,3},{8,10},{9,13},{10,... | collective-permute-start | bytes 1327112 | tf_op jit(solution)/shard_map/ppermute | solution.py:666
  268.6 13.4 %collective-permute-start.33 = (bf16[192,1152]{1,0:T(8,128)(2,1)}, bf16[192,1152]{1,0:T(8,128)(2,1)}, u32[]{:S(2)}, u32[]{:S(2)}) collective-permute-start(bf16[192,1152]{1,0:T(8,128)(2,1)} %join.5.refs_9_.refs_1_), channel_id=1, source_target_pairs={{0,4},{1,3},{2,6},{3,1},{4,0},{5,7},{6,2},{7,5},{8,12},{9,11},{10,... | collective-permute-start | bytes 1327112 | tf_op jit(solution)/shard_map/ppermute | solution.py:666
  269.0 20.9 %collective-permute-start.41 = (bf16[192,2048]{1,0:T(8,128)(2,1)S(1)}, bf16[192,2048]{1,0:T(8,128)(2,1)}, u32[]{:S(2)}, u32[]{:S(2)}) collective-permute-start(bf16[192,2048]{1,0:T(8,128)(2,1)S(1)} %copy-done.2), channel_id=1, source_target_pairs={{0,2},{1,5},{2,0},{3,7},{4,6},{5,1},{6,4},{7,3},{8,10},{9,13},{10,... | collective-permute-start | bytes 2359304 | tf_op jit(solution)/shard_map/ppermute | solution.py:666
  269.9 28.4 %collective-permute-start.42 = (bf16[192,2048]{1,0:T(8,128)(2,1)}, bf16[192,2048]{1,0:T(8,128)(2,1)}, u32[]{:S(2)}, u32[]{:S(2)}) collective-permute-start(bf16[192,2048]{1,0:T(8,128)(2,1)} %collective-permute-done.40.refs_2_), channel_id=1, source_target_pairs={{0,2},{1,5},{2,0},{3,7},{4,6},{5,1},{6,4},{7,3},{8,10},{9,13},{10,... | collective-permute-start | bytes 2359304 | tf_op jit(solution)/shard_map/ppermute | solution.py:666
  289.9 16.0 %collective-permute-start.43 = (bf16[192,2048]{1,0:T(8,128)(2,1)S(1)}, bf16[192,2048]{1,0:T(8,128)(2,1)}, u32[]{:S(2)}, u32[]{:S(2)}) collective-permute-start(bf16[192,2048]{1,0:T(8,128)(2,1)S(1)} %copy-done.2), channel_id=1, source_target_pairs={{0,1},{1,0},{2,3},{3,2},{4,5},{5,4},{6,7},{7,6},{8,9},{9,8},{10,11... | collective-permute-start | bytes 2359304 | tf_op jit(solution)/shard_map/ppermute | solution.py:666
  289.9 16.5 %collective-permute-start.35 = (bf16[192,1152]{1,0:T(8,128)(2,1)}, bf16[192,1152]{1,0:T(8,128)(2,1)}, u32[]{:S(2)}, u32[]{:S(2)}) collective-permute-start(bf16[192,1152]{1,0:T(8,128)(2,1)} %collective-permute-done.33.refs_2_), channel_id=1, source_target_pairs={{0,2},{1,5},{2,0},{3,7},{4,6},{5,1},{6,4},{7,3},{8,10},{9,13},{10,... | collective-permute-start | bytes 1327112 | tf_op jit(solution)/shard_map/ppermute | solution.py:666
  291.6 15.4 %collective-permute-start.44 = (bf16[192,2048]{1,0:T(8,128)(2,1)}, bf16[192,2048]{1,0:T(8,128)(2,1)}, u32[]{:S(2)}, u32[]{:S(2)}) collective-permute-start(bf16[192,2048]{1,0:T(8,128)(2,1)} %collective-permute-done.40.refs_2_), channel_id=1, source_target_pairs={{0,1},{1,0},{2,3},{3,2},{4,5},{5,4},{6,7},{7,6},{8,9},{9,8},{10,11... | collective-permute-start | bytes 2359304 | tf_op jit(solution)/shard_map/ppermute | solution.py:666
  291.6 14.9 %collective-permute-start.45 = (bf16[192,2048]{1,0:T(8,128)(2,1)}, bf16[192,2048]{1,0:T(8,128)(2,1)}, u32[]{:S(2)}, u32[]{:S(2)}) collective-permute-start(bf16[192,2048]{1,0:T(8,128)(2,1)} %collective-permute-done.41.refs_3_), channel_id=1, source_target_pairs={{0,1},{1,0},{2,3},{3,2},{4,5},{5,4},{6,7},{7,6},{8,9},{9,8},{10,11... | collective-permute-start | bytes 2359304 | tf_op jit(solution)/shard_map/ppermute | solution.py:666
  (44 other events, 313.6 us)

commit v3 on v2

--- a/solution.py
+++ b/solution.py
@@ -109,6 +109,11 @@
 
 def with_ones(v):
     return jnp.concatenate([v, jnp.ones_like(v)], axis=1)
+
+
+def heads_apart(x, second):
+    zero = jnp.zeros_like(x)
+    return jnp.concatenate([jnp.where(second, zero, x), jnp.where(second, x, zero)], axis=0)
 
 
 def turn_state(state, angle, on):
@@ -168,16 +173,24 @@
 
 
 def rows_kernel(
-    angle, block, sc, tok, q_ref, k_ref, v_ref, pre, init, cos, sin, table, w_out, w_up, w_down, gains, biases, cot,
+    angle, block, sc, tok, q_ref, k_ref, v_ref, pre, init, cos, sin, table, w_out, w_up_hbm, w_down_hbm, gains, biases, cot,
     out_ref, dres_one_ref, dnum_ref, dden_ref, part_ref, tot_ref, one_own, one_other, two_own, two_first, two_second, two_rest,
-    mixed, hid, slope, dhid, acc_down, acc_up, acc_out, ng, stage, norm_stage, sems, norm_sems,
+    w_up, w_down, mixed, hid, slope, dhid, acc_down, acc_up, acc_out, ng, stage, norm_stage, sems, norm_sems, w_sems,
 ):
     core = sc[0]
     step = pl.program_id(0)
     first = step == 0
 
+    def weight_copies():
+        return (
+            pltpu.make_async_copy(w_up_hbm, w_up, w_sems.at[0]),
+            pltpu.make_async_copy(w_down_hbm, w_down, w_sems.at[1]),
+        )
+
     @pl.when(first)
     def _():
+        for copy in weight_copies():
+            copy.start()
         ng[...] = jnp.zeros_like(ng)
         tot_ref[...] = jnp.zeros_like(tot_ref)
 
@@ -190,11 +203,8 @@
         state = unpack_state(pre[0, p] + turn_state(init[p], angle, later))
         q, k, v = q_ref[:, cols], k_ref[:, cols], v_ref[:, cols]
         total = nn(features(q.astype(f32), cos[...], sin[...]), state)
-        v_ones = with_ones(v)
-        zero = jnp.zeros_like(q)
-        score_0 = (nt(jnp.where(second, zero, q), k) * table[...]).astype(bf16)
-        score_1 = (nt(jnp.where(second, q, zero), k) * table[...]).astype(bf16)
-        total += jnp.where(second2, nn(score_1, v_ones), nn(score_0, v_ones))
+        scores = (nt(q, heads_apart(k, second)) * table[...]).astype(bf16)
+        total += nn(scores, heads_apart(with_ones(v), second2))
         inv = 1.0 / total[:, PAIR:]
         inverse.append(inv)
         mixed[:, cols] = (total[:, :PAIR] * inv).astype(bf16)
@@ -202,7 +212,12 @@
     n0, rstd0 = norm_parts(z)
     normed = n0 * gains[0:1] + biases[0:1]
     low = normed.astype(bf16)
-    z = normed
+
+    @pl.when(first)
+    def _():
+        for copy in weight_copies():
+            copy.wait()
+
     for j in range(FF // D):
         cols = slice(j * D, (j + 1) * D)
         h = nn(low, w_up[:, cols])
@@ -280,7 +295,7 @@
         for i, (acc, owner, _, _, _, _, size) in enumerate(jobs):
             if i >= slots:
                 move(i - slots, lambda copy: copy.wait())
-            me = jnp.where(core == owner, sc[1], sc[2])
+            me = jnp.where(core == owner, sc[3 if i < 4 else 1], sc[4 if i < 4 else 2])
             for b in range(D // block):
                 to = pl.multiple_of((jnp.int32(b) ^ me) * block, block)
                 stage[i % slots, pl.ds(to, block), :size] = acc[b * block : (b + 1) * block, :].astype(bf16)
@@ -320,8 +335,8 @@
         scalars=1,
         grid=(steps,),
         in_specs=[
-            chunk, chunk, chunk, chunk, states, once(PAIRS, FEAT, PAIR), thin, thin, once(CHUNK, CHUNK),
-            once(D, D), once(D, FF), once(FF, D), once(2, D), once(2, D), chunk,
+            chunk, chunk, chunk, chunk, states, once(PAIRS, FEAT, PAIR), thin, thin, once(CHUNK, 2 * CHUNK),
+            once(D, D), ANY, ANY, once(2, D), once(2, D), chunk,
         ],
         out_specs=[chunk, chunk, chunk, chunk, states, whole(PAIRS, FEAT, PAIR)] + [ANY] * 6,
         out_shape=[
@@ -331,10 +346,11 @@
             make(HALF + PAIR, bf16, D),
         ],
         scratch_shapes=[
+            pltpu.VMEM((D, FF), bf16), pltpu.VMEM((FF, D), bf16),
             pltpu.VMEM((CHUNK, D), bf16), pltpu.VMEM((CHUNK, FF), bf16), pltpu.VMEM((CHUNK, FF), f32),
             pltpu.VMEM((CHUNK, FF), bf16), pltpu.VMEM((FF, D), f32), pltpu.VMEM((D, FF), f32), pltpu.VMEM((D, D), f32),
             pltpu.VMEM((4, D), f32), pltpu.VMEM((3, D, D), bf16), pltpu.VMEM((2, D, PAIR), bf16),
-            pltpu.SemaphoreType.DMA((3,)), pltpu.SemaphoreType.DMA((2,)),
+            pltpu.SemaphoreType.DMA((3,)), pltpu.SemaphoreType.DMA((2,)), pltpu.SemaphoreType.DMA((2,)),
         ],
     )(sc, tokens, q, k, v, pre, init, cos, sin, table, w_out, w_up, w_down, gains, biases, cot)
 
@@ -361,10 +377,6 @@
 
     second = lane_head(CHUNK) == 1
     second2 = jnp.concatenate([second, second], axis=1)
-
-    def split(x, mask):
-        zero = jnp.zeros_like(x)
-        return jnp.where(mask, zero, x), jnp.where(mask, x, zero)
 
     for p in range(pairs):
         cols = slice(p * PAIR, (p + 1) * PAIR)
@@ -381,13 +393,13 @@
         dv = nn(features(k_wide, cos[...], sin[...]), d_state[:, :PAIR])
         dq = dq_feat[:, :PAIR] * cos[...] + dq_feat[:, PAIR:] * sin[...]
         dk = dk_feat[:, :PAIR] * cos[...] + dk_feat[:, PAIR:] * sin[...]
-        for grad_h, q_h, k_h, dnum_h in zip(split(grad, second2), split(q, second), split(k, second), split(dnum, second)):
-            d_score = (nt(grad_h, v_ones) * table[...]).astype(bf16)
-            dq += nn(d_score, k_h)
-            score_t = (nt(k_h, q) * table_t[...]).astype(bf16)
-            d_score_t = (nt(v_ones, grad_h) * table_t[...]).astype(bf16)
-            dk += nn(d_score_t, q_h)
-            dv += nn(score_t, dnum_h)
+        q_apart, k_apart = heads_apart(q, second), heads_apart(k, second)
+        d_scores = (nt(grad, heads_apart(v_ones, second2)) * table[...]).astype(bf16)
+        dq += nn(d_scores, k_apart)
+        scores_t = (nt(k, q_apart) * table_t[...]).astype(bf16)
+        d_scores_t = (nt(v_ones, heads_apart(grad, second2)) * table_t[...]).astype(bf16)
+        dk += nn(d_scores_t, q_apart)
+        dv += nn(scores_t, heads_apart(dnum, second))
         out_ref[:, cols] = (dq.astype(bf16).astype(f32) * sigmoid_of(q_wide)).astype(bf16)
         out_ref[:, slice(HALF + p * PAIR, HALF + (p + 1) * PAIR)] = (
             dk.astype(bf16).astype(f32) * sigmoid_of(k_wide)
@@ -439,7 +451,7 @@
         grid=(steps,),
         in_specs=[
             by_chunk(D, last), chunk, chunk, chunk, chunk, chunk, states, state, states, state, thin, thin,
-            whole(CHUNK, CHUNK), whole(CHUNK, CHUNK),
+            whole(CHUNK, 2 * CHUNK), whole(CHUNK, 2 * CHUNK),
         ] + [whole(D, HALF)] * (3 * own),
         out_specs=[by_chunk(3 * HALF, last)] + ([whole(HALF, 3 * HALF)] * 2 if own else [whole(D, HALF)] * 3),
         out_shape=[make(rows)] + ([make(HALF)] * 2 if own else [jax.ShapeDtypeStruct((D, HALF), bf16)] * 3),
@@ -531,27 +543,33 @@
     return small_call(join_kernel, parts, len(parts) * parts[0].shape[0], "join", deps)
 
 
-def restore(me, block, quarters, put):
-    for place in range(D // block):
-        ref, at = quarters[place * block // QUARTER], place * block % QUARTER
-        put(pl.multiple_of((jnp.int32(place) ^ me) * block, block), ref[at : at + block, :].astype(f32))
-
-
-def gather_kernel(block, per_core, sc, *refs):
+def restore(me, block, quarters, put, along_z=False):
+    count = QUARTER // block
+    for i, ref in enumerate(quarters):
+        for j in range(count):
+            place = j * len(quarters) + i if along_z else i * count + j
+            put(
+                pl.multiple_of((jnp.int32(place) ^ me) * block, block),
+                ref[j * block : (j + 1) * block, :].astype(f32),
+            )
+
+
+def gather_kernel(block, by_rows, sc, *refs):
     mine, other, out = refs[:4], refs[4:8], refs[8]
+    own_me, other_me = (sc[3], sc[4]) if by_rows else (sc[1], sc[2])
 
     def put(row, piece):
         out[pl.ds(row, block), :] = piece
 
-    is_mine = pl.program_id(0) // per_core == sc[0]
+    is_mine = pl.program_id(0) // 2 == sc[0]
 
     @pl.when(is_mine)
     def _():
-        restore(sc[1], block, mine, put)
+        restore(own_me, block, mine, put, by_rows)
 
     @pl.when(jnp.logical_not(is_mine))
     def _():
-        restore(sc[2], block, other, put)
+        restore(other_me, block, other, put, by_rows)
 
 
 def gather_units(sc, parts, block, by_rows, deps=()):
@@ -562,7 +580,7 @@
         return pl.BlockSpec((QUARTER, D), index)
 
     return ordered_call(
-        functools.partial(gather_kernel, block, 2),
+        functools.partial(gather_kernel, block, by_rows),
         "gather_units",
         scalars=1,
         deps=deps,
@@ -652,8 +670,8 @@
 
 def make_local(n_dp, n_head):
     n_z = n_dp // 2
-    direct = QUARTER % (16 * n_z) == 0 and n_z & (n_z - 1) == 0
-    places = n_z if direct else 1
+    direct = n_z == 4
+    places = 4 if direct else 1
     block = QUARTER // places
     both_axes = ("dp", "head")
 
@@ -677,22 +695,32 @@
     def swap_z(x, k):
         return swap(x, lambda d, h: (d ^ (2 * k), h))
 
-    def cut_z(keep, got, deps=()):
-        if direct:
-            parts = add_cut(keep, got, n_z, deps)
-            return [parts[0]] + [swap_z(parts[i], i) for i in range(1, n_z)]
+    def sum_z(keep, got):
         both = keep.astype(f32) + got.astype(f32)
         same_z = [[2 * i + j for i in range(n_z)] for j in range(2)]
         return lax.psum(both, "dp", axis_index_groups=same_z).astype(bf16)
 
-    def share_z(parts, deps=()):
-        if not direct:
-            return parts
+    def cut_z(keep, got, deps=()):
+        parts = add_cut(keep, got, 4, deps)
+        return [parts[0], swap_z(parts[1], 2), swap_z(parts[2], 1), swap_z(parts[3], 3)]
+
+    def share_z(parts, deps=(), neighbours=False):
         share = add_all(parts, deps)
-        return [share] + [swap_z(share, i) for i in range(1, n_z)]
+        near, far = swap_z(share, 1), swap_z(share, 2)
+        return [share, far, near, swap_z(far, 1) if neighbours else swap_z(share, 3)]
+
+    def step(pair, swap_next, deps=()):
+        keep, send = add_cut(*pair, 2, deps)
+        return [keep, swap_next(send)]
+
+    def swap_near(x):
+        return swap_z(x, 1)
+
+    def swap_far(x):
+        return swap_z(x, 2)
 
     def spread(parts, deps=()):
-        own = join(parts, deps) if direct else parts
+        own = join(parts, deps) if direct else parts[0]
         second = swap_second(own)
         first = swap_first(own)
         both = swap_first(second)
@@ -704,15 +732,17 @@
         assert LENGTH == 2 * rows and n_head % 4 == 0 and n_dp % 2 == 0
         head, dp = lax.axis_index("head"), lax.axis_index("dp")
         core, x, y, z = head % 2, head // 2, dp % 2, dp // 2
-        rank = z if direct else 0
+        rank = z % 2 * 2 + z // 2 if direct else 0
         by_x, by_y = (2 * x + y) * places + rank, (2 * y + x) * places + rank
-        sc = jnp.stack([core, jnp.where(core == 0, by_x, by_y), jnp.where(core == 0, by_y, by_x)]).astype(jnp.int32)
+        z_x, z_y = (rank * 4 + 2 * x + y, rank * 4 + 2 * y + x) if direct else (by_x, by_y)
+        sc = jnp.stack([core, *(jnp.where(core == 0, *pair) for pair in ((by_x, by_y), (by_y, by_x), (z_x, z_y), (z_y, z_x)))])
+        sc = sc.astype(jnp.int32)
         angle = STEP_ANGLE * np.arange(rows)
         cos = jnp.asarray(np.broadcast_to(np.cos(angle)[:, None], (rows, PAIR)), f32)
         sin = jnp.asarray(np.broadcast_to(np.sin(angle)[:, None], (rows, PAIR)), f32)
         gap = np.arange(CHUNK)[:, None] - np.arange(CHUNK)[None, :]
         weights = np.where(gap >= 0, np.cos(STEP_ANGLE * gap), 0.0)
-        table, table_t = jnp.asarray(weights, f32), jnp.asarray(weights.T, f32)
+        table, table_t = (jnp.asarray(np.concatenate([w, w], axis=1), f32) for w in (weights, weights.T))
 
         q, k, v, pre, total = project(tokens, w_query, w_key, w_value, cos, sin)
         init = swap_core(total)
@@ -722,39 +752,42 @@
         one_got = swap_core(one_other)
         d_init = swap_core(d_total)
         two_got = [swap_core(x) for x in two_other]
-        one_keep, one_send = add_cut(one_own, one_got, 2)
-        one_got = swap_first(one_send)
+        along = (swap_near, swap_far, swap_first, swap_second) if direct else (swap_first, swap_second)
+        one = step([one_own, one_got], along[0])
         two_keep, two_send = small_call(
-            add_cut_parts_kernel, [two_own, *two_got], [HALF, HALF], "add_cut", deps=(one_keep,)
+            add_cut_parts_kernel, [two_own, *two_got], [HALF, HALF], "add_cut", deps=(one[0],)
         )
-        two_got = swap_first(two_send)
+        two = [two_keep, swap_first(two_send)]
         att = functools.partial(
             attend_back, sc, tokens, q, k, v, dnum, dden, pre, init, part, d_init, cos, sin, table, table_t, block
         )
         d_other, *three_other = att(deps=(two_keep,))
         three_got = [swap_core(x) for x in three_other]
-        one_keep, one_send = add_cut(one_keep, one_got, 2, deps=(d_other,))
-        one_got = swap_second(one_send)
-        two_keep, two_send = add_cut(two_keep, two_got, 2, deps=(one_keep,))
-        two_got = swap_second(two_send)
-        d_own, three_keep, three_send = att(three_got, deps=(two_keep,))
-        three_got = swap_first(three_send)
-        one_parts = cut_z(one_keep, one_got, deps=(three_keep,))
-        two_parts = cut_z(two_keep, two_got, deps=(one_parts[0],))
-        d_tokens = token_grad(sc, dres_one, d_other, d_own, w_query, w_key, w_value, deps=(two_parts[0],))
-        three_keep, three_send = add_cut(three_keep, three_got, 2, deps=(d_tokens,))
-        three_got = swap_second(three_send)
-        one_parts = share_z(one_parts, deps=(three_keep,))
-        three_parts = cut_z(three_keep, three_got, deps=(one_parts[0],))
-        two_parts = share_z(two_parts, deps=(three_parts[0],))
-        one_parts = spread(one_parts, deps=(two_parts[0],))
-        three_parts = share_z(three_parts, deps=(one_parts[0],))
-        two_parts = spread(two_parts, deps=(three_parts[0],))
-        three_parts = spread(three_parts, deps=(two_parts[0],))
-        grad_down = gather_units(sc, one_parts, block, True, deps=(three_parts[0],))
-        grad_up = gather_units(sc, two_parts, block, False, deps=(grad_down,))
-        grad_out, grad_gains, grad_biases = gather_rest(sc, two_parts, block, deps=(grad_up,))
-        grad_qkv = gather_qkv(sc, three_parts, block, deps=(grad_out,))
+        one = step(one, along[1], deps=(d_other,))
+        two = step(two, swap_second, deps=(one[0],))
+        d_own, three_keep, three_send = att(three_got, deps=(two[0],))
+        three = [three_keep, swap_first(three_send)]
+        if direct:
+            one = step(one, swap_first, deps=(three_keep,))
+            two = step(two, swap_near, deps=(one[0],))
+            one = step(one, swap_second, deps=(two[0],))
+            three = step(three, swap_second, deps=(one[0],))
+            two = step(two, swap_far, deps=(three[0],))
+            one = share_z(one, deps=(two[0],))
+            three = cut_z(*three, deps=(one[0],))
+            two = share_z(two, deps=(three[0],), neighbours=True)
+            one = spread(one, deps=(two[0],))
+            three = share_z(three, deps=(one[0],))
+            two = spread(two, deps=(three[0],))
+        else:
+            three = step(three, swap_second)
+            one, two, three = spread([sum_z(*one)]), spread([sum_z(*two)]), [sum_z(*three)]
+        d_tokens = token_grad(sc, dres_one, d_other, d_own, w_query, w_key, w_value, deps=(two[0],))
+        three = spread(three, deps=(d_tokens,))
+        grad_down = gather_units(sc, one, block, True, deps=(three[0],))
+        grad_up = gather_units(sc, two, block, False, deps=(grad_down,))
+        grad_out, grad_gains, grad_biases = gather_rest(sc, two, block, deps=(grad_up,))
+        grad_qkv = gather_qkv(sc, three, block, deps=(grad_out,))
         return out, d_tokens, *grad_qkv, grad_out, grad_up, grad_down, grad_gains, grad_biases
 
     return local

time: 328 us -> 299 us (0.912)
  starting transfers between devices: 72.6 us -> 45.7 us
  waiting for transfers between devices: 58.9 us -> 63.7 us
  Pallas kernels: 185 us -> 181 us
    ppermute x54 -> x52, starting transfers between devices: 72.6 us -> 45.7 us  [swap(): return lax.ppermute(x, both_axes, pairs)]
    ppermute x54 -> x52, waiting for transfers between devices: 58.9 us -> 63.7 us  [swap(): return lax.ppermute(x, both_axes, pairs)]
    pallas_call x23 -> x25, Pallas kernels: 185 us -> 181 us  [ordered_call(): return lambda *args: call(*args, *deps)]
    unnamed x44 -> x46, local copies, waits for them, and re-layouts: 7.26 us -> 6.76 us
  transfers between devices with their start and end apart: 54 -> 52, of which waited for: 14 -> 16; matrix products, arithmetic and copies ran while one was open for 0% -> 0% of each run, Pallas kernels for 31% -> 34%
where the time goes in v3:
time: 299 us; the launch traced here: 298 us
  Pallas kernels  181 us (61%)
  waiting for transfers between devices  63.7 us (21%)
  starting transfers between devices  45.7 us (15%)
  local copies, waits for them, and re-layouts  7.42 us (2%)
    pallas_call x25, Pallas kernels, ordered_call(): return lambda *args: call(*args, *deps)  181 us
    ppermute x52, waiting for transfers between devices, swap(): return lax.ppermute(x, both_axes, pairs)  63.7 us
    ppermute x52, starting transfers between devices, swap(): return lax.ppermute(x, both_axes, pairs)  45.7 us
    unnamed x46, local copies, waits for them, and re-layouts  6.76 us
  transfers between devices with their start and end apart: 52, of which 16 were waited for; matrix products, arithmetic and copies ran while one was open for 0% of the time, Pallas kernels for 34%

profile of v3, /device:TPU:0, one launch (start us, length us, event | category | flops | bytes accessed | tf_op | source)
XLA Modules:
  0.0 298.3 jit_solution(5356846674156767013)
XLA Ops:
  0.6 11.0 %project.1 = (bf16[1024,768]{1,0:T(8,128)(2,1)}, bf16[1024,768]{1,0:T(8,128)(2,1)}, bf16[1024,768]{1,0:T(8,128)(2,1)}, f32[4,6,256,128]{3,2,1,0:T(8,128)}, f32[6,256,128]{2,1,0:T(8,128)}) custom-call(bf16[1024,768]{1,0:T(8,128)(2,1)} %refs_1_.7, bf16[768,768]{1,0:T(8,128)(2,1)} %refs_7_.2, bf16[768,768]{1,0:T(8,128)(2,1)} %refs_8_.2, ...), custom_call_target="tpu_custom_call" | custom-call | flops 12650000384 | bytes 1 | tf_op jit(solution)/shard_map/project/pallas_call | solution.py:71
  15.2 61.9 %rows.1 = (bf16[1024,768]{1,0:T(8,128)(2,1)}, f32[1024,768]{1,0:T(8,128)}, bf16[1024,768]{1,0:T(8,128)(2,1)}, bf16[1024,768]{1,0:T(8,128)(2,1)}, f32[4,6,256,128...) custom-call(s32[5]{0:T(128)} %stack.23.refs_0_, ...), custom_call_target="tpu_custom_call" | custom-call | flops 69000003584 | bytes 1 | tf_op jit(solution)/shard_map/rows/pallas_call | solution.py:71
  78.6 3.5 %collective-permute-done.5.refs_1_ = bf16[768,1536]{1,0:T(8,128)(2,1)} collective-permute-done((bf16[768,1536]{1,0:T(8,128)(2,1)}, bf16[768,1536]{1,0:T(8,128)(2,1)}, u32[]{:S(2)}, u32[]{:S(2)}) %collective-permute-start.5) | collective-permute-done | bytes 2359328 | tf_op jit(solution)/shard_map/ppermute | solution.py:684
  82.1 4.1 %add_cut.10 = (bf16[384,1536]{1,0:T(8,128)(2,1)}, bf16[384,1536]{1,0:T(8,128)(2,1)}) custom-call(bf16[768,1536]{1,0:T(8,128)(2,1)} %get-tuple-element.77.refs_0_, bf16[768,1536]{1,0:T(8,128)(2,1)} %collective-permute-done.5.refs_1_), custom_call_target="tpu_custom_call" | custom-call | flops 2875000064 | bytes 1 | tf_op jit(solution)/shard_map/add_cut/pallas_call | solution.py:71
  86.2 2.9 collective-permute-start.10
  89.1 5.1 %add_cut.11 = (bf16[384,2048]{1,0:T(8,128)(2,1)}, bf16[384,2048]{1,0:T(8,128)(2,1)}) custom-call(bf16[768,2048]{1,0:T(8,128)(2,1)} %get-tuple-element.73.refs_0_, bf16[768,768]{1,0:T(8,128)(2,1)} %collective-permute-done.2.refs_1_, bf16[768,768]{1,0:T(8,128)(2,1)} %collective-permute-done.3.refs_2_, bf16[768,512]{1,0:T(8,128)(2,1)} %collective-permute-done.4.refs_3_, ...), custom_call_target="tpu_custom_call" | custom-call | flops 2875000064 | bytes 1 | tf_op jit(solution)/shard_map/add_cut/pallas_call | solution.py:71
  96.6 16.2 %attend_back.2 = (bf16[1024,1152]{1,0:T(8,128)(2,1)}, bf16[768,384]{1,0:T(8,128)(2,1)}, bf16[768,384]{1,0:T(8,128)(2,1)}, bf16[768,384]{1,0:T(8,128)(2,1)}) custom-call(s32[5]{0:T(128)} %stack.23.refs_0_, bf16[1024,768]{1,0:T(8,128)(2,1)} %refs_1_.7, bf16[1024,768]{1,0:T(8,128)(2,1)} %get-tuple-element.62.refs_2_, ...), custom_call_target="tpu_custom_call" | custom-call | flops 21849999360 | bytes 1 | tf_op jit(solution)/shard_map/attend_back/pallas_call | solution.py:71
  113.5 2.3 collective-permute-done.10.refs_1_
  115.7 2.8 add_cut.12
  118.5 2.7 collective-permute-start.12
  121.3 3.2 %add_cut.13 = (bf16[192,2048]{1,0:T(8,128)(2,1)}, bf16[192,2048]{1,0:T(8,128)(2,1)}) custom-call(bf16[384,2048]{1,0:T(8,128)(2,1)} %get-tuple-element.80.refs_15_.refs_0_, bf16[384,2048]{1,0:T(8,128)(2,1)} %collective-permute-done.9.refs_1_, bf16[192,1536]{1,0:T(8,128)(2,1)} %get-tuple-element.87.refs_2_.refs_0_), custom_call_target="tpu_custom_call" | custom-call | flops 2875000064 | bytes 1 | tf_op jit(solution)/shard_map/add_cut/pallas_call | solution.py:71
  126.8 17.3 %attend_back.3 = (bf16[1024,1152]{1,0:T(8,128)(2,1)}, bf16[384,1152]{1,0:T(8,128)(2,1)}, bf16[384,1152]{1,0:T(8,128)(2,1)}) custom-call(s32[5]{0:T(128)} %stack.23.refs_0_, bf16[1024,768]{1,0:T(8,128)(2,1)} %refs_1_.7, bf16[1024,768]{1,0:T(8,128)(2,1)} %get-tuple-element.62.refs_2_, bf16[1024,768]{1,0:T(8,128)(2,1)} %get-tuple-element.63.refs_3_, ...), custom_call_target="tpu_custom_call" | custom-call | flops 21849999360 | bytes 1 | tf_op jit(solution)/shard_map/attend_back/pallas_call | solution.py:71
  147.3 2.1 add_cut.14
  150.7 2.3 add_cut.15
  153.7 7.0 %collective-permute-done.15.refs_1_ = bf16[96,1536]{1,0:T(8,128)(2,1)} collective-permute-done((bf16[96,1536]{1,0:T(8,128)(2,1)}, bf16[96,1536]{1,0:T(8,128)(2,1)}, u32[]{:S(2)}, u32[]{:S(2)}) %collective-permute-start.15) | collective-permute-done | bytes 294944 | tf_op jit(solution)/shard_map/ppermute | solution.py:684
  164.0 2.4 add_cut.17
  173.1 2.8 collective-permute-start.25
  178.8 2.8 collective-permute-start.22
  181.6 15.8 %collective-permute-done.16.refs_1_ = bf16[48,2048]{1,0:T(8,128)(2,1)S(1)} collective-permute-done((bf16[48,2048]{1,0:T(8,128)(2,1)S(1)}, bf16[48,2048]{1,0:T(8,128)(2,1)S(1)}, u32[]{:S(2)}, u32[]{:S(2)}) %collective-permute-start.16) | collective-permute-done | bytes 196640 | tf_op jit(solution)/shard_map/ppermute | solution.py:684
  201.5 2.8 collective-permute-start.19
  209.8 3.8 %collective-permute-done.19.refs_1_ = bf16[48,2048]{1,0:T(8,128)(2,1)S(1)} collective-permute-done((bf16[48,2048]{1,0:T(8,128)(2,1)}, bf16[48,2048]{1,0:T(8,128)(2,1)S(1)}, u32[]{:S(2)}, u32[]{:S(2)}) %collective-permute-start.19) | collective-permute-done | bytes 196640 | tf_op jit(solution)/shard_map/ppermute | solution.py:684
  215.4 2.9 collective-permute-start.30
  221.1 2.1 join.4.refs_10_.refs_1_
  226.3 2.2 collective-permute-start.38
  228.5 10.4 %token_grad.1.refs_4_ = f32[1024,768]{1,0:T(8,128)} custom-call(s32[5]{0:T(128)} %stack.23.refs_0_, f32[1024,768]{1,0:T(8,128)} %get-tuple-element.68.refs_1_, bf16[1024,1152]{1,0:T(8,128)(2,1)} %get-tuple-element.81.refs_2_, bf16[1024,1152]{1,0:T(8,128)(2,1)} %get-tuple-element.89.refs_3_, bf16[768,768]{1,0:T(8,128)(2,1)} %refs_7_.2, ...), custom_call_target="tpu_custom_call" | custom-call | flops 11500000256 | bytes 1 | tf_op jit(solution)/shard_map/token_grad/pallas_call | solution.py:71
  245.5 8.9 %collective-permute-done.32.refs_3_ = bf16[192,1152]{1,0:T(8,128)(2,1)} collective-permute-done((bf16[192,1152]{1,0:T(8,128)(2,1)}, bf16[192,1152]{1,0:T(8,128)(2,1)}, u32[]{:S(2)}, u32[]{:S(2)}) %collective-permute-start.32) | collective-permute-done | bytes 442400 | tf_op jit(solution)/shard_map/ppermute | solution.py:684
  258.6 4.3 %collective-permute-done.39.refs_3_ = bf16[192,2048]{1,0:T(8,128)(2,1)} collective-permute-done((bf16[192,2048]{1,0:T(8,128)(2,1)S(1)}, bf16[192,2048]{1,0:T(8,128)(2,1)}, u32[]{:S(2)}, u32[]{:S(2)}) %collective-permute-start.39) | collective-permute-done | bytes 786464 | tf_op jit(solution)/shard_map/ppermute | solution.py:684
  264.2 7.1 %collective-permute-done.40.refs_4_ = bf16[192,2048]{1,0:T(8,128)(2,1)} collective-permute-done((bf16[192,2048]{1,0:T(8,128)(2,1)}, bf16[192,2048]{1,0:T(8,128)(2,1)}, u32[]{:S(2)}, u32[]{:S(2)}) %collective-permute-start.40) | collective-permute-done | bytes 786464 | tf_op jit(solution)/shard_map/ppermute | solution.py:684
  271.5 7.5 %gather_units.2.refs_9_ = f32[3072,768]{1,0:T(8,128)} custom-call(s32[5]{0:T(128)} %stack.23.refs_0_, bf16[192,1536]{1,0:T(8,128)(2,1)} %join.3.refs_4_.refs_1_, bf16[192,1536]{1,0:T(8,128)(2,1)} %collective-permute-done.45.refs_2_, bf16[192,1536]{1,0:T(8,128)(2,1)} %collective-permute-done.46.refs_3_, bf16[192,1536]{1,0:T(8,128)(2,1)} %collective-permute-done.47.refs_4_, ...), custom_call_target="tpu_custom_call" | custom-call | flops 9200000000 | bytes 1 | tf_op jit(solution)/shard_map/gather_units/pallas_call | solution.py:71
  280.2 7.6 %gather_units.3.refs_9_ = f32[768,3072]{1,0:T(8,128)} custom-call(s32[5]{0:T(128)} %stack.23.refs_0_, bf16[192,2048]{1,0:T(8,128)(2,1)} %join.4.refs_10_.refs_1_, bf16[192,2048]{1,0:T(8,128)(2,1)} %collective-permute-done.38.refs_2_, bf16[192,2048]{1,0:T(8,128)(2,1)} %collective-permute-done.39.refs_3_, bf16[192,2048]{1,0:T(8,128)(2,1)} %collective-permute-done.40.refs_4_, ...), custom_call_target="tpu_custom_call" | custom-call | flops 9200000000 | bytes 1 | tf_op jit(solution)/shard_map/gather_units/pallas_call | solution.py:71
  287.7 3.7 %gather_rest.1 = (f32[768,768]{1,0:T(8,128)}, f32[2,768]{1,0:T(2,128)}, f32[2,768]{1,0:T(2,128)}) custom-call(s32[5]{0:T(128)} %stack.23.refs_0_, bf16[192,2048]{1,0:T(8,128)(2,1)} %join.4.refs_10_.refs_1_, bf16[192,2048]{1,0:T(8,128)(2,1)} %collective-permute-done.38.refs_2_, bf16[192,2048]{1,0:T(8,128)(2,1)} %collective-permute-done.39.refs_3_, ...), custom_call_target="tpu_custom_call" | custom-call | flops 4600000000 | bytes 1 | tf_op jit(solution)/shard_map/gather_rest/pallas_call | solution.py:71
  292.5 5.9 %gather_qkv.1 = (f32[768,768]{1,0:T(8,128)}, f32[768,768]{1,0:T(8,128)}, f32[768,768]{1,0:T(8,128)}) custom-call(s32[5]{0:T(128)} %stack.23.refs_0_, bf16[192,1152]{1,0:T(8,128)(2,1)} %join.5.refs_9_.refs_1_, bf16[192,1152]{1,0:T(8,128)(2,1)} %collective-permute-done.31.refs_2_, bf16[192,1152]{1,0:T(8,128)(2,1)} %collective-permute-done.32.refs_3_, ...), custom_call_target="tpu_custom_call" | custom-call | flops 6325000192 | bytes 1 | tf_op jit(solution)/shard_map/gather_qkv/pallas_call | solution.py:71
  (144 shorter events, 60.0 us)
Async XLA Ops:
  78.2 17.5 %collective-permute-start.1 = (f32[6,256,128]{2,1,0:T(8,128)}, f32[6,256,128]{2,1,0:T(8,128)S(1)}, u32[]{:S(2)}, u32[]{:S(2)}) collective-permute-start(f32[6,256,128]{2,1,0:T(8,128)} %get-tuple-element.72), channel_id=1, source_target_pairs={{0,1},{1,0},{2,3},{3,2},{4,5},{5,4},{6,7},{7,6},{8,9},{9,8},{10,11... | collective-permute-start | bytes 2359304 | tf_op jit(solution)/shard_map/ppermute | solution.py:684
  86.2 29.5 %collective-permute-start.10 = (bf16[384,1536]{1,0:T(8,128)(2,1)}, bf16[384,1536]{1,0:T(8,128)(2,1)}, u32[]{:S(2)}, u32[]{:S(2)}) collective-permute-start(bf16[384,1536]{1,0:T(8,128)(2,1)} %get-tuple-element.86), channel_id=1, source_target_pairs={{0,8},{1,9},{2,10},{3,11},{4,12},{5,13},{6,14},{7,15},{8,0},{9,1},... | collective-permute-start | bytes 3538952 | tf_op jit(solution)/shard_map/ppermute | solution.py:684
  94.2 27.0 %collective-permute-start.9 = (bf16[384,2048]{1,0:T(8,128)(2,1)}, bf16[384,2048]{1,0:T(8,128)(2,1)}, u32[]{:S(2)}, u32[]{:S(2)}) collective-permute-start(bf16[384,2048]{1,0:T(8,128)(2,1)} %get-tuple-element.85), channel_id=1, source_target_pairs={{0,2},{1,5},{2,0},{3,7},{4,6},{5,1},{6,4},{7,3},{8,10},{9,13},{10,... | collective-permute-start | bytes 4718600 | tf_op jit(solution)/shard_map/ppermute | solution.py:684
  112.8 13.2 %collective-permute-start.6 = (bf16[768,384]{1,0:T(8,128)(2,1)}, bf16[768,384]{1,0:T(8,128)(2,1)S(1)}, u32[]{:S(2)}, u32[]{:S(2)}) collective-permute-start(bf16[768,384]{1,0:T(8,128)(2,1)} %get-tuple-element.82), channel_id=1, source_target_pairs={{0,1},{1,0},{2,3},{3,2},{4,5},{5,4},{6,7},{7,6},{8,9},{9,8},{10,11... | collective-permute-start | bytes 1769480 | tf_op jit(solution)/shard_map/ppermute | solution.py:684
  112.9 13.1 %collective-permute-start.7 = (bf16[768,384]{1,0:T(8,128)(2,1)}, bf16[768,384]{1,0:T(8,128)(2,1)}, u32[]{:S(2)}, u32[]{:S(2)}) collective-permute-start(bf16[768,384]{1,0:T(8,128)(2,1)} %get-tuple-element.83), channel_id=1, source_target_pairs={{0,1},{1,0},{2,3},{3,2},{4,5},{5,4},{6,7},{7,6},{8,9},{9,8},{10,11... | collective-permute-start | bytes 1769480 | tf_op jit(solution)/shard_map/ppermute | solution.py:684
  113.4 12.6 %collective-permute-start.8 = (bf16[768,384]{1,0:T(8,128)(2,1)}, bf16[768,384]{1,0:T(8,128)(2,1)}, u32[]{:S(2)}, u32[]{:S(2)}) collective-permute-start(bf16[768,384]{1,0:T(8,128)(2,1)} %get-tuple-element.84), channel_id=1, source_target_pairs={{0,1},{1,0},{2,3},{3,2},{4,5},{5,4},{6,7},{7,6},{8,9},{9,8},{10,11... | collective-permute-start | bytes 1769480 | tf_op jit(solution)/shard_map/ppermute | solution.py:684
  118.5 28.8 %collective-permute-start.12 = (bf16[192,1536]{1,0:T(8,128)(2,1)}, bf16[192,1536]{1,0:T(8,128)(2,1)}, u32[]{:S(2)}, u32[]{:S(2)}) collective-permute-start(bf16[192,1536]{1,0:T(8,128)(2,1)} %get-tuple-element.91), channel_id=1, source_target_pairs={{0,16},{1,17},{2,18},{3,19},{4,20},{5,21},{6,22},{7,23},{8,24},{9,... | collective-permute-start | bytes 1769480 | tf_op jit(solution)/shard_map/ppermute | solution.py:684
  124.5 26.3 %collective-permute-start.11 = (bf16[192,2048]{1,0:T(8,128)(2,1)}, bf16[192,2048]{1,0:T(8,128)(2,1)}, u32[]{:S(2)}, u32[]{:S(2)}) collective-permute-start(bf16[192,2048]{1,0:T(8,128)(2,1)} %get-tuple-element.90), channel_id=1, source_target_pairs={{0,4},{1,3},{2,6},{3,1},{4,0},{5,7},{6,2},{7,5},{8,12},{9,11},{10,... | collective-permute-start | bytes 2359304 | tf_op jit(solution)/shard_map/ppermute | solution.py:684
  144.2 18.9 %collective-permute-start.14 = (bf16[384,1152]{1,0:T(8,128)(2,1)}, bf16[384,1152]{1,0:T(8,128)(2,1)S(1)}, u32[]{:S(2)}, u32[]{:S(2)}) collective-permute-start(bf16[384,1152]{1,0:T(8,128)(2,1)} %get-tuple-element.96), channel_id=1, source_target_pairs={{0,2},{1,5},{2,0},{3,7},{4,6},{5,1},{6,4},{7,3},{8,10},{9,13},{10,... | collective-permute-start | bytes 2654216 | tf_op jit(solution)/shard_map/ppermute | solution.py:684
  153.1 14.9 %collective-permute-start.13 = (bf16[96,2048]{1,0:T(8,128)(2,1)}, bf16[96,2048]{1,0:T(8,128)(2,1)}, u32[]{:S(2)}, u32[]{:S(2)}) collective-permute-start(bf16[96,2048]{1,0:T(8,128)(2,1)} %get-tuple-element.95), channel_id=1, source_target_pairs={{0,8},{1,9},{2,10},{3,11},{4,12},{5,13},{6,14},{7,15},{8,0},{9,1},... | collective-permute-start | bytes 1179656 | tf_op jit(solution)/shard_map/ppermute | solution.py:684
  171.6 28.3 %collective-permute-start.27 = (bf16[48,1536]{1,0:T(8,128)(2,1)}, bf16[48,1536]{1,0:T(8,128)(2,1)S(1)}, u32[]{:S(2)}, u32[]{:S(2)}) collective-permute-start(bf16[48,1536]{1,0:T(8,128)(2,1)} %add_all.3.refs_2_.refs_0_), channel_id=1, source_target_pairs={{0,24},{1,25},{2,26},{3,27},{4,28},{5,29},{6,30},{7,31},{8,16},{9,... | collective-permute-start | bytes 442376 | tf_op jit(solution)/shard_map/ppermute | solution.py:684
  172.9 28.2 %collective-permute-start.26 = (bf16[48,1536]{1,0:T(8,128)(2,1)}, bf16[48,1536]{1,0:T(8,128)(2,1)}, u32[]{:S(2)}, u32[]{:S(2)}) collective-permute-start(bf16[48,1536]{1,0:T(8,128)(2,1)} %add_all.3.refs_2_.refs_0_), channel_id=1, source_target_pairs={{0,8},{1,9},{2,10},{3,11},{4,12},{5,13},{6,14},{7,15},{8,0},{9,1},... | collective-permute-start | bytes 442376 | tf_op jit(solution)/shard_map/ppermute | solution.py:684
  173.1 28.4 %collective-permute-start.25 = (bf16[48,1536]{1,0:T(8,128)(2,1)}, bf16[48,1536]{1,0:T(8,128)(2,1)}, u32[]{:S(2)}, u32[]{:S(2)}) collective-permute-start(bf16[48,1536]{1,0:T(8,128)(2,1)} %add_all.3.refs_2_.refs_0_), channel_id=1, source_target_pairs={{0,16},{1,17},{2,18},{3,19},{4,20},{5,21},{6,22},{7,23},{8,24},{9,... | collective-permute-start | bytes 442376 | tf_op jit(solution)/shard_map/ppermute | solution.py:684
  176.0 21.4 %collective-permute-start.16 = (bf16[48,2048]{1,0:T(8,128)(2,1)S(1)}, bf16[48,2048]{1,0:T(8,128)(2,1)S(1)}, u32[]{:S(2)}, u32[]{:S(2)}) collective-permute-start(bf16[48,2048]{1,0:T(8,128)(2,1)S(1)} %copy-done.13), channel_id=1, source_target_pairs={{0,16},{1,17},{2,18},{3,19},{4,20},{5,21},{6,22},{7,23},{8,24},{9,... | collective-permute-start | bytes 589832 | tf_op jit(solution)/shard_map/ppermute | solution.py:684
  178.8 27.5 %collective-permute-start.22 = (bf16[48,1152]{1,0:T(8,128)(2,1)}, bf16[48,1152]{1,0:T(8,128)(2,1)}, u32[]{:S(2)}, u32[]{:S(2)}) collective-permute-start(bf16[48,1152]{1,0:T(8,128)(2,1)} %get-tuple-element.105), channel_id=1, source_target_pairs={{0,16},{1,17},{2,18},{3,19},{4,20},{5,21},{6,22},{7,23},{8,24},{9,... | collective-permute-start | bytes 331784 | tf_op jit(solution)/shard_map/ppermute | solution.py:684
  201.1 14.3 %collective-permute-start.20 = (bf16[48,2048]{1,0:T(8,128)(2,1)}, bf16[48,2048]{1,0:T(8,128)(2,1)S(1)}, u32[]{:S(2)}, u32[]{:S(2)}) collective-permute-start(bf16[48,2048]{1,0:T(8,128)(2,1)} %add_all.4.refs_4_.refs_0_), channel_id=1, source_target_pairs={{0,8},{1,9},{2,10},{3,11},{4,12},{5,13},{6,14},{7,15},{8,0},{9,1},... | collective-permute-start | bytes 589832 | tf_op jit(solution)/shard_map/ppermute | solution.py:684
  206.3 36.6 %collective-permute-start.48 = (bf16[192,1536]{1,0:T(8,128)(2,1)}, bf16[192,1536]{1,0:T(8,128)(2,1)}, u32[]{:S(2)}, u32[]{:S(2)}) collective-permute-start(bf16[192,1536]{1,0:T(8,128)(2,1)} %join.3.refs_4_.refs_1_), channel_id=1, source_target_pairs={{0,1},{1,0},{2,3},{3,2},{4,5},{5,4},{6,7},{7,6},{8,9},{9,8},{10,11... | collective-permute-start | bytes 1769480 | tf_op jit(solution)/shard_map/ppermute | solution.py:684
  207.7 35.8 %collective-permute-start.46 = (bf16[192,1536]{1,0:T(8,128)(2,1)}, bf16[192,1536]{1,0:T(8,128)(2,1)}, u32[]{:S(2)}, u32[]{:S(2)}) collective-permute-start(bf16[192,1536]{1,0:T(8,128)(2,1)} %join.3.refs_4_.refs_1_), channel_id=1, source_target_pairs={{0,2},{1,5},{2,0},{3,7},{4,6},{5,1},{6,4},{7,3},{8,10},{9,13},{10,... | collective-permute-start | bytes 1769480 | tf_op jit(solution)/shard_map/ppermute | solution.py:684
  207.8 31.1 %collective-permute-start.45 = (bf16[192,1536]{1,0:T(8,128)(2,1)}, bf16[192,1536]{1,0:T(8,128)(2,1)}, u32[]{:S(2)}, u32[]{:S(2)}) collective-permute-start(bf16[192,1536]{1,0:T(8,128)(2,1)} %join.3.refs_4_.refs_1_), channel_id=1, source_target_pairs={{0,4},{1,3},{2,6},{3,1},{4,0},{5,7},{6,2},{7,5},{8,12},{9,11},{10,... | collective-permute-start | bytes 1769480 | tf_op jit(solution)/shard_map/ppermute | solution.py:684
  223.3 15.7 %collective-permute-start.28 = (bf16[48,1152]{1,0:T(8,128)(2,1)S(1)}, bf16[48,1152]{1,0:T(8,128)(2,1)}, u32[]{:S(2)}, u32[]{:S(2)}) collective-permute-start(bf16[48,1152]{1,0:T(8,128)(2,1)S(1)} %copy-done.20), channel_id=1, source_target_pairs={{0,16},{1,17},{2,18},{3,19},{4,20},{5,21},{6,22},{7,23},{8,24},{9,... | collective-permute-start | bytes 331784 | tf_op jit(solution)/shard_map/ppermute | solution.py:684
  226.3 17.5 %collective-permute-start.38 = (bf16[192,2048]{1,0:T(8,128)(2,1)}, bf16[192,2048]{1,0:T(8,128)(2,1)}, u32[]{:S(2)}, u32[]{:S(2)}) collective-permute-start(bf16[192,2048]{1,0:T(8,128)(2,1)} %join.4.refs_10_.refs_1_), channel_id=1, source_target_pairs={{0,4},{1,3},{2,6},{3,1},{4,0},{5,7},{6,2},{7,5},{8,12},{9,11},{10,... | collective-permute-start | bytes 2359304 | tf_op jit(solution)/shard_map/ppermute | solution.py:684
  238.9 17.4 %collective-permute-start.47 = (bf16[192,1536]{1,0:T(8,128)(2,1)}, bf16[192,1536]{1,0:T(8,128)(2,1)}, u32[]{:S(2)}, u32[]{:S(2)}) collective-permute-start(bf16[192,1536]{1,0:T(8,128)(2,1)} %collective-permute-done.45.refs_2_), channel_id=1, source_target_pairs={{0,2},{1,5},{2,0},{3,7},{4,6},{5,1},{6,4},{7,3},{8,10},{9,13},{10,... | collective-permute-start | bytes 1769480 | tf_op jit(solution)/shard_map/ppermute | solution.py:684
  240.9 13.5 %collective-permute-start.32 = (bf16[192,1152]{1,0:T(8,128)(2,1)}, bf16[192,1152]{1,0:T(8,128)(2,1)}, u32[]{:S(2)}, u32[]{:S(2)}) collective-permute-start(bf16[192,1152]{1,0:T(8,128)(2,1)} %join.5.refs_9_.refs_1_), channel_id=1, source_target_pairs={{0,2},{1,5},{2,0},{3,7},{4,6},{5,1},{6,4},{7,3},{8,10},{9,13},{10,... | collective-permute-start | bytes 1327112 | tf_op jit(solution)/shard_map/ppermute | solution.py:684
  242.9 13.4 %collective-permute-start.31 = (bf16[192,1152]{1,0:T(8,128)(2,1)}, bf16[192,1152]{1,0:T(8,128)(2,1)}, u32[]{:S(2)}, u32[]{:S(2)}) collective-permute-start(bf16[192,1152]{1,0:T(8,128)(2,1)} %join.5.refs_9_.refs_1_), channel_id=1, source_target_pairs={{0,4},{1,3},{2,6},{3,1},{4,0},{5,7},{6,2},{7,5},{8,12},{9,11},{10,... | collective-permute-start | bytes 1327112 | tf_op jit(solution)/shard_map/ppermute | solution.py:684
  243.5 19.4 %collective-permute-start.39 = (bf16[192,2048]{1,0:T(8,128)(2,1)S(1)}, bf16[192,2048]{1,0:T(8,128)(2,1)}, u32[]{:S(2)}, u32[]{:S(2)}) collective-permute-start(bf16[192,2048]{1,0:T(8,128)(2,1)S(1)} %copy-done.2), channel_id=1, source_target_pairs={{0,2},{1,5},{2,0},{3,7},{4,6},{5,1},{6,4},{7,3},{8,10},{9,13},{10,... | collective-permute-start | bytes 2359304 | tf_op jit(solution)/shard_map/ppermute | solution.py:684
  243.8 27.5 %collective-permute-start.40 = (bf16[192,2048]{1,0:T(8,128)(2,1)}, bf16[192,2048]{1,0:T(8,128)(2,1)}, u32[]{:S(2)}, u32[]{:S(2)}) collective-permute-start(bf16[192,2048]{1,0:T(8,128)(2,1)} %collective-permute-done.38.refs_2_), channel_id=1, source_target_pairs={{0,2},{1,5},{2,0},{3,7},{4,6},{5,1},{6,4},{7,3},{8,10},{9,13},{10,... | collective-permute-start | bytes 2359304 | tf_op jit(solution)/shard_map/ppermute | solution.py:684
  256.8 22.3 %collective-permute-start.41 = (bf16[192,2048]{1,0:T(8,128)(2,1)S(1)}, bf16[192,2048]{1,0:T(8,128)(2,1)}, u32[]{:S(2)}, u32[]{:S(2)}) collective-permute-start(bf16[192,2048]{1,0:T(8,128)(2,1)S(1)} %copy-done.2), channel_id=1, source_target_pairs={{0,1},{1,0},{2,3},{3,2},{4,5},{5,4},{6,7},{7,6},{8,9},{9,8},{10,11... | collective-permute-start | bytes 2359304 | tf_op jit(solution)/shard_map/ppermute | solution.py:684
  258.5 20.9 %collective-permute-start.33 = (bf16[192,1152]{1,0:T(8,128)(2,1)}, bf16[192,1152]{1,0:T(8,128)(2,1)}, u32[]{:S(2)}, u32[]{:S(2)}) collective-permute-start(bf16[192,1152]{1,0:T(8,128)(2,1)} %collective-permute-done.31.refs_2_), channel_id=1, source_target_pairs={{0,2},{1,5},{2,0},{3,7},{4,6},{5,1},{6,4},{7,3},{8,10},{9,13},{10,... | collective-permute-start | bytes 1327112 | tf_op jit(solution)/shard_map/ppermute | solution.py:684
  262.9 17.0 %collective-permute-start.42 = (bf16[192,2048]{1,0:T(8,128)(2,1)}, bf16[192,2048]{1,0:T(8,128)(2,1)}, u32[]{:S(2)}, u32[]{:S(2)}) collective-permute-start(bf16[192,2048]{1,0:T(8,128)(2,1)} %collective-permute-done.38.refs_2_), channel_id=1, source_target_pairs={{0,1},{1,0},{2,3},{3,2},{4,5},{5,4},{6,7},{7,6},{8,9},{9,8},{10,11... | collective-permute-start | bytes 2359304 | tf_op jit(solution)/shard_map/ppermute | solution.py:684
  263.9 15.7 %collective-permute-start.43 = (bf16[192,2048]{1,0:T(8,128)(2,1)}, bf16[192,2048]{1,0:T(8,128)(2,1)}, u32[]{:S(2)}, u32[]{:S(2)}) collective-permute-start(bf16[192,2048]{1,0:T(8,128)(2,1)} %collective-permute-done.39.refs_3_), channel_id=1, source_target_pairs={{0,1},{1,0},{2,3},{3,2},{4,5},{5,4},{6,7},{7,6},{8,9},{9,8},{10,11... | collective-permute-start | bytes 2359304 | tf_op jit(solution)/shard_map/ppermute | solution.py:684
  279.1 12.4 %collective-permute-start.34 = (bf16[192,1152]{1,0:T(8,128)(2,1)}, bf16[192,1152]{1,0:T(8,128)(2,1)S(1)}, u32[]{:S(2)}, u32[]{:S(2)}) collective-permute-start(bf16[192,1152]{1,0:T(8,128)(2,1)} %join.5.refs_9_.refs_1_), channel_id=1, source_target_pairs={{0,1},{1,0},{2,3},{3,2},{4,5},{5,4},{6,7},{7,6},{8,9},{9,8},{10,11... | collective-permute-start | bytes 1327112 | tf_op jit(solution)/shard_map/ppermute | solution.py:684
  279.4 12.1 %collective-permute-start.35 = (bf16[192,1152]{1,0:T(8,128)(2,1)}, bf16[192,1152]{1,0:T(8,128)(2,1)S(1)}, u32[]{:S(2)}, u32[]{:S(2)}) collective-permute-start(bf16[192,1152]{1,0:T(8,128)(2,1)} %collective-permute-done.31.refs_2_), channel_id=1, source_target_pairs={{0,1},{1,0},{2,3},{3,2},{4,5},{5,4},{6,7},{7,6},{8,9},{9,8},{10,11... | collective-permute-start | bytes 1327112 | tf_op jit(solution)/shard_map/ppermute | solution.py:684
  (43 other events, 230.9 us)

commit v4 on v3

--- a/solution.py
+++ b/solution.py
@@ -24,7 +24,7 @@
 LIMIT = 63 * 2**20
 PACE = 1.0
 WEIGHTS = dict(
-    project=11, rows=60, attend_back=19, token_grad=10, gather_units=8, gather_qkv=5.5, gather_rest=4, add_cut=2.5, add_all=2, join=2
+    project=11, rows=60, attend_back=19, token_grad=10, gather_units=8, gather_qkv=5.5, gather_two=12, add_cut=2.5, add_all=2, join=2
 )
 
 f32 = jnp.float32
@@ -487,6 +487,10 @@
 def small_call(kernel, ins, out_rows, name, deps=()):
     width = ins[0].shape[1]
     many = isinstance(out_rows, (list, tuple))
+    cuts = 2 if ins[0].shape[0] == D and all(x.shape == ins[0].shape for x in ins) else 1
+
+    def spec(x_rows, x_width):
+        return pl.BlockSpec((x_rows, x_width // cuts), lambda i: (0, i))
 
     def shape(rows):
         return jax.ShapeDtypeStruct((rows, width), bf16)
@@ -495,9 +499,9 @@
         kernel,
         name,
         deps=deps,
-        grid=(1,),
-        in_specs=[whole(*x.shape) for x in ins],
-        out_specs=[whole(r, width) for r in out_rows] if many else whole(out_rows, width),
+        grid=(cuts,),
+        in_specs=[spec(*x.shape) for x in ins],
+        out_specs=[spec(r, width) for r in out_rows] if many else spec(out_rows, width),
         out_shape=[shape(r) for r in out_rows] if many else shape(out_rows),
     )(*ins)
 
@@ -630,8 +634,11 @@
     )(sc, *parts)
 
 
-def gather_rest_kernel(block, sc, *refs):
-    group, out, gains, biases, rows = refs[:8], *refs[8:]
+def gather_two_kernel(block, sc, *refs):
+    units, group = (*refs[:8], refs[16]), refs[8:16]
+    out, gains, biases, rows = refs[17:]
+    step = pl.program_id(0)
+    gather_kernel(block, False, sc, *units)
 
     def put(row, piece):
         out[pl.ds(row, block), :] = piece
@@ -639,9 +646,11 @@
     def put_norm(row, piece):
         rows[pl.ds(row, block), :] = piece
 
-    half_of(block, sc, group, 0, HALF, put)
-
-    @pl.when(pl.program_id(0) == 0)
+    @pl.when(step < 2)
+    def _():
+        half_of(block, sc, group, 0, HALF, put)
+
+    @pl.when(step == 0)
     def _():
         half_of(block, sc, group, HALF, PAIR, put_norm)
         for i in range(2):
@@ -652,20 +661,29 @@
                 biases[i : i + 1, cols] = rows[second : second + 1, :]
 
 
-def gather_rest(sc, parts, block, deps=()):
+def gather_two(sc, parts, block, deps=()):
+    def at(own):
+        def index(g, sc):
+            return (0, jnp.clip(g - 2 * (sc[0] if own else 1 - sc[0]), 0, 1))
+
+        return pl.BlockSpec((QUARTER, D), index)
+
     norm = jax.ShapeDtypeStruct((2, D), f32)
-    spec = pl.BlockSpec((QUARTER, HALF + PAIR), lambda g, sc: (0, 2 * D // (HALF + PAIR)))
+    rest = pl.BlockSpec((QUARTER, HALF + PAIR), lambda g, sc: (0, 2 * D // (HALF + PAIR)))
     return ordered_call(
-        functools.partial(gather_rest_kernel, block),
-        "gather_rest",
+        functools.partial(gather_two_kernel, block),
+        "gather_two",
         scalars=1,
         deps=deps,
-        grid=(2,),
-        in_specs=[spec] * 8,
-        out_specs=[pl.BlockSpec((D, HALF), lambda g, sc: (0, g)), whole(2, D), whole(2, D)],
-        out_shape=[jax.ShapeDtypeStruct((D, D), f32), norm, norm],
+        grid=(4,),
+        in_specs=[at(True)] * 4 + [at(False)] * 4 + [rest] * 8,
+        out_specs=[
+            pl.BlockSpec((D, D), lambda g, sc: (0, g)), pl.BlockSpec((D, HALF), lambda g, sc: (0, jnp.minimum(g, 1))),
+            whole(2, D), whole(2, D),
+        ],
+        out_shape=[jax.ShapeDtypeStruct((D, 4 * D), f32), jax.ShapeDtypeStruct((D, D), f32), norm, norm],
         scratch_shapes=[pltpu.VMEM((D, PAIR), f32)],
-    )(sc, *parts)
+    )(sc, *parts, *parts)
 
 
 def make_local(n_dp, n_head):
@@ -785,8 +803,7 @@
         d_tokens = token_grad(sc, dres_one, d_other, d_own, w_query, w_key, w_value, deps=(two[0],))
         three = spread(three, deps=(d_tokens,))
         grad_down = gather_units(sc, one, block, True, deps=(three[0],))
-        grad_up = gather_units(sc, two, block, False, deps=(grad_down,))
-        grad_out, grad_gains, grad_biases = gather_rest(sc, two, block, deps=(grad_up,))
+        grad_up, grad_out, grad_gains, grad_biases = gather_two(sc, two, block, deps=(grad_down,))
         grad_qkv = gather_qkv(sc, three, block, deps=(grad_out,))
         return out, d_tokens, *grad_qkv, grad_out, grad_up, grad_down, grad_gains, grad_biases
 

time: 299 us -> 296 us (0.990)
  Pallas kernels: 181 us -> 178 us
    pallas_call x25 -> x24, Pallas kernels: 181 us -> 178 us  [ordered_call(): return lambda *args: call(*args, *deps)]
where the time goes in v4:
time: 296 us
  Pallas kernels  178 us (60%)
  waiting for transfers between devices  63.3 us (21%)
  starting transfers between devices  46.1 us (16%)
  local copies, waits for them, and re-layouts  7.42 us (3%)
    pallas_call x24, Pallas kernels, ordered_call(): return lambda *args: call(*args, *deps)  178 us
    ppermute x52, waiting for transfers between devices, swap(): return lax.ppermute(x, both_axes, pairs)  63.3 us
    ppermute x52, starting transfers between devices, swap(): return lax.ppermute(x, both_axes, pairs)  46.1 us
    unnamed x46, local copies, waits for them, and re-layouts  6.75 us
  transfers between devices with their start and end apart: 52, of which 16 were waited for; matrix products, arithmetic and copies ran while one was open for 0% of the time, Pallas kernels for 34%

profile of v4, /device:TPU:0, one launch (start us, length us, event | category | flops | bytes accessed | tf_op | source)
XLA Modules:
  0.0 295.6 jit_solution(1284319527296050280)
XLA Ops:
  0.6 11.0 %project.1 = (bf16[1024,768]{1,0:T(8,128)(2,1)}, bf16[1024,768]{1,0:T(8,128)(2,1)}, bf16[1024,768]{1,0:T(8,128)(2,1)}, f32[4,6,256,128]{3,2,1,0:T(8,128)}, f32[6,256,128]{2,1,0:T(8,128)}) custom-call(bf16[1024,768]{1,0:T(8,128)(2,1)} %refs_1_.7, bf16[768,768]{1,0:T(8,128)(2,1)} %refs_7_.2, bf16[768,768]{1,0:T(8,128)(2,1)} %refs_8_.2, ...), custom_call_target="tpu_custom_call" | custom-call | flops 12650000384 | bytes 1 | tf_op jit(solution)/shard_map/project/pallas_call | solution.py:71
  15.2 61.9 %rows.1 = (bf16[1024,768]{1,0:T(8,128)(2,1)}, f32[1024,768]{1,0:T(8,128)}, bf16[1024,768]{1,0:T(8,128)(2,1)}, bf16[1024,768]{1,0:T(8,128)(2,1)}, f32[4,6,256,128...) custom-call(s32[5]{0:T(128)} %stack.23.refs_0_, ...), custom_call_target="tpu_custom_call" | custom-call | flops 69000003584 | bytes 1 | tf_op jit(solution)/shard_map/rows/pallas_call | solution.py:71
  78.6 3.5 %collective-permute-done.5.refs_1_ = bf16[768,1536]{1,0:T(8,128)(2,1)} collective-permute-done((bf16[768,1536]{1,0:T(8,128)(2,1)}, bf16[768,1536]{1,0:T(8,128)(2,1)}, u32[]{:S(2)}, u32[]{:S(2)}) %collective-permute-start.5) | collective-permute-done | bytes 2359328 | tf_op jit(solution)/shard_map/ppermute | solution.py:702
  82.1 3.6 %add_cut.10 = (bf16[384,1536]{1,0:T(8,128)(2,1)}, bf16[384,1536]{1,0:T(8,128)(2,1)}) custom-call(bf16[768,1536]{1,0:T(8,128)(2,1)} %get-tuple-element.78.refs_0_, bf16[768,1536]{1,0:T(8,128)(2,1)} %collective-permute-done.5.refs_1_), custom_call_target="tpu_custom_call" | custom-call | flops 2875000064 | bytes 1 | tf_op jit(solution)/shard_map/add_cut/pallas_call | solution.py:71
  85.7 2.9 collective-permute-start.10
  88.6 5.1 %add_cut.11 = (bf16[384,2048]{1,0:T(8,128)(2,1)}, bf16[384,2048]{1,0:T(8,128)(2,1)}) custom-call(bf16[768,2048]{1,0:T(8,128)(2,1)} %get-tuple-element.74.refs_0_, bf16[768,768]{1,0:T(8,128)(2,1)} %collective-permute-done.2.refs_1_, bf16[768,768]{1,0:T(8,128)(2,1)} %collective-permute-done.3.refs_2_, bf16[768,512]{1,0:T(8,128)(2,1)} %collective-permute-done.4.refs_3_, ...), custom_call_target="tpu_custom_call" | custom-call | flops 2875000064 | bytes 1 | tf_op jit(solution)/shard_map/add_cut/pallas_call | solution.py:71
  96.6 16.2 %attend_back.2 = (bf16[1024,1152]{1,0:T(8,128)(2,1)}, bf16[768,384]{1,0:T(8,128)(2,1)}, bf16[768,384]{1,0:T(8,128)(2,1)}, bf16[768,384]{1,0:T(8,128)(2,1)}) custom-call(s32[5]{0:T(128)} %stack.23.refs_0_, bf16[1024,768]{1,0:T(8,128)(2,1)} %refs_1_.7, bf16[1024,768]{1,0:T(8,128)(2,1)} %get-tuple-element.63.refs_2_, ...), custom_call_target="tpu_custom_call" | custom-call | flops 21849999360 | bytes 1 | tf_op jit(solution)/shard_map/attend_back/pallas_call | solution.py:71
  115.2 2.8 add_cut.12
  118.0 2.8 collective-permute-start.12
  120.8 3.2 %add_cut.13 = (bf16[192,2048]{1,0:T(8,128)(2,1)}, bf16[192,2048]{1,0:T(8,128)(2,1)}) custom-call(bf16[384,2048]{1,0:T(8,128)(2,1)} %get-tuple-element.81.refs_15_.refs_0_, bf16[384,2048]{1,0:T(8,128)(2,1)} %collective-permute-done.9.refs_1_, bf16[192,1536]{1,0:T(8,128)(2,1)} %get-tuple-element.88.refs_2_.refs_0_), custom_call_target="tpu_custom_call" | custom-call | flops 2875000064 | bytes 1 | tf_op jit(solution)/shard_map/add_cut/pallas_call | solution.py:71
  126.3 17.3 %attend_back.3 = (bf16[1024,1152]{1,0:T(8,128)(2,1)}, bf16[384,1152]{1,0:T(8,128)(2,1)}, bf16[384,1152]{1,0:T(8,128)(2,1)}) custom-call(s32[5]{0:T(128)} %stack.23.refs_0_, bf16[1024,768]{1,0:T(8,128)(2,1)} %refs_1_.7, bf16[1024,768]{1,0:T(8,128)(2,1)} %get-tuple-element.63.refs_2_, bf16[1024,768]{1,0:T(8,128)(2,1)} %get-tuple-element.64.refs_3_, ...), custom_call_target="tpu_custom_call" | custom-call | flops 21849999360 | bytes 1 | tf_op jit(solution)/shard_map/attend_back/pallas_call | solution.py:71
  146.8 2.1 add_cut.14
  150.3 2.3 add_cut.15
  153.3 7.0 %collective-permute-done.15.refs_1_ = bf16[96,1536]{1,0:T(8,128)(2,1)} collective-permute-done((bf16[96,1536]{1,0:T(8,128)(2,1)}, bf16[96,1536]{1,0:T(8,128)(2,1)}, u32[]{:S(2)}, u32[]{:S(2)}) %collective-permute-start.15) | collective-permute-done | bytes 294944 | tf_op jit(solution)/shard_map/ppermute | solution.py:702
  163.5 2.4 add_cut.17
  172.7 2.8 collective-permute-start.25
  178.3 2.8 collective-permute-start.22
  181.1 15.8 %collective-permute-done.16.refs_1_ = bf16[48,2048]{1,0:T(8,128)(2,1)S(1)} collective-permute-done((bf16[48,2048]{1,0:T(8,128)(2,1)S(1)}, bf16[48,2048]{1,0:T(8,128)(2,1)S(1)}, u32[]{:S(2)}, u32[]{:S(2)}) %collective-permute-start.16) | collective-permute-done | bytes 196640 | tf_op jit(solution)/shard_map/ppermute | solution.py:702
  201.1 2.8 collective-permute-start.19
  209.3 3.8 %collective-permute-done.19.refs_1_ = bf16[48,2048]{1,0:T(8,128)(2,1)S(1)} collective-permute-done((bf16[48,2048]{1,0:T(8,128)(2,1)}, bf16[48,2048]{1,0:T(8,128)(2,1)S(1)}, u32[]{:S(2)}, u32[]{:S(2)}) %collective-permute-start.19) | collective-permute-done | bytes 196640 | tf_op jit(solution)/shard_map/ppermute | solution.py:702
  215.0 2.9 collective-permute-start.30
  217.8 2.1 collective-permute-done.21.refs_3_
  220.6 2.1 join.4.refs_10_.refs_1_.refs_9_
  222.8 2.0 collective-permute-start.28
  225.8 2.2 collective-permute-start.38
  228.0 10.4 %token_grad.1.refs_4_ = f32[1024,768]{1,0:T(8,128)} custom-call(s32[5]{0:T(128)} %stack.23.refs_0_, f32[1024,768]{1,0:T(8,128)} %get-tuple-element.69.refs_1_, bf16[1024,1152]{1,0:T(8,128)(2,1)} %get-tuple-element.82.refs_2_, bf16[1024,1152]{1,0:T(8,128)(2,1)} %get-tuple-element.90.refs_3_, bf16[768,768]{1,0:T(8,128)(2,1)} %refs_7_.2, ...), custom_call_target="tpu_custom_call" | custom-call | flops 11500000256 | bytes 1 | tf_op jit(solution)/shard_map/token_grad/pallas_call | solution.py:71
  245.1 8.9 %collective-permute-done.32.refs_3_ = bf16[192,1152]{1,0:T(8,128)(2,1)} collective-permute-done((bf16[192,1152]{1,0:T(8,128)(2,1)}, bf16[192,1152]{1,0:T(8,128)(2,1)}, u32[]{:S(2)}, u32[]{:S(2)}) %collective-permute-start.32) | collective-permute-done | bytes 442400 | tf_op jit(solution)/shard_map/ppermute | solution.py:702
  258.2 4.3 %collective-permute-done.39.refs_3_.refs_11_ = bf16[192,2048]{1,0:T(8,128)(2,1)} collective-permute-done((bf16[192,2048]{1,0:T(8,128)(2,1)S(1)}, bf16[192,2048]{1,0:T(8,128)(2,1)}, u32[]{:S(2)}, u32[]{:S(2)}) %collective-permute-start.39) | collective-permute-done | bytes 786464 | tf_op jit(solution)/shard_map/ppermute | solution.py:702
  263.8 7.1 %collective-permute-done.40.refs_4_.refs_12_ = bf16[192,2048]{1,0:T(8,128)(2,1)} collective-permute-done((bf16[192,2048]{1,0:T(8,128)(2,1)}, bf16[192,2048]{1,0:T(8,128)(2,1)}, u32[]{:S(2)}, u32[]{:S(2)}) %collective-permute-start.40) | collective-permute-done | bytes 786464 | tf_op jit(solution)/shard_map/ppermute | solution.py:702
  271.1 7.5 %gather_units.1.refs_17_ = f32[3072,768]{1,0:T(8,128)} custom-call(s32[5]{0:T(128)} %stack.23.refs_0_, bf16[192,1536]{1,0:T(8,128)(2,1)} %join.3.refs_4_.refs_1_, bf16[192,1536]{1,0:T(8,128)(2,1)} %collective-permute-done.45.refs_2_, bf16[192,1536]{1,0:T(8,128)(2,1)} %collective-permute-done.46.refs_3_, bf16[192,1536]{1,0:T(8,128)(2,1)} %collective-permute-done.47.refs_4_, ...), custom_call_target="tpu_custom_call" | custom-call | flops 9200000000 | bytes 1 | tf_op jit(solution)/shard_map/gather_units/pallas_call | solution.py:71
  279.7 9.0 %gather_two.1 = (f32[768,3072]{1,0:T(8,128)}, f32[768,768]{1,0:T(8,128)}, f32[2,768]{1,0:T(2,128)}, f32[2,768]{1,0:T(2,128)}) custom-call(s32[5]{0:T(128)} %stack.23.refs_0_, bf16[192,2048]{1,0:T(8,128)(2,1)} %join.4.refs_10_.refs_1_.refs_9_, bf16[192,2048]{1,0:T(8,128)(2,1)} %collective-permute-done.38.refs_2_.refs_10_, ...), custom_call_target="tpu_custom_call" | custom-call | flops 13800000512 | bytes 1 | tf_op jit(solution)/shard_map/gather_two/pallas_call | solution.py:71
  289.8 5.9 %gather_qkv.1 = (f32[768,768]{1,0:T(8,128)}, f32[768,768]{1,0:T(8,128)}, f32[768,768]{1,0:T(8,128)}) custom-call(s32[5]{0:T(128)} %stack.23.refs_0_, bf16[192,1152]{1,0:T(8,128)(2,1)} %join.5.refs_9_.refs_1_, bf16[192,1152]{1,0:T(8,128)(2,1)} %collective-permute-done.31.refs_2_, bf16[192,1152]{1,0:T(8,128)(2,1)} %collective-permute-done.32.refs_3_, ...), custom_call_target="tpu_custom_call" | custom-call | flops 6325000192 | bytes 1 | tf_op jit(solution)/shard_map/gather_qkv/pallas_call | solution.py:71
  (143 shorter events, 58.1 us)
Async XLA Ops:
  78.2 17.5 %collective-permute-start.1 = (f32[6,256,128]{2,1,0:T(8,128)}, f32[6,256,128]{2,1,0:T(8,128)S(1)}, u32[]{:S(2)}, u32[]{:S(2)}) collective-permute-start(f32[6,256,128]{2,1,0:T(8,128)} %get-tuple-element.73), channel_id=1, source_target_pairs={{0,1},{1,0},{2,3},{3,2},{4,5},{5,4},{6,7},{7,6},{8,9},{9,8},{10,11... | collective-permute-start | bytes 2359304 | tf_op jit(solution)/shard_map/ppermute | solution.py:702
  85.7 29.5 %collective-permute-start.10 = (bf16[384,1536]{1,0:T(8,128)(2,1)}, bf16[384,1536]{1,0:T(8,128)(2,1)}, u32[]{:S(2)}, u32[]{:S(2)}) collective-permute-start(bf16[384,1536]{1,0:T(8,128)(2,1)} %get-tuple-element.87), channel_id=1, source_target_pairs={{0,8},{1,9},{2,10},{3,11},{4,12},{5,13},{6,14},{7,15},{8,0},{9,1},... | collective-permute-start | bytes 3538952 | tf_op jit(solution)/shard_map/ppermute | solution.py:702
  93.7 27.1 %collective-permute-start.9 = (bf16[384,2048]{1,0:T(8,128)(2,1)}, bf16[384,2048]{1,0:T(8,128)(2,1)}, u32[]{:S(2)}, u32[]{:S(2)}) collective-permute-start(bf16[384,2048]{1,0:T(8,128)(2,1)} %get-tuple-element.86), channel_id=1, source_target_pairs={{0,2},{1,5},{2,0},{3,7},{4,6},{5,1},{6,4},{7,3},{8,10},{9,13},{10,... | collective-permute-start | bytes 4718600 | tf_op jit(solution)/shard_map/ppermute | solution.py:702
  112.8 12.8 %collective-permute-start.6 = (bf16[768,384]{1,0:T(8,128)(2,1)}, bf16[768,384]{1,0:T(8,128)(2,1)S(1)}, u32[]{:S(2)}, u32[]{:S(2)}) collective-permute-start(bf16[768,384]{1,0:T(8,128)(2,1)} %get-tuple-element.83), channel_id=1, source_target_pairs={{0,1},{1,0},{2,3},{3,2},{4,5},{5,4},{6,7},{7,6},{8,9},{9,8},{10,11... | collective-permute-start | bytes 1769480 | tf_op jit(solution)/shard_map/ppermute | solution.py:702
  112.8 12.7 %collective-permute-start.7 = (bf16[768,384]{1,0:T(8,128)(2,1)}, bf16[768,384]{1,0:T(8,128)(2,1)}, u32[]{:S(2)}, u32[]{:S(2)}) collective-permute-start(bf16[768,384]{1,0:T(8,128)(2,1)} %get-tuple-element.84), channel_id=1, source_target_pairs={{0,1},{1,0},{2,3},{3,2},{4,5},{5,4},{6,7},{7,6},{8,9},{9,8},{10,11... | collective-permute-start | bytes 1769480 | tf_op jit(solution)/shard_map/ppermute | solution.py:702
  113.3 12.2 %collective-permute-start.8 = (bf16[768,384]{1,0:T(8,128)(2,1)}, bf16[768,384]{1,0:T(8,128)(2,1)}, u32[]{:S(2)}, u32[]{:S(2)}) collective-permute-start(bf16[768,384]{1,0:T(8,128)(2,1)} %get-tuple-element.85), channel_id=1, source_target_pairs={{0,1},{1,0},{2,3},{3,2},{4,5},{5,4},{6,7},{7,6},{8,9},{9,8},{10,11... | collective-permute-start | bytes 1769480 | tf_op jit(solution)/shard_map/ppermute | solution.py:702
  118.0 28.8 %collective-permute-start.12 = (bf16[192,1536]{1,0:T(8,128)(2,1)}, bf16[192,1536]{1,0:T(8,128)(2,1)}, u32[]{:S(2)}, u32[]{:S(2)}) collective-permute-start(bf16[192,1536]{1,0:T(8,128)(2,1)} %get-tuple-element.92), channel_id=1, source_target_pairs={{0,16},{1,17},{2,18},{3,19},{4,20},{5,21},{6,22},{7,23},{8,24},{9,... | collective-permute-start | bytes 1769480 | tf_op jit(solution)/shard_map/ppermute | solution.py:702
  124.0 26.2 %collective-permute-start.11 = (bf16[192,2048]{1,0:T(8,128)(2,1)}, bf16[192,2048]{1,0:T(8,128)(2,1)}, u32[]{:S(2)}, u32[]{:S(2)}) collective-permute-start(bf16[192,2048]{1,0:T(8,128)(2,1)} %get-tuple-element.91), channel_id=1, source_target_pairs={{0,4},{1,3},{2,6},{3,1},{4,0},{5,7},{6,2},{7,5},{8,12},{9,11},{10,... | collective-permute-start | bytes 2359304 | tf_op jit(solution)/shard_map/ppermute | solution.py:702
  143.7 18.9 %collective-permute-start.14 = (bf16[384,1152]{1,0:T(8,128)(2,1)}, bf16[384,1152]{1,0:T(8,128)(2,1)S(1)}, u32[]{:S(2)}, u32[]{:S(2)}) collective-permute-start(bf16[384,1152]{1,0:T(8,128)(2,1)} %get-tuple-element.97), channel_id=1, source_target_pairs={{0,2},{1,5},{2,0},{3,7},{4,6},{5,1},{6,4},{7,3},{8,10},{9,13},{10,... | collective-permute-start | bytes 2654216 | tf_op jit(solution)/shard_map/ppermute | solution.py:702
  148.9 11.4 %collective-permute-start.15 = (bf16[96,1536]{1,0:T(8,128)(2,1)}, bf16[96,1536]{1,0:T(8,128)(2,1)}, u32[]{:S(2)}, u32[]{:S(2)}) collective-permute-start(bf16[96,1536]{1,0:T(8,128)(2,1)} %get-tuple-element.98), channel_id=1, source_target_pairs={{0,2},{1,5},{2,0},{3,7},{4,6},{5,1},{6,4},{7,3},{8,10},{9,13},{10,... | collective-permute-start | bytes 884744 | tf_op jit(solution)/shard_map/ppermute | solution.py:702
  152.6 14.9 %collective-permute-start.13 = (bf16[96,2048]{1,0:T(8,128)(2,1)}, bf16[96,2048]{1,0:T(8,128)(2,1)}, u32[]{:S(2)}, u32[]{:S(2)}) collective-permute-start(bf16[96,2048]{1,0:T(8,128)(2,1)} %get-tuple-element.96), channel_id=1, source_target_pairs={{0,8},{1,9},{2,10},{3,11},{4,12},{5,13},{6,14},{7,15},{8,0},{9,1},... | collective-permute-start | bytes 1179656 | tf_op jit(solution)/shard_map/ppermute | solution.py:702
  171.1 28.3 %collective-permute-start.27 = (bf16[48,1536]{1,0:T(8,128)(2,1)}, bf16[48,1536]{1,0:T(8,128)(2,1)S(1)}, u32[]{:S(2)}, u32[]{:S(2)}) collective-permute-start(bf16[48,1536]{1,0:T(8,128)(2,1)} %add_all.3.refs_2_.refs_0_), channel_id=1, source_target_pairs={{0,24},{1,25},{2,26},{3,27},{4,28},{5,29},{6,30},{7,31},{8,16},{9,... | collective-permute-start | bytes 442376 | tf_op jit(solution)/shard_map/ppermute | solution.py:702
  172.4 28.2 %collective-permute-start.26 = (bf16[48,1536]{1,0:T(8,128)(2,1)}, bf16[48,1536]{1,0:T(8,128)(2,1)}, u32[]{:S(2)}, u32[]{:S(2)}) collective-permute-start(bf16[48,1536]{1,0:T(8,128)(2,1)} %add_all.3.refs_2_.refs_0_), channel_id=1, source_target_pairs={{0,8},{1,9},{2,10},{3,11},{4,12},{5,13},{6,14},{7,15},{8,0},{9,1},... | collective-permute-start | bytes 442376 | tf_op jit(solution)/shard_map/ppermute | solution.py:702
  172.7 28.4 %collective-permute-start.25 = (bf16[48,1536]{1,0:T(8,128)(2,1)}, bf16[48,1536]{1,0:T(8,128)(2,1)}, u32[]{:S(2)}, u32[]{:S(2)}) collective-permute-start(bf16[48,1536]{1,0:T(8,128)(2,1)} %add_all.3.refs_2_.refs_0_), channel_id=1, source_target_pairs={{0,16},{1,17},{2,18},{3,19},{4,20},{5,21},{6,22},{7,23},{8,24},{9,... | collective-permute-start | bytes 442376 | tf_op jit(solution)/shard_map/ppermute | solution.py:702
  175.5 21.4 %collective-permute-start.16 = (bf16[48,2048]{1,0:T(8,128)(2,1)S(1)}, bf16[48,2048]{1,0:T(8,128)(2,1)S(1)}, u32[]{:S(2)}, u32[]{:S(2)}) collective-permute-start(bf16[48,2048]{1,0:T(8,128)(2,1)S(1)} %copy-done.13), channel_id=1, source_target_pairs={{0,16},{1,17},{2,18},{3,19},{4,20},{5,21},{6,22},{7,23},{8,24},{9,... | collective-permute-start | bytes 589832 | tf_op jit(solution)/shard_map/ppermute | solution.py:702
  178.3 27.5 %collective-permute-start.22 = (bf16[48,1152]{1,0:T(8,128)(2,1)}, bf16[48,1152]{1,0:T(8,128)(2,1)}, u32[]{:S(2)}, u32[]{:S(2)}) collective-permute-start(bf16[48,1152]{1,0:T(8,128)(2,1)} %get-tuple-element.106), channel_id=1, source_target_pairs={{0,16},{1,17},{2,18},{3,19},{4,20},{5,21},{6,22},{7,23},{8,24},{9,... | collective-permute-start | bytes 331784 | tf_op jit(solution)/shard_map/ppermute | solution.py:702
  200.6 14.3 %collective-permute-start.20 = (bf16[48,2048]{1,0:T(8,128)(2,1)}, bf16[48,2048]{1,0:T(8,128)(2,1)S(1)}, u32[]{:S(2)}, u32[]{:S(2)}) collective-permute-start(bf16[48,2048]{1,0:T(8,128)(2,1)} %add_all.4.refs_4_.refs_0_), channel_id=1, source_target_pairs={{0,8},{1,9},{2,10},{3,11},{4,12},{5,13},{6,14},{7,15},{8,0},{9,1},... | collective-permute-start | bytes 589832 | tf_op jit(solution)/shard_map/ppermute | solution.py:702
  201.1 12.0 %collective-permute-start.19 = (bf16[48,2048]{1,0:T(8,128)(2,1)}, bf16[48,2048]{1,0:T(8,128)(2,1)S(1)}, u32[]{:S(2)}, u32[]{:S(2)}) collective-permute-start(bf16[48,2048]{1,0:T(8,128)(2,1)} %add_all.4.refs_4_.refs_0_), channel_id=1, source_target_pairs={{0,16},{1,17},{2,18},{3,19},{4,20},{5,21},{6,22},{7,23},{8,24},{9,... | collective-permute-start | bytes 589832 | tf_op jit(solution)/shard_map/ppermute | solution.py:702
  205.8 36.6 %collective-permute-start.48 = (bf16[192,1536]{1,0:T(8,128)(2,1)}, bf16[192,1536]{1,0:T(8,128)(2,1)}, u32[]{:S(2)}, u32[]{:S(2)}) collective-permute-start(bf16[192,1536]{1,0:T(8,128)(2,1)} %join.3.refs_4_.refs_1_), channel_id=1, source_target_pairs={{0,1},{1,0},{2,3},{3,2},{4,5},{5,4},{6,7},{7,6},{8,9},{9,8},{10,11... | collective-permute-start | bytes 1769480 | tf_op jit(solution)/shard_map/ppermute | solution.py:702
  207.3 35.8 %collective-permute-start.46 = (bf16[192,1536]{1,0:T(8,128)(2,1)}, bf16[192,1536]{1,0:T(8,128)(2,1)}, u32[]{:S(2)}, u32[]{:S(2)}) collective-permute-start(bf16[192,1536]{1,0:T(8,128)(2,1)} %join.3.refs_4_.refs_1_), channel_id=1, source_target_pairs={{0,2},{1,5},{2,0},{3,7},{4,6},{5,1},{6,4},{7,3},{8,10},{9,13},{10,... | collective-permute-start | bytes 1769480 | tf_op jit(solution)/shard_map/ppermute | solution.py:702
  207.3 31.1 %collective-permute-start.45 = (bf16[192,1536]{1,0:T(8,128)(2,1)}, bf16[192,1536]{1,0:T(8,128)(2,1)}, u32[]{:S(2)}, u32[]{:S(2)}) collective-permute-start(bf16[192,1536]{1,0:T(8,128)(2,1)} %join.3.refs_4_.refs_1_), channel_id=1, source_target_pairs={{0,4},{1,3},{2,6},{3,1},{4,0},{5,7},{6,2},{7,5},{8,12},{9,11},{10,... | collective-permute-start | bytes 1769480 | tf_op jit(solution)/shard_map/ppermute | solution.py:702
  222.8 15.7 %collective-permute-start.28 = (bf16[48,1152]{1,0:T(8,128)(2,1)S(1)}, bf16[48,1152]{1,0:T(8,128)(2,1)}, u32[]{:S(2)}, u32[]{:S(2)}) collective-permute-start(bf16[48,1152]{1,0:T(8,128)(2,1)S(1)} %copy-done.20), channel_id=1, source_target_pairs={{0,16},{1,17},{2,18},{3,19},{4,20},{5,21},{6,22},{7,23},{8,24},{9,... | collective-permute-start | bytes 331784 | tf_op jit(solution)/shard_map/ppermute | solution.py:702
  225.8 17.5 %collective-permute-start.38 = (bf16[192,2048]{1,0:T(8,128)(2,1)}, bf16[192,2048]{1,0:T(8,128)(2,1)}, u32[]{:S(2)}, u32[]{:S(2)}) collective-permute-start(bf16[192,2048]{1,0:T(8,128)(2,1)} %join.4.refs_10_.refs_1_.refs_9_), channel_id=1, source_target_pairs={{0,4},{1,3},{2,6},{3,1},{4,0},{5,7},{6,2},{7,5},{8,12},{9,11},{10,... | collective-permute-start | bytes 2359304 | tf_op jit(solution)/shard_map/ppermute | solution.py:702
  238.4 17.4 %collective-permute-start.47 = (bf16[192,1536]{1,0:T(8,128)(2,1)}, bf16[192,1536]{1,0:T(8,128)(2,1)}, u32[]{:S(2)}, u32[]{:S(2)}) collective-permute-start(bf16[192,1536]{1,0:T(8,128)(2,1)} %collective-permute-done.45.refs_2_), channel_id=1, source_target_pairs={{0,2},{1,5},{2,0},{3,7},{4,6},{5,1},{6,4},{7,3},{8,10},{9,13},{10,... | collective-permute-start | bytes 1769480 | tf_op jit(solution)/shard_map/ppermute | solution.py:702
  240.4 13.6 %collective-permute-start.32 = (bf16[192,1152]{1,0:T(8,128)(2,1)}, bf16[192,1152]{1,0:T(8,128)(2,1)}, u32[]{:S(2)}, u32[]{:S(2)}) collective-permute-start(bf16[192,1152]{1,0:T(8,128)(2,1)} %join.5.refs_9_.refs_1_), channel_id=1, source_target_pairs={{0,2},{1,5},{2,0},{3,7},{4,6},{5,1},{6,4},{7,3},{8,10},{9,13},{10,... | collective-permute-start | bytes 1327112 | tf_op jit(solution)/shard_map/ppermute | solution.py:702
  242.4 13.4 %collective-permute-start.31 = (bf16[192,1152]{1,0:T(8,128)(2,1)}, bf16[192,1152]{1,0:T(8,128)(2,1)}, u32[]{:S(2)}, u32[]{:S(2)}) collective-permute-start(bf16[192,1152]{1,0:T(8,128)(2,1)} %join.5.refs_9_.refs_1_), channel_id=1, source_target_pairs={{0,4},{1,3},{2,6},{3,1},{4,0},{5,7},{6,2},{7,5},{8,12},{9,11},{10,... | collective-permute-start | bytes 1327112 | tf_op jit(solution)/shard_map/ppermute | solution.py:702
  243.0 19.4 %collective-permute-start.39 = (bf16[192,2048]{1,0:T(8,128)(2,1)S(1)}, bf16[192,2048]{1,0:T(8,128)(2,1)}, u32[]{:S(2)}, u32[]{:S(2)}) collective-permute-start(bf16[192,2048]{1,0:T(8,128)(2,1)S(1)} %copy-done.2), channel_id=1, source_target_pairs={{0,2},{1,5},{2,0},{3,7},{4,6},{5,1},{6,4},{7,3},{8,10},{9,13},{10,... | collective-permute-start | bytes 2359304 | tf_op jit(solution)/shard_map/ppermute | solution.py:702
  243.3 27.5 %collective-permute-start.40 = (bf16[192,2048]{1,0:T(8,128)(2,1)}, bf16[192,2048]{1,0:T(8,128)(2,1)}, u32[]{:S(2)}, u32[]{:S(2)}) collective-permute-start(bf16[192,2048]{1,0:T(8,128)(2,1)} %collective-permute-done.38.refs_2_.refs_10_), channel_id=1, source_target_pairs={{0,2},{1,5},{2,0},{3,7},{4,6},{5,1},{6,4},{7,3},{8,10},{9,13},{10,... | collective-permute-start | bytes 2359304 | tf_op jit(solution)/shard_map/ppermute | solution.py:702
  256.3 22.3 %collective-permute-start.41 = (bf16[192,2048]{1,0:T(8,128)(2,1)S(1)}, bf16[192,2048]{1,0:T(8,128)(2,1)}, u32[]{:S(2)}, u32[]{:S(2)}) collective-permute-start(bf16[192,2048]{1,0:T(8,128)(2,1)S(1)} %copy-done.2), channel_id=1, source_target_pairs={{0,1},{1,0},{2,3},{3,2},{4,5},{5,4},{6,7},{7,6},{8,9},{9,8},{10,11... | collective-permute-start | bytes 2359304 | tf_op jit(solution)/shard_map/ppermute | solution.py:702
  258.0 20.9 %collective-permute-start.33 = (bf16[192,1152]{1,0:T(8,128)(2,1)}, bf16[192,1152]{1,0:T(8,128)(2,1)}, u32[]{:S(2)}, u32[]{:S(2)}) collective-permute-start(bf16[192,1152]{1,0:T(8,128)(2,1)} %collective-permute-done.31.refs_2_), channel_id=1, source_target_pairs={{0,2},{1,5},{2,0},{3,7},{4,6},{5,1},{6,4},{7,3},{8,10},{9,13},{10,... | collective-permute-start | bytes 1327112 | tf_op jit(solution)/shard_map/ppermute | solution.py:702
  262.5 17.0 %collective-permute-start.42 = (bf16[192,2048]{1,0:T(8,128)(2,1)}, bf16[192,2048]{1,0:T(8,128)(2,1)}, u32[]{:S(2)}, u32[]{:S(2)}) collective-permute-start(bf16[192,2048]{1,0:T(8,128)(2,1)} %collective-permute-done.38.refs_2_.refs_10_), channel_id=1, source_target_pairs={{0,1},{1,0},{2,3},{3,2},{4,5},{5,4},{6,7},{7,6},{8,9},{9,8},{10,11... | collective-permute-start | bytes 2359304 | tf_op jit(solution)/shard_map/ppermute | solution.py:702
  263.5 15.7 %collective-permute-start.43 = (bf16[192,2048]{1,0:T(8,128)(2,1)}, bf16[192,2048]{1,0:T(8,128)(2,1)}, u32[]{:S(2)}, u32[]{:S(2)}) collective-permute-start(bf16[192,2048]{1,0:T(8,128)(2,1)} %collective-permute-done.39.refs_3_.refs_11_), channel_id=1, source_target_pairs={{0,1},{1,0},{2,3},{3,2},{4,5},{5,4},{6,7},{7,6},{8,9},{9,8},{10,11... | collective-permute-start | bytes 2359304 | tf_op jit(solution)/shard_map/ppermute | solution.py:702
  (43 other events, 221.5 us)

commit v5 on v4

--- a/solution.py
+++ b/solution.py
@@ -223,7 +223,7 @@
         h = nn(low, w_up[:, cols])
         phi = 0.5 * (1.0 + lax.erf(h * (0.5**0.5)))
         hid[:, cols] = (h * phi).astype(bf16)
-        slope[:, cols] = phi + h * jnp.exp(-0.5 * h * h) * ((2 * math.pi) ** -0.5)
+        slope[:, cols] = (phi + h * jnp.exp(-0.5 * h * h) * ((2 * math.pi) ** -0.5)).astype(bf16)
     z = normed + nn(hid[...], w_down[...])
     n1, rstd1 = norm_parts(z)
     out_ref[...] = (n1 * gains[1:2] + biases[1:2]).astype(bf16)
@@ -234,7 +234,7 @@
     dffn = dres.astype(bf16)
     for j in range(FF // D):
         cols = slice(j * D, (j + 1) * D)
-        dhid[:, cols] = (nt(dffn, w_down[cols, :]) * slope[:, cols]).astype(bf16)
+        dhid[:, cols] = (nt(dffn, w_down[cols, :]) * slope[:, cols].astype(f32)).astype(bf16)
     g = dres + nt(dhid[...], w_up[...])
     ng[0:1] += jnp.sum(g * n0, axis=0, keepdims=True)
     ng[1:2] += jnp.sum(g, axis=0, keepdims=True)
@@ -347,7 +347,7 @@
         ],
         scratch_shapes=[
             pltpu.VMEM((D, FF), bf16), pltpu.VMEM((FF, D), bf16),
-            pltpu.VMEM((CHUNK, D), bf16), pltpu.VMEM((CHUNK, FF), bf16), pltpu.VMEM((CHUNK, FF), f32),
+            pltpu.VMEM((CHUNK, D), bf16), pltpu.VMEM((CHUNK, FF), bf16), pltpu.VMEM((CHUNK, FF), bf16),
             pltpu.VMEM((CHUNK, FF), bf16), pltpu.VMEM((FF, D), f32), pltpu.VMEM((D, FF), f32), pltpu.VMEM((D, D), f32),
             pltpu.VMEM((4, D), f32), pltpu.VMEM((3, D, D), bf16), pltpu.VMEM((2, D, PAIR), bf16),
             pltpu.SemaphoreType.DMA((3,)), pltpu.SemaphoreType.DMA((2,)), pltpu.SemaphoreType.DMA((2,)),

time: 296 us -> 297 us (level)
  no operation moved by 1% of the time
where the time goes in v5:
time: 297 us; the launch traced here: 296 us
  Pallas kernels  178 us (60%)
  waiting for transfers between devices  63.2 us (21%)
  starting transfers between devices  46.2 us (16%)
  local copies, waits for them, and re-layouts  7.4 us (2%)
    pallas_call x24, Pallas kernels, ordered_call(): return lambda *args: call(*args, *deps)  178 us
    ppermute x52, waiting for transfers between devices, swap(): return lax.ppermute(x, both_axes, pairs)  63.2 us
    ppermute x52, starting transfers between devices, swap(): return lax.ppermute(x, both_axes, pairs)  46.2 us
    unnamed x46, local copies, waits for them, and re-layouts  6.73 us
  transfers between devices with their start and end apart: 52, of which 16 were waited for; matrix products, arithmetic and copies ran while one was open for 0% of the time, Pallas kernels for 34%

profile of v5, /device:TPU:0, one launch (start us, length us, event | category | flops | bytes accessed | tf_op | source)
XLA Modules:
  0.0 295.7 jit_solution(9500310788587436754)
XLA Ops:
  0.6 11.0 %project.1 = (bf16[1024,768]{1,0:T(8,128)(2,1)}, bf16[1024,768]{1,0:T(8,128)(2,1)}, bf16[1024,768]{1,0:T(8,128)(2,1)}, f32[4,6,256,128]{3,2,1,0:T(8,128)}, f32[6,256,128]{2,1,0:T(8,128)}) custom-call(bf16[1024,768]{1,0:T(8,128)(2,1)} %refs_1_.7, bf16[768,768]{1,0:T(8,128)(2,1)} %refs_7_.2, bf16[768,768]{1,0:T(8,128)(2,1)} %refs_8_.2, ...), custom_call_target="tpu_custom_call" | custom-call | flops 12650000384 | bytes 1 | tf_op jit(solution)/shard_map/project/pallas_call | solution.py:71
  15.2 62.0 %rows.1 = (bf16[1024,768]{1,0:T(8,128)(2,1)}, f32[1024,768]{1,0:T(8,128)}, bf16[1024,768]{1,0:T(8,128)(2,1)}, bf16[1024,768]{1,0:T(8,128)(2,1)}, f32[4,6,256,128...) custom-call(s32[5]{0:T(128)} %stack.23.refs_0_, ...), custom_call_target="tpu_custom_call" | custom-call | flops 69000003584 | bytes 1 | tf_op jit(solution)/shard_map/rows/pallas_call | solution.py:71
  78.8 3.5 %collective-permute-done.5.refs_1_ = bf16[768,1536]{1,0:T(8,128)(2,1)} collective-permute-done((bf16[768,1536]{1,0:T(8,128)(2,1)}, bf16[768,1536]{1,0:T(8,128)(2,1)}, u32[]{:S(2)}, u32[]{:S(2)}) %collective-permute-start.5) | collective-permute-done | bytes 2359328 | tf_op jit(solution)/shard_map/ppermute | solution.py:702
  82.3 3.6 %add_cut.10 = (bf16[384,1536]{1,0:T(8,128)(2,1)}, bf16[384,1536]{1,0:T(8,128)(2,1)}) custom-call(bf16[768,1536]{1,0:T(8,128)(2,1)} %get-tuple-element.78.refs_0_, bf16[768,1536]{1,0:T(8,128)(2,1)} %collective-permute-done.5.refs_1_), custom_call_target="tpu_custom_call" | custom-call | flops 2875000064 | bytes 1 | tf_op jit(solution)/shard_map/add_cut/pallas_call | solution.py:71
  85.9 2.9 collective-permute-start.10
  88.7 5.1 %add_cut.11 = (bf16[384,2048]{1,0:T(8,128)(2,1)}, bf16[384,2048]{1,0:T(8,128)(2,1)}) custom-call(bf16[768,2048]{1,0:T(8,128)(2,1)} %get-tuple-element.74.refs_0_, bf16[768,768]{1,0:T(8,128)(2,1)} %collective-permute-done.2.refs_1_, bf16[768,768]{1,0:T(8,128)(2,1)} %collective-permute-done.3.refs_2_, bf16[768,512]{1,0:T(8,128)(2,1)} %collective-permute-done.4.refs_3_, ...), custom_call_target="tpu_custom_call" | custom-call | flops 2875000064 | bytes 1 | tf_op jit(solution)/shard_map/add_cut/pallas_call | solution.py:71
  96.7 16.2 %attend_back.2 = (bf16[1024,1152]{1,0:T(8,128)(2,1)}, bf16[768,384]{1,0:T(8,128)(2,1)}, bf16[768,384]{1,0:T(8,128)(2,1)}, bf16[768,384]{1,0:T(8,128)(2,1)}) custom-call(s32[5]{0:T(128)} %stack.23.refs_0_, bf16[1024,768]{1,0:T(8,128)(2,1)} %refs_1_.7, bf16[1024,768]{1,0:T(8,128)(2,1)} %get-tuple-element.63.refs_2_, ...), custom_call_target="tpu_custom_call" | custom-call | flops 21849999360 | bytes 1 | tf_op jit(solution)/shard_map/attend_back/pallas_call | solution.py:71
  115.4 2.8 add_cut.12
  118.2 2.8 collective-permute-start.12
  120.9 3.2 %add_cut.13 = (bf16[192,2048]{1,0:T(8,128)(2,1)}, bf16[192,2048]{1,0:T(8,128)(2,1)}) custom-call(bf16[384,2048]{1,0:T(8,128)(2,1)} %get-tuple-element.81.refs_15_.refs_0_, bf16[384,2048]{1,0:T(8,128)(2,1)} %collective-permute-done.9.refs_1_, bf16[192,1536]{1,0:T(8,128)(2,1)} %get-tuple-element.88.refs_2_.refs_0_), custom_call_target="tpu_custom_call" | custom-call | flops 2875000064 | bytes 1 | tf_op jit(solution)/shard_map/add_cut/pallas_call | solution.py:71
  126.5 17.3 %attend_back.3 = (bf16[1024,1152]{1,0:T(8,128)(2,1)}, bf16[384,1152]{1,0:T(8,128)(2,1)}, bf16[384,1152]{1,0:T(8,128)(2,1)}) custom-call(s32[5]{0:T(128)} %stack.23.refs_0_, bf16[1024,768]{1,0:T(8,128)(2,1)} %refs_1_.7, bf16[1024,768]{1,0:T(8,128)(2,1)} %get-tuple-element.63.refs_2_, bf16[1024,768]{1,0:T(8,128)(2,1)} %get-tuple-element.64.refs_3_, ...), custom_call_target="tpu_custom_call" | custom-call | flops 21849999360 | bytes 1 | tf_op jit(solution)/shard_map/attend_back/pallas_call | solution.py:71
  146.9 2.1 add_cut.14
  150.4 2.3 add_cut.15
  153.4 7.0 %collective-permute-done.15.refs_1_ = bf16[96,1536]{1,0:T(8,128)(2,1)} collective-permute-done((bf16[96,1536]{1,0:T(8,128)(2,1)}, bf16[96,1536]{1,0:T(8,128)(2,1)}, u32[]{:S(2)}, u32[]{:S(2)}) %collective-permute-start.15) | collective-permute-done | bytes 294944 | tf_op jit(solution)/shard_map/ppermute | solution.py:702
  163.6 2.4 add_cut.17
  172.8 2.8 collective-permute-start.25
  178.4 2.8 collective-permute-start.22
  181.2 15.8 %collective-permute-done.16.refs_1_ = bf16[48,2048]{1,0:T(8,128)(2,1)S(1)} collective-permute-done((bf16[48,2048]{1,0:T(8,128)(2,1)S(1)}, bf16[48,2048]{1,0:T(8,128)(2,1)S(1)}, u32[]{:S(2)}, u32[]{:S(2)}) %collective-permute-start.16) | collective-permute-done | bytes 196640 | tf_op jit(solution)/shard_map/ppermute | solution.py:702
  201.2 2.8 collective-permute-start.19
  209.5 3.8 %collective-permute-done.19.refs_1_ = bf16[48,2048]{1,0:T(8,128)(2,1)S(1)} collective-permute-done((bf16[48,2048]{1,0:T(8,128)(2,1)}, bf16[48,2048]{1,0:T(8,128)(2,1)S(1)}, u32[]{:S(2)}, u32[]{:S(2)}) %collective-permute-start.19) | collective-permute-done | bytes 196640 | tf_op jit(solution)/shard_map/ppermute | solution.py:702
  215.1 2.9 collective-permute-start.30
  218.0 2.1 collective-permute-done.21.refs_3_
  220.8 2.1 join.4.refs_10_.refs_1_.refs_9_
  222.9 2.0 collective-permute-start.28
  226.0 2.2 collective-permute-start.38
  228.1 10.4 %token_grad.1.refs_4_ = f32[1024,768]{1,0:T(8,128)} custom-call(s32[5]{0:T(128)} %stack.23.refs_0_, f32[1024,768]{1,0:T(8,128)} %get-tuple-element.69.refs_1_, bf16[1024,1152]{1,0:T(8,128)(2,1)} %get-tuple-element.82.refs_2_, bf16[1024,1152]{1,0:T(8,128)(2,1)} %get-tuple-element.90.refs_3_, bf16[768,768]{1,0:T(8,128)(2,1)} %refs_7_.2, ...), custom_call_target="tpu_custom_call" | custom-call | flops 11500000256 | bytes 1 | tf_op jit(solution)/shard_map/token_grad/pallas_call | solution.py:71
  245.2 8.9 %collective-permute-done.32.refs_3_ = bf16[192,1152]{1,0:T(8,128)(2,1)} collective-permute-done((bf16[192,1152]{1,0:T(8,128)(2,1)}, bf16[192,1152]{1,0:T(8,128)(2,1)}, u32[]{:S(2)}, u32[]{:S(2)}) %collective-permute-start.32) | collective-permute-done | bytes 442400 | tf_op jit(solution)/shard_map/ppermute | solution.py:702
  258.3 4.3 %collective-permute-done.39.refs_3_.refs_11_ = bf16[192,2048]{1,0:T(8,128)(2,1)} collective-permute-done((bf16[192,2048]{1,0:T(8,128)(2,1)S(1)}, bf16[192,2048]{1,0:T(8,128)(2,1)}, u32[]{:S(2)}, u32[]{:S(2)}) %collective-permute-start.39) | collective-permute-done | bytes 786464 | tf_op jit(solution)/shard_map/ppermute | solution.py:702
  263.9 7.1 %collective-permute-done.40.refs_4_.refs_12_ = bf16[192,2048]{1,0:T(8,128)(2,1)} collective-permute-done((bf16[192,2048]{1,0:T(8,128)(2,1)}, bf16[192,2048]{1,0:T(8,128)(2,1)}, u32[]{:S(2)}, u32[]{:S(2)}) %collective-permute-start.40) | collective-permute-done | bytes 786464 | tf_op jit(solution)/shard_map/ppermute | solution.py:702
  271.2 7.5 %gather_units.1.refs_17_ = f32[3072,768]{1,0:T(8,128)} custom-call(s32[5]{0:T(128)} %stack.23.refs_0_, bf16[192,1536]{1,0:T(8,128)(2,1)} %join.3.refs_4_.refs_1_, bf16[192,1536]{1,0:T(8,128)(2,1)} %collective-permute-done.45.refs_2_, bf16[192,1536]{1,0:T(8,128)(2,1)} %collective-permute-done.46.refs_3_, bf16[192,1536]{1,0:T(8,128)(2,1)} %collective-permute-done.47.refs_4_, ...), custom_call_target="tpu_custom_call" | custom-call | flops 9200000000 | bytes 1 | tf_op jit(solution)/shard_map/gather_units/pallas_call | solution.py:71
  279.8 9.0 %gather_two.1 = (f32[768,3072]{1,0:T(8,128)}, f32[768,768]{1,0:T(8,128)}, f32[2,768]{1,0:T(2,128)}, f32[2,768]{1,0:T(2,128)}) custom-call(s32[5]{0:T(128)} %stack.23.refs_0_, bf16[192,2048]{1,0:T(8,128)(2,1)} %join.4.refs_10_.refs_1_.refs_9_, bf16[192,2048]{1,0:T(8,128)(2,1)} %collective-permute-done.38.refs_2_.refs_10_, ...), custom_call_target="tpu_custom_call" | custom-call | flops 13800000512 | bytes 1 | tf_op jit(solution)/shard_map/gather_two/pallas_call | solution.py:71
  289.9 5.9 %gather_qkv.1 = (f32[768,768]{1,0:T(8,128)}, f32[768,768]{1,0:T(8,128)}, f32[768,768]{1,0:T(8,128)}) custom-call(s32[5]{0:T(128)} %stack.23.refs_0_, bf16[192,1152]{1,0:T(8,128)(2,1)} %join.5.refs_9_.refs_1_, bf16[192,1152]{1,0:T(8,128)(2,1)} %collective-permute-done.31.refs_2_, bf16[192,1152]{1,0:T(8,128)(2,1)} %collective-permute-done.32.refs_3_, ...), custom_call_target="tpu_custom_call" | custom-call | flops 6325000192 | bytes 1 | tf_op jit(solution)/shard_map/gather_qkv/pallas_call | solution.py:71
  (143 shorter events, 58.2 us)
Async XLA Ops:
  78.3 17.4 %collective-permute-start.1 = (f32[6,256,128]{2,1,0:T(8,128)}, f32[6,256,128]{2,1,0:T(8,128)S(1)}, u32[]{:S(2)}, u32[]{:S(2)}) collective-permute-start(f32[6,256,128]{2,1,0:T(8,128)} %get-tuple-element.73), channel_id=1, source_target_pairs={{0,1},{1,0},{2,3},{3,2},{4,5},{5,4},{6,7},{7,6},{8,9},{9,8},{10,11... | collective-permute-start | bytes 2359304 | tf_op jit(solution)/shard_map/ppermute | solution.py:702
  85.9 29.5 %collective-permute-start.10 = (bf16[384,1536]{1,0:T(8,128)(2,1)}, bf16[384,1536]{1,0:T(8,128)(2,1)}, u32[]{:S(2)}, u32[]{:S(2)}) collective-permute-start(bf16[384,1536]{1,0:T(8,128)(2,1)} %get-tuple-element.87), channel_id=1, source_target_pairs={{0,8},{1,9},{2,10},{3,11},{4,12},{5,13},{6,14},{7,15},{8,0},{9,1},... | collective-permute-start | bytes 3538952 | tf_op jit(solution)/shard_map/ppermute | solution.py:702
  93.9 27.1 %collective-permute-start.9 = (bf16[384,2048]{1,0:T(8,128)(2,1)}, bf16[384,2048]{1,0:T(8,128)(2,1)}, u32[]{:S(2)}, u32[]{:S(2)}) collective-permute-start(bf16[384,2048]{1,0:T(8,128)(2,1)} %get-tuple-element.86), channel_id=1, source_target_pairs={{0,2},{1,5},{2,0},{3,7},{4,6},{5,1},{6,4},{7,3},{8,10},{9,13},{10,... | collective-permute-start | bytes 4718600 | tf_op jit(solution)/shard_map/ppermute | solution.py:702
  112.9 12.8 %collective-permute-start.6 = (bf16[768,384]{1,0:T(8,128)(2,1)}, bf16[768,384]{1,0:T(8,128)(2,1)S(1)}, u32[]{:S(2)}, u32[]{:S(2)}) collective-permute-start(bf16[768,384]{1,0:T(8,128)(2,1)} %get-tuple-element.83), channel_id=1, source_target_pairs={{0,1},{1,0},{2,3},{3,2},{4,5},{5,4},{6,7},{7,6},{8,9},{9,8},{10,11... | collective-permute-start | bytes 1769480 | tf_op jit(solution)/shard_map/ppermute | solution.py:702
  113.0 12.7 %collective-permute-start.7 = (bf16[768,384]{1,0:T(8,128)(2,1)}, bf16[768,384]{1,0:T(8,128)(2,1)}, u32[]{:S(2)}, u32[]{:S(2)}) collective-permute-start(bf16[768,384]{1,0:T(8,128)(2,1)} %get-tuple-element.84), channel_id=1, source_target_pairs={{0,1},{1,0},{2,3},{3,2},{4,5},{5,4},{6,7},{7,6},{8,9},{9,8},{10,11... | collective-permute-start | bytes 1769480 | tf_op jit(solution)/shard_map/ppermute | solution.py:702
  113.5 12.2 %collective-permute-start.8 = (bf16[768,384]{1,0:T(8,128)(2,1)}, bf16[768,384]{1,0:T(8,128)(2,1)}, u32[]{:S(2)}, u32[]{:S(2)}) collective-permute-start(bf16[768,384]{1,0:T(8,128)(2,1)} %get-tuple-element.85), channel_id=1, source_target_pairs={{0,1},{1,0},{2,3},{3,2},{4,5},{5,4},{6,7},{7,6},{8,9},{9,8},{10,11... | collective-permute-start | bytes 1769480 | tf_op jit(solution)/shard_map/ppermute | solution.py:702
  118.2 28.8 %collective-permute-start.12 = (bf16[192,1536]{1,0:T(8,128)(2,1)}, bf16[192,1536]{1,0:T(8,128)(2,1)}, u32[]{:S(2)}, u32[]{:S(2)}) collective-permute-start(bf16[192,1536]{1,0:T(8,128)(2,1)} %get-tuple-element.92), channel_id=1, source_target_pairs={{0,16},{1,17},{2,18},{3,19},{4,20},{5,21},{6,22},{7,23},{8,24},{9,... | collective-permute-start | bytes 1769480 | tf_op jit(solution)/shard_map/ppermute | solution.py:702
  124.1 26.2 %collective-permute-start.11 = (bf16[192,2048]{1,0:T(8,128)(2,1)}, bf16[192,2048]{1,0:T(8,128)(2,1)}, u32[]{:S(2)}, u32[]{:S(2)}) collective-permute-start(bf16[192,2048]{1,0:T(8,128)(2,1)} %get-tuple-element.91), channel_id=1, source_target_pairs={{0,4},{1,3},{2,6},{3,1},{4,0},{5,7},{6,2},{7,5},{8,12},{9,11},{10,... | collective-permute-start | bytes 2359304 | tf_op jit(solution)/shard_map/ppermute | solution.py:702
  143.8 18.9 %collective-permute-start.14 = (bf16[384,1152]{1,0:T(8,128)(2,1)}, bf16[384,1152]{1,0:T(8,128)(2,1)S(1)}, u32[]{:S(2)}, u32[]{:S(2)}) collective-permute-start(bf16[384,1152]{1,0:T(8,128)(2,1)} %get-tuple-element.97), channel_id=1, source_target_pairs={{0,2},{1,5},{2,0},{3,7},{4,6},{5,1},{6,4},{7,3},{8,10},{9,13},{10,... | collective-permute-start | bytes 2654216 | tf_op jit(solution)/shard_map/ppermute | solution.py:702
  149.0 11.3 %collective-permute-start.15 = (bf16[96,1536]{1,0:T(8,128)(2,1)}, bf16[96,1536]{1,0:T(8,128)(2,1)}, u32[]{:S(2)}, u32[]{:S(2)}) collective-permute-start(bf16[96,1536]{1,0:T(8,128)(2,1)} %get-tuple-element.98), channel_id=1, source_target_pairs={{0,2},{1,5},{2,0},{3,7},{4,6},{5,1},{6,4},{7,3},{8,10},{9,13},{10,... | collective-permute-start | bytes 884744 | tf_op jit(solution)/shard_map/ppermute | solution.py:702
  152.7 14.9 %collective-permute-start.13 = (bf16[96,2048]{1,0:T(8,128)(2,1)}, bf16[96,2048]{1,0:T(8,128)(2,1)}, u32[]{:S(2)}, u32[]{:S(2)}) collective-permute-start(bf16[96,2048]{1,0:T(8,128)(2,1)} %get-tuple-element.96), channel_id=1, source_target_pairs={{0,8},{1,9},{2,10},{3,11},{4,12},{5,13},{6,14},{7,15},{8,0},{9,1},... | collective-permute-start | bytes 1179656 | tf_op jit(solution)/shard_map/ppermute | solution.py:702
  171.2 28.3 %collective-permute-start.27 = (bf16[48,1536]{1,0:T(8,128)(2,1)}, bf16[48,1536]{1,0:T(8,128)(2,1)S(1)}, u32[]{:S(2)}, u32[]{:S(2)}) collective-permute-start(bf16[48,1536]{1,0:T(8,128)(2,1)} %add_all.3.refs_2_.refs_0_), channel_id=1, source_target_pairs={{0,24},{1,25},{2,26},{3,27},{4,28},{5,29},{6,30},{7,31},{8,16},{9,... | collective-permute-start | bytes 442376 | tf_op jit(solution)/shard_map/ppermute | solution.py:702
  172.6 28.2 %collective-permute-start.26 = (bf16[48,1536]{1,0:T(8,128)(2,1)}, bf16[48,1536]{1,0:T(8,128)(2,1)}, u32[]{:S(2)}, u32[]{:S(2)}) collective-permute-start(bf16[48,1536]{1,0:T(8,128)(2,1)} %add_all.3.refs_2_.refs_0_), channel_id=1, source_target_pairs={{0,8},{1,9},{2,10},{3,11},{4,12},{5,13},{6,14},{7,15},{8,0},{9,1},... | collective-permute-start | bytes 442376 | tf_op jit(solution)/shard_map/ppermute | solution.py:702
  172.8 28.4 %collective-permute-start.25 = (bf16[48,1536]{1,0:T(8,128)(2,1)}, bf16[48,1536]{1,0:T(8,128)(2,1)}, u32[]{:S(2)}, u32[]{:S(2)}) collective-permute-start(bf16[48,1536]{1,0:T(8,128)(2,1)} %add_all.3.refs_2_.refs_0_), channel_id=1, source_target_pairs={{0,16},{1,17},{2,18},{3,19},{4,20},{5,21},{6,22},{7,23},{8,24},{9,... | collective-permute-start | bytes 442376 | tf_op jit(solution)/shard_map/ppermute | solution.py:702
  175.6 21.4 %collective-permute-start.16 = (bf16[48,2048]{1,0:T(8,128)(2,1)S(1)}, bf16[48,2048]{1,0:T(8,128)(2,1)S(1)}, u32[]{:S(2)}, u32[]{:S(2)}) collective-permute-start(bf16[48,2048]{1,0:T(8,128)(2,1)S(1)} %copy-done.13), channel_id=1, source_target_pairs={{0,16},{1,17},{2,18},{3,19},{4,20},{5,21},{6,22},{7,23},{8,24},{9,... | collective-permute-start | bytes 589832 | tf_op jit(solution)/shard_map/ppermute | solution.py:702
  178.4 27.5 %collective-permute-start.22 = (bf16[48,1152]{1,0:T(8,128)(2,1)}, bf16[48,1152]{1,0:T(8,128)(2,1)}, u32[]{:S(2)}, u32[]{:S(2)}) collective-permute-start(bf16[48,1152]{1,0:T(8,128)(2,1)} %get-tuple-element.106), channel_id=1, source_target_pairs={{0,16},{1,17},{2,18},{3,19},{4,20},{5,21},{6,22},{7,23},{8,24},{9,... | collective-permute-start | bytes 331784 | tf_op jit(solution)/shard_map/ppermute | solution.py:702
  200.7 14.3 %collective-permute-start.20 = (bf16[48,2048]{1,0:T(8,128)(2,1)}, bf16[48,2048]{1,0:T(8,128)(2,1)S(1)}, u32[]{:S(2)}, u32[]{:S(2)}) collective-permute-start(bf16[48,2048]{1,0:T(8,128)(2,1)} %add_all.4.refs_4_.refs_0_), channel_id=1, source_target_pairs={{0,8},{1,9},{2,10},{3,11},{4,12},{5,13},{6,14},{7,15},{8,0},{9,1},... | collective-permute-start | bytes 589832 | tf_op jit(solution)/shard_map/ppermute | solution.py:702
  201.2 12.0 %collective-permute-start.19 = (bf16[48,2048]{1,0:T(8,128)(2,1)}, bf16[48,2048]{1,0:T(8,128)(2,1)S(1)}, u32[]{:S(2)}, u32[]{:S(2)}) collective-permute-start(bf16[48,2048]{1,0:T(8,128)(2,1)} %add_all.4.refs_4_.refs_0_), channel_id=1, source_target_pairs={{0,16},{1,17},{2,18},{3,19},{4,20},{5,21},{6,22},{7,23},{8,24},{9,... | collective-permute-start | bytes 589832 | tf_op jit(solution)/shard_map/ppermute | solution.py:702
  205.9 36.6 %collective-permute-start.48 = (bf16[192,1536]{1,0:T(8,128)(2,1)}, bf16[192,1536]{1,0:T(8,128)(2,1)}, u32[]{:S(2)}, u32[]{:S(2)}) collective-permute-start(bf16[192,1536]{1,0:T(8,128)(2,1)} %join.3.refs_4_.refs_1_), channel_id=1, source_target_pairs={{0,1},{1,0},{2,3},{3,2},{4,5},{5,4},{6,7},{7,6},{8,9},{9,8},{10,11... | collective-permute-start | bytes 1769480 | tf_op jit(solution)/shard_map/ppermute | solution.py:702
  207.4 35.7 %collective-permute-start.46 = (bf16[192,1536]{1,0:T(8,128)(2,1)}, bf16[192,1536]{1,0:T(8,128)(2,1)}, u32[]{:S(2)}, u32[]{:S(2)}) collective-permute-start(bf16[192,1536]{1,0:T(8,128)(2,1)} %join.3.refs_4_.refs_1_), channel_id=1, source_target_pairs={{0,2},{1,5},{2,0},{3,7},{4,6},{5,1},{6,4},{7,3},{8,10},{9,13},{10,... | collective-permute-start | bytes 1769480 | tf_op jit(solution)/shard_map/ppermute | solution.py:702
  207.5 31.1 %collective-permute-start.45 = (bf16[192,1536]{1,0:T(8,128)(2,1)}, bf16[192,1536]{1,0:T(8,128)(2,1)}, u32[]{:S(2)}, u32[]{:S(2)}) collective-permute-start(bf16[192,1536]{1,0:T(8,128)(2,1)} %join.3.refs_4_.refs_1_), channel_id=1, source_target_pairs={{0,4},{1,3},{2,6},{3,1},{4,0},{5,7},{6,2},{7,5},{8,12},{9,11},{10,... | collective-permute-start | bytes 1769480 | tf_op jit(solution)/shard_map/ppermute | solution.py:702
  222.9 15.7 %collective-permute-start.28 = (bf16[48,1152]{1,0:T(8,128)(2,1)S(1)}, bf16[48,1152]{1,0:T(8,128)(2,1)}, u32[]{:S(2)}, u32[]{:S(2)}) collective-permute-start(bf16[48,1152]{1,0:T(8,128)(2,1)S(1)} %copy-done.20), channel_id=1, source_target_pairs={{0,16},{1,17},{2,18},{3,19},{4,20},{5,21},{6,22},{7,23},{8,24},{9,... | collective-permute-start | bytes 331784 | tf_op jit(solution)/shard_map/ppermute | solution.py:702
  226.0 17.6 %collective-permute-start.38 = (bf16[192,2048]{1,0:T(8,128)(2,1)}, bf16[192,2048]{1,0:T(8,128)(2,1)}, u32[]{:S(2)}, u32[]{:S(2)}) collective-permute-start(bf16[192,2048]{1,0:T(8,128)(2,1)} %join.4.refs_10_.refs_1_.refs_9_), channel_id=1, source_target_pairs={{0,4},{1,3},{2,6},{3,1},{4,0},{5,7},{6,2},{7,5},{8,12},{9,11},{10,... | collective-permute-start | bytes 2359304 | tf_op jit(solution)/shard_map/ppermute | solution.py:702
  238.5 17.4 %collective-permute-start.47 = (bf16[192,1536]{1,0:T(8,128)(2,1)}, bf16[192,1536]{1,0:T(8,128)(2,1)}, u32[]{:S(2)}, u32[]{:S(2)}) collective-permute-start(bf16[192,1536]{1,0:T(8,128)(2,1)} %collective-permute-done.45.refs_2_), channel_id=1, source_target_pairs={{0,2},{1,5},{2,0},{3,7},{4,6},{5,1},{6,4},{7,3},{8,10},{9,13},{10,... | collective-permute-start | bytes 1769480 | tf_op jit(solution)/shard_map/ppermute | solution.py:702
  240.5 13.5 %collective-permute-start.32 = (bf16[192,1152]{1,0:T(8,128)(2,1)}, bf16[192,1152]{1,0:T(8,128)(2,1)}, u32[]{:S(2)}, u32[]{:S(2)}) collective-permute-start(bf16[192,1152]{1,0:T(8,128)(2,1)} %join.5.refs_9_.refs_1_), channel_id=1, source_target_pairs={{0,2},{1,5},{2,0},{3,7},{4,6},{5,1},{6,4},{7,3},{8,10},{9,13},{10,... | collective-permute-start | bytes 1327112 | tf_op jit(solution)/shard_map/ppermute | solution.py:702
  242.5 13.4 %collective-permute-start.31 = (bf16[192,1152]{1,0:T(8,128)(2,1)}, bf16[192,1152]{1,0:T(8,128)(2,1)}, u32[]{:S(2)}, u32[]{:S(2)}) collective-permute-start(bf16[192,1152]{1,0:T(8,128)(2,1)} %join.5.refs_9_.refs_1_), channel_id=1, source_target_pairs={{0,4},{1,3},{2,6},{3,1},{4,0},{5,7},{6,2},{7,5},{8,12},{9,11},{10,... | collective-permute-start | bytes 1327112 | tf_op jit(solution)/shard_map/ppermute | solution.py:702
  243.1 19.4 %collective-permute-start.39 = (bf16[192,2048]{1,0:T(8,128)(2,1)S(1)}, bf16[192,2048]{1,0:T(8,128)(2,1)}, u32[]{:S(2)}, u32[]{:S(2)}) collective-permute-start(bf16[192,2048]{1,0:T(8,128)(2,1)S(1)} %copy-done.2), channel_id=1, source_target_pairs={{0,2},{1,5},{2,0},{3,7},{4,6},{5,1},{6,4},{7,3},{8,10},{9,13},{10,... | collective-permute-start | bytes 2359304 | tf_op jit(solution)/shard_map/ppermute | solution.py:702
  243.5 27.4 %collective-permute-start.40 = (bf16[192,2048]{1,0:T(8,128)(2,1)}, bf16[192,2048]{1,0:T(8,128)(2,1)}, u32[]{:S(2)}, u32[]{:S(2)}) collective-permute-start(bf16[192,2048]{1,0:T(8,128)(2,1)} %collective-permute-done.38.refs_2_.refs_10_), channel_id=1, source_target_pairs={{0,2},{1,5},{2,0},{3,7},{4,6},{5,1},{6,4},{7,3},{8,10},{9,13},{10,... | collective-permute-start | bytes 2359304 | tf_op jit(solution)/shard_map/ppermute | solution.py:702
  256.4 22.3 %collective-permute-start.41 = (bf16[192,2048]{1,0:T(8,128)(2,1)S(1)}, bf16[192,2048]{1,0:T(8,128)(2,1)}, u32[]{:S(2)}, u32[]{:S(2)}) collective-permute-start(bf16[192,2048]{1,0:T(8,128)(2,1)S(1)} %copy-done.2), channel_id=1, source_target_pairs={{0,1},{1,0},{2,3},{3,2},{4,5},{5,4},{6,7},{7,6},{8,9},{9,8},{10,11... | collective-permute-start | bytes 2359304 | tf_op jit(solution)/shard_map/ppermute | solution.py:702
  258.1 20.9 %collective-permute-start.33 = (bf16[192,1152]{1,0:T(8,128)(2,1)}, bf16[192,1152]{1,0:T(8,128)(2,1)}, u32[]{:S(2)}, u32[]{:S(2)}) collective-permute-start(bf16[192,1152]{1,0:T(8,128)(2,1)} %collective-permute-done.31.refs_2_), channel_id=1, source_target_pairs={{0,2},{1,5},{2,0},{3,7},{4,6},{5,1},{6,4},{7,3},{8,10},{9,13},{10,... | collective-permute-start | bytes 1327112 | tf_op jit(solution)/shard_map/ppermute | solution.py:702
  262.5 17.0 %collective-permute-start.42 = (bf16[192,2048]{1,0:T(8,128)(2,1)}, bf16[192,2048]{1,0:T(8,128)(2,1)}, u32[]{:S(2)}, u32[]{:S(2)}) collective-permute-start(bf16[192,2048]{1,0:T(8,128)(2,1)} %collective-permute-done.38.refs_2_.refs_10_), channel_id=1, source_target_pairs={{0,1},{1,0},{2,3},{3,2},{4,5},{5,4},{6,7},{7,6},{8,9},{9,8},{10,11... | collective-permute-start | bytes 2359304 | tf_op jit(solution)/shard_map/ppermute | solution.py:702
  263.6 15.7 %collective-permute-start.43 = (bf16[192,2048]{1,0:T(8,128)(2,1)}, bf16[192,2048]{1,0:T(8,128)(2,1)}, u32[]{:S(2)}, u32[]{:S(2)}) collective-permute-start(bf16[192,2048]{1,0:T(8,128)(2,1)} %collective-permute-done.39.refs_3_.refs_11_), channel_id=1, source_target_pairs={{0,1},{1,0},{2,3},{3,2},{4,5},{5,4},{6,7},{7,6},{8,9},{9,8},{10,11... | collective-permute-start | bytes 2359304 | tf_op jit(solution)/shard_map/ppermute | solution.py:702
  (43 other events, 221.5 us)
